TPU v7x, 128 devices: a whole 4x4x4 slice. The times are simulated.
128 devices in a mesh: dp: 4 (over z), pipe: 8 (over y, x_lo), tensor: 4 (over x_hi, core).
Axes of the slice: x: 4 (x_hi: 2, x_lo: 2; x = x_hi * 2 + x_lo), y: 4, z: 4, core: 2. Of those that a mesh axis runs over, the one named last changes fastest.
Arguments:
- vision: bfloat16 [1024, 8192], P('dp', 'tensor'), may hold values from -6 to 6
- features: bfloat16 [1024, 7680], P('dp'), may hold values from -6 to 6
- queries: bfloat16 [2048, 8192], P('dp', 'tensor'), may hold values from -4 to 4
- ctx_grad: bfloat16 [2048, 8192], P('dp', 'tensor'), may hold values from -4 to 4
- row_mask: int32 [2048], P('dp'), may hold values 0 or 1
- key_weight: bfloat16 [8, 8192, 1024], P('pipe', None, 'tensor'), may hold values from -0.0625 to 0.0625
- value_weight: bfloat16 [8, 8192, 1024], P('pipe', None, 'tensor'), may hold values from -0.0625 to 0.0625
- key_gain: float32 [8, 128], P('pipe'), may hold values from 0.1 to 1.9
Outputs:
- key_weight_grad: float32 [8, 8192, 1024], P('pipe', 'dp', 'tensor')
- value_weight_grad: float32 [8, 8192, 1024], P('pipe', 'dp', 'tensor')
- projector_grad: float32 [7680, 8192], P('dp', ('pipe', 'tensor'))
All inputs are finite; a program needn't handle non-finite values. No bound on the sum of `row_mask` on one device may be relied on, other than what follows from the above.
Results may differ from a plain program's by a relative error of at most 0.009.
Values may be sent and summed in bfloat16 or wider, within the bound.
No kernel may reach another device: no remote copies, remote signals or barrier semaphores. Data moves between devices by JAX's collectives and lax.ppermute only.
A program may use at most 128 MiB of HBM per device.

v0:
```python
import jax
import jax.numpy as jnp
from jax import lax
from jax.sharding import PartitionSpec as P

norm_eps = 1e-05


def local_grads(gathered, queries, ctx_grad, row_mask, key_proj, value_proj, key_gain):
    head_size = key_gain.shape[0]
    vis_rows = gathered.shape[0]
    text_rows = queries.shape[0]
    kv_heads = key_proj.shape[1] // head_size
    group_size = queries.shape[1] // head_size // kv_heads
    score_scale = head_size ** (-0.5)
    key_raw = jnp.dot(gathered, key_proj, preferred_element_type=jnp.float32).reshape(
        vis_rows, kv_heads, head_size
    )
    inv_rms = lax.rsqrt(jnp.mean(key_raw * key_raw, -1, keepdims=True) + norm_eps)
    keys = (key_raw * inv_rms * key_gain).astype(jnp.bfloat16)
    values = jnp.dot(gathered, value_proj, preferred_element_type=jnp.float32).astype(jnp.bfloat16)
    values = values.reshape(vis_rows, kv_heads, head_size)
    query_heads = queries.reshape(text_rows, kv_heads, group_size, head_size)
    masked = ctx_grad * row_mask[:, None].astype(jnp.bfloat16)
    masked = masked.reshape(text_rows, kv_heads, group_size, head_size)
    scores = (
        jnp.einsum("tkgd,vkd->kgtv", query_heads, keys, preferred_element_type=jnp.float32)
        * score_scale
    )
    exp_scores = jnp.exp(scores)
    attn_probs = exp_scores / jnp.sum(exp_scores, -1, keepdims=True)
    probs_bf = attn_probs.astype(jnp.bfloat16)
    context = jnp.einsum("kgtv,vkd->tkgd", probs_bf, values, preferred_element_type=jnp.float32)
    row_delta = jnp.sum(masked.astype(jnp.float32) * context, -1).transpose(1, 2, 0)[..., None]
    value_grad = jnp.einsum(
        "kgtv,tkgd->vkd", probs_bf, masked, preferred_element_type=jnp.float32
    ).astype(jnp.bfloat16)
    prob_grad = jnp.einsum("tkgd,vkd->kgtv", masked, values, preferred_element_type=jnp.float32)
    score_grad = (attn_probs * (prob_grad - row_delta) * score_scale).astype(jnp.bfloat16)
    normed_grad = jnp.einsum(
        "kgtv,tkgd->vkd", score_grad, query_heads, preferred_element_type=jnp.float32
    )
    scaled = normed_grad * key_gain
    key_grad = inv_rms * (
        scaled - key_raw * inv_rms * inv_rms * jnp.mean(scaled * key_raw, -1, keepdims=True)
    )
    key_grad = key_grad.astype(jnp.bfloat16)
    return (key_grad.reshape(vis_rows, -1), value_grad.reshape(vis_rows, -1))


def contract_rows(left, right):
    return lax.dot_general(
        left, right, (((1,), (1,)), ((), ())), preferred_element_type=jnp.float32
    )


def contract_first(left, right):
    return lax.dot_general(
        left, right, (((0,), (0,)), ((), ())), preferred_element_type=jnp.float32
    )


def shards(vision, features, queries, ctx_grad, row_mask, key_weight, value_weight, key_gain):
    gathered = lax.all_gather(vision, "tensor", axis=1, tiled=True)
    key_proj = key_weight[0]
    value_proj = value_weight[0]
    key_grad, value_grad = local_grads(
        gathered, queries, ctx_grad, row_mask, key_proj, value_proj, key_gain[0]
    )
    summed = lax.psum_scatter(
        contract_rows(key_proj, key_grad) + contract_rows(value_proj, value_grad),
        ("pipe", "tensor"),
        scatter_dimension=0,
        tiled=True,
    )
    token_grad = summed.astype(jnp.bfloat16)
    key_term = contract_first(gathered, key_grad)
    value_term = contract_first(gathered, value_grad)
    key_total, value_total = (
        lax.psum_scatter(key_term, "dp", scatter_dimension=0, tiled=True),
        lax.psum_scatter(value_term, "dp", scatter_dimension=0, tiled=True),
    )
    projector_term = lax.dot_general(
        features, token_grad, (((0,), (1,)), ((), ())), preferred_element_type=jnp.float32
    )
    projector_total = lax.psum_scatter(projector_term, "dp", scatter_dimension=0, tiled=True)
    return (key_total[None], value_total[None], projector_total)


def solution(mesh):
    in_specs = (
        P("dp", "tensor"),
        P("dp", None),
        P("dp", "tensor"),
        P("dp", "tensor"),
        P("dp"),
        P("pipe", None, "tensor"),
        P("pipe", None, "tensor"),
        P("pipe", None),
    )
    out_specs = (P("pipe", "dp", "tensor"), P("pipe", "dp", "tensor"), P("dp", ("pipe", "tensor")))
    return jax.shard_map(shards, mesh=mesh, in_specs=in_specs, out_specs=out_specs, check_vma=False)
```

profile of v0, /device:TPU:1, one launch (start us, length us, event | category | flops | bytes accessed | tf_op | source)
XLA Modules:
  0.0 509.1 jit_solution(14356714939236365850)
XLA Ops:
  7.2 0.0 all-gather.2.cloned.1.call-start
  7.2 0.7 all-gather.2.cloned.1.call-update
  7.9 0.0 reduce-scatter.9.cloned.1.call-start
  7.9 6.4 %copy.39 = bf16[256,8192]{1,0:T(8,128)(2,1)} copy(bf16[256,8192]{0,1:T(8,128)(2,1)} %bitcast.120) | data formatting | bytes 8388608 | tf_op jit(solution)/shard_map/dot_general | solution.py:16
  14.4 0.0 copy-start.6
  14.4 4.1 copy.43
  18.5 0.0 copy-done.6
  18.5 0.0 copy-done.5
  18.5 0.2 multiply_bitcast_fusion
  18.7 0.6 copy.44
  19.3 32.5 %all-gather.2.cloned.1.call-done = bf16[256,8192]{1,0:T(8,128)(2,1)} async-done(((bf16[256,2048]{1,0:T(8,128)(2,1)}), bf16[256,8192]{1,0:T(8,128)(2,1)}) %all-gather.2.cloned.1.call-update) | async-done | bytes 4194320 | tf_op jit(solution)/shard_map/all_gather | solution.py:64
  51.8 4.9 multiply_reduce_fusion.1
  56.7 0.0 copy-done.4
  56.8 0.0 copy-done.7
  56.8 1.6 bitcast_reduce_fusion
  58.4 0.0 copy-start.2
  58.4 3.2 copy-done.2
  61.6 2.6 fusion.18
  64.2 7.9 %copy.34 = bf16[2,8,512,256]{3,1,0,2:T(8,128)(2,1)} copy(bf16[2,8,512,256]{2,3,1,0:T(8,128)(2,1)} %fusion.18) | data formatting | bytes 8388608 | tf_op jit(solution)/shard_map/convert_element_type | solution.py:32
  72.1 3.3 fusion.36
  75.4 0.1 copy-done.1
  75.5 4.2 fusion.37
  79.8 0.0 copy-done
  79.8 1.9 fusion.6
  81.6 0.2 copy.24
  81.8 8.1 %multiply_reduce_fusion = (f32[256,2]{0,1:T(2,128)S(1)}, f32[256,2,128]{0,2,1:T(8,128)S(1)}) fusion(f32[256,2,128]{0,2,1:T(8,128)S(1)} %get-tuple-element.10, f32[128]{0:T(128)S(1)} %bitcast.134, bf16[512,2,8,128]{0,3,2,1:T(8,128)(2,1)} %bitcast.121, f32[2,8,512]{2,1,0:T(8,128)S(1)} %copy.24, bf16[256,2,128,1]{0,2,3,1:T(8,128)(2,1)S(1)} %bitcast.132, ...), kind=kOutput, calls=%fused_computation.35 | convolution fusion | flops 1086520832 | bytes 13306368 | tf_op jit(solution)/shard_map/kgtv,tkgd->vkd/dot_general | solution.py:40
  89.9 0.1 multiply_convert_fusion
  89.9 0.0 copy-start.3
  90.0 3.6 fusion.10
  93.6 0.0 copy-done.3
  93.6 4.5 fusion
  98.2 0.0 reduce-scatter.9.cloned.1.call-update
  98.2 0.0 reduce-scatter.5.cloned.1.call-start
  98.2 6.7 %convolution_bitcast_fusion.2 = f32[8192,256]{0,1:T(8,128)} fusion(bf16[256,256]{0,1:T(8,128)(2,1)S(1)} %bitcast.130, bf16[256,8192]{1,0:T(8,128)(2,1)} %all-gather.2.cloned.1.call-done), kind=kOutput, calls=%fused_computation.4 | convolution fusion | flops 1073741824 | bytes 12713984 | tf_op jit(solution)/shard_map/dot_general | solution.py:58
  104.9 0.0 reduce-scatter.5.cloned.1.call-update
  104.9 0.3 reduce-scatter.7.cloned.1.call-start
  105.2 6.9 %convolution_bitcast_fusion.1 = f32[8192,256]{0,1:T(8,128)} fusion(bf16[256,256]{0,1:T(8,128)(2,1)S(1)} %bitcast.128, bf16[256,8192]{1,0:T(8,128)(2,1)} %all-gather.2.cloned.1.call-done), kind=kOutput, calls=%fused_computation.3 | convolution fusion | flops 1073741824 | bytes 12713984 | tf_op jit(solution)/shard_map/dot_general | solution.py:58
  112.1 0.0 reduce-scatter.7.cloned.1.call-update
  112.1 0.0 reduce-scatter.11.cloned.1.call-start
  112.2 136.8 %reduce-scatter.9.cloned.1.call-done = f32[256,256]{0,1:T(8,128)} async-done(((f32[8192,256]{0,1:T(8,128)}), f32[256,256]{0,1:T(8,128)}) %reduce-scatter.9.cloned.1.call-update) | async-done | bytes 262160 | tf_op jit(solution)/shard_map/reduce_scatter | solution.py:70
  249.0 6.5 %convolution_bitcast_fusion = f32[7680,256]{0,1:T(8,128)} fusion(bf16[256,7680]{1,0:T(8,128)(2,1)} %param.9, f32[256,256]{0,1:T(8,128)} %reduce-scatter.9.cloned.1.call-done), kind=kOutput, calls=%fused_computation | convolution fusion | flops 1006698496 | bytes 12058624 | tf_op jit(solution)/shard_map/dot_general | solution.py:83
  255.5 0.0 reduce-scatter.11.cloned.1.call-update
  255.5 82.7 %reduce-scatter.5.cloned.1.call-done = f32[2048,256]{0,1:T(8,128)} async-done(((f32[8192,256]{0,1:T(8,128)}), f32[2048,256]{0,1:T(8,128)}) %reduce-scatter.5.cloned.1.call-update) | async-done | bytes 2097168 | tf_op jit(solution)/shard_map/reduce_scatter | solution.py:80
  338.2 2.9 copy.29
  341.1 79.8 %reduce-scatter.7.cloned.1.call-done = f32[2048,256]{0,1:T(8,128)} async-done(((f32[8192,256]{0,1:T(8,128)}), f32[2048,256]{0,1:T(8,128)}) %reduce-scatter.7.cloned.1.call-update) | async-done | bytes 2097168 | tf_op jit(solution)/shard_map/reduce_scatter | solution.py:81
  420.9 2.9 copy.30
  423.8 76.0 %reduce-scatter.11.cloned.1.call-done = f32[1920,256]{0,1:T(8,128)} async-done(((f32[7680,256]{0,1:T(8,128)}), f32[1920,256]{0,1:T(8,128)}) %reduce-scatter.11.cloned.1.call-update) | async-done | bytes 1966096 | tf_op jit(solution)/shard_map/reduce_scatter | solution.py:86
  499.8 2.8 copy.31
  (8 shorter events, 0.0 us)
Async XLA Ops:
  7.2 44.7 %all-gather.2.cloned.1.call-start = ((), (), s32[]{:S(2)}) async-start(), calls=%async_computation.4 | async-start | bytes 5242880 | tf_op jit(solution)/shard_map/all_gather | solution.py:64
  7.9 241.1 %reduce-scatter.9.cloned.1.call-start = ((), (), s32[]{:S(2)}) async-start(), calls=%async_computation.7 | async-start | bytes 8650752 | tf_op jit(solution)/shard_map/reduce_scatter | solution.py:70
  14.4 4.1 copy-start.6
  14.4 4.1 copy-start.5
  51.8 4.9 copy-start.4
  51.8 4.9 copy-start.7
  58.4 3.2 copy-start.2
  72.1 3.4 copy-start.1
  75.5 4.2 copy-start
  89.9 3.7 copy-start.3
  98.2 240.0 %reduce-scatter.5.cloned.1.call-start = ((), (), s32[]{:S(2)}) async-start(), calls=%async_computation.5 | async-start | bytes 10485760 | tf_op jit(solution)/shard_map/reduce_scatter | solution.py:80
  104.9 316.0 %reduce-scatter.7.cloned.1.call-start = ((), (), s32[]{:S(2)}) async-start(), calls=%async_computation.6 | async-start | bytes 10485760 | tf_op jit(solution)/shard_map/reduce_scatter | solution.py:81
  112.1 387.7 %reduce-scatter.11.cloned.1.call-start = ((), (), s32[]{:S(2)}) async-start(), calls=%async_computation.8 | async-start | bytes 9830400 | tf_op jit(solution)/shard_map/reduce_scatter | solution.py:86
Sparse Core Ops, SparseCore 0:
  9.7 42.1 all-gather.1
  98.3 150.6 reduce-scatter.8
  251.5 86.7 reduce-scatter.4
  340.6 80.2 reduce-scatter.6
  423.1 76.5 reduce-scatter.10
where the time goes:
time: 510 us; the launch traced here: 509 us
  waiting for transfers between devices  409 us (80%)
  matrix products  52.2 us (10%)
  local copies, waits for them, and re-layouts  31.1 us (6%)
  between operations  13.9 us (3%)
    reduce_scatter x1, waiting for transfers between devices, shards(): lax.psum_scatter(contract_rows(key_proj, key_grad) + contract_rows(value_...  137 us
    reduce_scatter x1, waiting for transfers between devices, shards(): lax.psum_scatter(key_term, 'dp', scatter_dimension=0, tiled=True)  82.7 us
    reduce_scatter x1, waiting for transfers between devices, shards(): lax.psum_scatter(value_term, 'dp', scatter_dimension=0, tiled=True)  79.8 us
    reduce_scatter x1, waiting for transfers between devices, shards(): lax.psum_scatter(projector_term, 'dp', scatter_dimension=0, tiled=True)  76 us
    all_gather x1, waiting for transfers between devices, shards(): gathered = lax.all_gather(vision, 'tensor', axis=1, tiled=True)  32.5 us
    dot_general x2, matrix products, contract_first(): lax.dot_general(left, right, (((0,), (0,)), ((), ())), preferred_element_...  13.5 us
    unnamed x20, local copies, waits for them, and re-layouts  12.6 us
  transfers between devices with their start and end apart: 5, of which 5 were waited for; matrix products, arithmetic and copies ran while one was open for 7% of the time, Pallas kernels for 0%

commit v1 on v0

v1 whole, which is shorter than its diff:
```python
import jax
import jax.numpy as jnp
from jax import lax
from jax.experimental import pallas as pl
from jax.experimental.pallas import tpu as pltpu
from jax.sharding import PartitionSpec as P

norm_eps = 1e-05
every_axis = ("dp", "pipe", "tensor")
bf16 = jnp.bfloat16
f32 = jnp.float32
head_size = 128
score_scale = head_size**-0.5
log2_e = 1.4426950408889634
megabyte = 2**20


def flat_index(z, y, x, core):
    return z * 32 + y * 8 + (x & 1) * 4 + (x >> 1) * 2 + core


def exchange_pairs(moved):
    pairs = []
    for z in range(4):
        for y in range(4):
            for x in range(4):
                for core in range(2):
                    pairs.append((flat_index(z, y, x, core), flat_index(*moved(z, y, x, core))))
    return pairs


def send(array, moved):
    return lax.ppermute(array, every_axis, exchange_pairs(moved))


def to_core(z, y, x, core):
    return z, y, x, 1 - core


def to_near_x(z, y, x, core):
    return z, y, x ^ 3, core


def first_stage(k):
    return lambda z, y, x, core: (z, y, x ^ k, core) if core == 0 else (z, y ^ k, x, core)


def second_stage(k):
    return lambda z, y, x, core: (z, y ^ k, x, core) if core == 0 else (z, y, x ^ k, core)


def along_z(k):
    return lambda z, y, x, core: (z ^ k, y, x, core)


def near_z(z, y, x, core):
    return (z ^ 1 if core == 0 else z ^ 3), y, x, core


params = pltpu.CompilerParams(vmem_limit_bytes=20 * megabyte)
large_params = pltpu.CompilerParams(vmem_limit_bytes=40 * megabyte)
def dot(left, right, left_dim=1, right_dim=0):
    return lax.dot_general(
        left, right, (((left_dim,), (right_dim,)), ((), ())), preferred_element_type=f32
    )


in_vmem = pl.BlockSpec(memory_space=pltpu.VMEM)
in_smem = pl.BlockSpec(memory_space=pltpu.SMEM)


in_hbm = pl.BlockSpec(memory_space=pltpu.HBM)


def far_away(array):
    return pltpu.with_memory_space_constraint(array, pltpu.HBM)


def chosen_spec(rows, columns, k, place):
    return pl.BlockSpec(
        (rows, columns), lambda i, table: (0, jnp.where(table[place] == k, i, 0))
    )


def cut_features(features, table):
    rows, width = features.shape
    width //= 4
    half = rows // 2

    def kernel(table, near_in, far_in, near_out, far_out):
        near_out[...] = near_in[...]
        far_out[...] = far_in[...]

    return pl.pallas_call(
        kernel,
        grid_spec=pltpu.PrefetchScalarGridSpec(
            num_scalar_prefetch=1,
            grid=(2,),
            in_specs=[
                pl.BlockSpec((half, width), lambda i, table: (i, table[0])),
                pl.BlockSpec((half // 2, width), lambda i, table: (2 * table[2] + i, table[1])),
            ],
            out_specs=[
                pl.BlockSpec((half, width), lambda i, table: (i, 0)),
                pl.BlockSpec((half // 2, width), lambda i, table: (i, 0)),
            ],
        ),
        out_shape=[jax.ShapeDtypeStruct((r, width), bf16) for r in (rows, half)],
        compiler_params=params,
        name="cut_features",
    )(table, far_away(features), far_away(features))


def project(slices, positions, key_proj, value_proj, start=None):
    rows, width = slices[0].shape
    columns = key_proj.shape[1]
    n = len(slices)

    def kernel(table, *refs):
        slice_refs, projections, rest = refs[:n], refs[n : n + 2], refs[n + 2 :]
        out, held, sems = rest[-3:]
        copies = []
        for i in range(n):
            lines = pl.ds(pl.multiple_of(table[i] * width, width), width)
            for j in range(2):
                copy = pltpu.make_async_copy(projections[j].at[lines, :], held.at[i, j], sems.at[i, j])
                copy.start()
                copies.append(copy)
        for j in range(2):
            place = slice(j * columns, (j + 1) * columns)
            total = 0.0 if start is None else rest[0][:, place]
            for i in range(n):
                copies[2 * i + j].wait()
                total += dot(slice_refs[i][...], held[i, j])
            out[:, place] = total

    operands = [*slices, far_away(key_proj), far_away(value_proj)]
    if start is not None:
        operands.append(start)
    return pl.pallas_call(
        kernel,
        in_specs=[in_smem] + [in_vmem] * n + [in_hbm] * 2 + [in_vmem] * (len(operands) - n - 2),
        out_specs=in_vmem,
        out_shape=jax.ShapeDtypeStruct((rows, 2 * columns), f32),
        scratch_shapes=[pltpu.VMEM((n, 2, width, columns), bf16), pltpu.SemaphoreType.DMA((n, 2))],
        compiler_params=params,
        name="project",
    )(positions, *operands)


def choose(slices, table):
    rows, width = slices[0].shape
    half = rows // 2

    def kernel(table, *refs):
        near, far = refs[4:]
        for k in range(4):

            @pl.when(table[0] == k)
            def _():
                near[...] = refs[k][...]

            @pl.when(table[1] == k)
            def _():
                far[...] = refs[k][pl.ds(pl.multiple_of(table[2] * half, half), half), :]

    return pl.pallas_call(
        kernel,
        in_specs=[in_smem] + [in_vmem] * 4,
        out_specs=[in_vmem] * 2,
        out_shape=[jax.ShapeDtypeStruct((r, width), bf16) for r in (rows, half)],
        compiler_params=params,
        name="choose",
    )(table, *slices)


def middle(last_slice, raw, queries, masked, gain, key_proj, value_proj, table):
    vis_rows, width = last_slice.shape
    depth, columns = key_proj.shape
    kv_heads = columns // head_size
    text_rows = queries.shape[0]
    group = queries.shape[1] // head_size // kv_heads
    group_width = group * head_size
    half = vis_rows // 2
    slices = depth // width
    blocks = 16
    lines = depth // blocks
    unroll = 4

    def kernel(
        table, slice_ref, raw_ref, gain_ref, query_hbm, masked_hbm, key_hbm, value_hbm,
        grads, other_terms, own_terms,
        weights, query_ref, masked_ref, keys, values, sums, turned, text_sems, weight_sems,
    ):
        def weight_copies(i):
            place = pl.ds(pl.multiple_of(table[i] * width, width), width)
            return [
                pltpu.make_async_copy(source.at[place, :], weights.at[j, place, :], weight_sems.at[i, j])
                for j, source in enumerate((key_hbm, value_hbm))
            ]

        def text_copies(head):
            place = pl.ds(head * group_width, group_width)
            return [
                pltpu.make_async_copy(source.at[:, place], target.at[head], text_sems.at[head, j])
                for j, (source, target) in enumerate(((query_hbm, query_ref), (masked_hbm, masked_ref)))
            ]

        all_weight_copies = [weight_copies(i) for i in range(slices)]
        all_text_copies = [text_copies(head) for head in range(kv_heads)]
        for copy in all_weight_copies[0] + sum(all_text_copies, []) + sum(all_weight_copies[1:], []):
            copy.start()
        for copy in all_weight_copies[0]:
            copy.wait()
        place = pl.ds(pl.multiple_of(table[0] * width, width), width)
        key_all = raw_ref[:, :columns] + dot(slice_ref[...], weights[0, place, :])
        value_all = (raw_ref[:, columns:] + dot(slice_ref[...], weights[1, place, :])).astype(bf16)
        for head in range(kv_heads):
            lanes = slice(head * head_size, (head + 1) * head_size)
            key_raw = key_all[:, lanes]
            inv_rms = lax.rsqrt(jnp.mean(key_raw * key_raw, -1, keepdims=True) + norm_eps)
            keys[...] = (key_raw * inv_rms * gain_ref[...]).astype(bf16)
            values[...] = value_all[:, lanes]
            sums[...] = jnp.zeros_like(sums)
            for copy in all_text_copies[head]:
                copy.wait()

            def step(i, carry):
                for j in range(unroll):
                    text = pl.ds(pl.multiple_of((i * unroll + j) * head_size, head_size), head_size)
                    query = query_ref[head, :, text]
                    grad = masked_ref[head, :, text]
                    exp_scores = jnp.exp2(dot(keys[...], query, 1, 1) * (score_scale * log2_e))
                    prob_grad = dot(values[...], grad, 1, 1)
                    probs = exp_scores * (1.0 / jnp.sum(exp_scores, 0, keepdims=True))
                    row_delta = jnp.sum(probs * prob_grad, 0, keepdims=True)
                    sums[1] += dot(probs.astype(bf16), grad)
                    sums[0] += dot((probs * (prob_grad - row_delta)).astype(bf16), query)
                return carry

            lax.fori_loop(0, group // unroll, step, 0)
            scaled = sums[0] * score_scale * gain_ref[...]
            mean = jnp.mean(scaled * key_raw, -1, keepdims=True)
            key_grad = inv_rms * (scaled - key_raw * inv_rms * inv_rms * mean)
            grads[:, lanes] = key_grad.astype(bf16)
            grads[:, columns + head * head_size : columns + (head + 1) * head_size] = sums[1].astype(bf16)

        for copy in sum(all_weight_copies[1:], []):
            copy.wait()
        for i in range(2):
            here = (table[slices + 2 * blocks] + i) % 2 * half
            turned[i * half : (i + 1) * half, :] = grads[pl.ds(pl.multiple_of(here, half), half), :]

        def token_step(i, carry):
            here = pl.ds(pl.multiple_of(i * lines, lines), lines)
            other_place = pl.multiple_of(table[slices + i] * lines, lines)
            own_place = pl.multiple_of(table[slices + blocks + i] * lines, lines)
            term = dot(weights[0, here, :], turned[:, :columns], 1, 1)
            term += dot(weights[1, here, :], turned[:, columns:], 1, 1)
            own_terms[pl.ds(own_place, lines), :] = term[:, :half].astype(bf16)
            other_terms[pl.ds(other_place, lines), :] = term[:, half:].astype(bf16)
            return carry

        lax.fori_loop(0, blocks, token_step, 0, unroll=4)

    return pl.pallas_call(
        kernel,
        in_specs=[in_smem] + [in_vmem] * 3 + [in_hbm] * 4,
        out_specs=[in_vmem] * 3,
        out_shape=[jax.ShapeDtypeStruct((vis_rows, 2 * columns), bf16)]
        + [jax.ShapeDtypeStruct((depth, half), bf16)] * 2,
        scratch_shapes=[
            pltpu.VMEM((2, depth, columns), bf16),
            pltpu.VMEM((kv_heads, text_rows, group_width), bf16),
            pltpu.VMEM((kv_heads, text_rows, group_width), bf16),
            pltpu.VMEM((vis_rows, head_size), bf16),
            pltpu.VMEM((vis_rows, head_size), bf16),
            pltpu.VMEM((2, vis_rows, head_size), f32),
            pltpu.VMEM((vis_rows, 2 * columns), bf16),
            pltpu.SemaphoreType.DMA((kv_heads, 2)),
            pltpu.SemaphoreType.DMA((slices, 2)),
        ],
        compiler_params=large_params,
        name="middle",
    )(table, last_slice, raw, gain, *map(far_away, (queries, masked, key_proj, value_proj)))


def add_terms(own_terms, core_terms):
    rows, tokens = own_terms.shape
    part = rows // 4

    def kernel(own, other, *outs):
        for i, out in enumerate(outs):
            lines = slice(i * part, (i + 1) * part)
            out[...] = (own[lines, :].astype(f32) + other[lines, :].astype(f32)).astype(bf16)

    return pl.pallas_call(
        kernel,
        in_specs=[in_vmem] * 2,
        out_specs=[in_vmem] * 4,
        out_shape=[jax.ShapeDtypeStruct((part, tokens), bf16)] * 4,
        compiler_params=params,
        name="add_terms",
    )(own_terms, core_terms)


def weight_grads(gathered, own_place, visions, grads):
    width = visions[0].shape[1]
    rows = gathered[0].shape[0]
    columns = grads[0].shape[1] // 2
    steps = 4
    block = width // steps
    count = len(visions)

    def kernel(table, *refs):
        own, others, grad_refs = refs[:4], refs[4 : 4 + count], refs[4 + count : 5 + 2 * count]
        key_out, value_out, picked = refs[-3:]
        for k in range(4):

            @pl.when(table[0] == k)
            def _():
                picked[...] = own[k][...]

        total = 0.0
        for vision, grad in zip([picked, *others], grad_refs):
            total += dot(vision[...], grad[...], 0, 0)
        key_out[...] = total[:, :columns]
        value_out[...] = total[:, columns:]

    return pl.pallas_call(
        kernel,
        grid_spec=pltpu.PrefetchScalarGridSpec(
            num_scalar_prefetch=1,
            grid=(steps,),
            in_specs=[chosen_spec(rows, block, k, 0) for k in range(4)]
            + [pl.BlockSpec((v.shape[0], block), lambda i, table: (0, i)) for v in visions]
            + [pl.BlockSpec(g.shape, lambda i, table: (0, 0)) for g in grads],
            out_specs=[pl.BlockSpec((block, columns), lambda i, table: (i, 0))] * 2,
            scratch_shapes=[pltpu.VMEM((rows, block), bf16)],
        ),
        out_shape=[jax.ShapeDtypeStruct((width, columns), f32)] * 2,
        compiler_params=params,
        name="weight_grads",
    )(own_place, *gathered, *visions, *grads)


def projector_grad(features, others, tokens, dp_place):
    width = others[0].shape[1]
    columns = tokens[0].shape[0]
    steps = 3
    block = width // steps
    count = len(tokens)

    def kernel(place, *refs):
        out = refs[-1]
        total = 0.0
        for feature, token in zip(refs[:count], refs[count : 2 * count]):
            total += dot(feature[...], token[...].astype(f32).T.astype(bf16), 0, 0)
        out[...] = total

    return pl.pallas_call(
        kernel,
        grid_spec=pltpu.PrefetchScalarGridSpec(
            num_scalar_prefetch=1,
            grid=(steps,),
            in_specs=[pl.BlockSpec((features.shape[0], block), lambda i, place: (0, place[0] * steps + i))]
            + [pl.BlockSpec((f.shape[0], block), lambda i, place: (0, i)) for f in others]
            + [pl.BlockSpec(t.shape, lambda i, place: (0, 0)) for t in tokens],
            out_specs=pl.BlockSpec((block, columns), lambda i, place: (i, 0)),
        ),
        out_shape=jax.ShapeDtypeStruct((width, columns), f32),
        compiler_params=params,
        name="projector_grad",
    )(dp_place, features, *others, *tokens)


def int_table(*values):
    return jnp.stack([jnp.asarray(v, jnp.int32) for v in values])


def shards(vision, features, queries, ctx_grad, row_mask, key_weight, value_weight, key_gain):
    z = lax.axis_index("dp")
    pipe = lax.axis_index("pipe")
    tensor = lax.axis_index("tensor")
    y, core = pipe // 2, tensor % 2
    x = (tensor // 2) * 2 + pipe % 2
    key_proj, value_proj = key_weight[0], value_weight[0]
    rows = vision.shape[0]
    half = rows // 2
    dv = features.shape[1] // 4
    near = jnp.where(core == 0, z ^ 1, z ^ 3)

    from_core = send(vision, to_core)
    from_x = send(vision, to_near_x)

    feature_near, feature_far = cut_features(features, int_table(near, z ^ 2, core))
    feature_near = send(feature_near, near_z)
    feature_far = send(feature_far, along_z(2))

    masked = ctx_grad * row_mask[:, None].astype(bf16)
    raw = project([vision, from_core], int_table(tensor, tensor ^ 1), key_proj, value_proj)
    from_x, raw, masked, feature_near, feature_far = lax.optimization_barrier(
        (from_x, raw, masked, feature_near, feature_far)
    )
    from_xc = send(from_x, to_core)
    raw = project([from_x], int_table(tensor ^ 2), key_proj, value_proj, raw)
    from_xc, raw = lax.optimization_barrier((from_xc, raw))
    gathered = [vision, from_core, from_x, from_xc]
    vision_near, vision_far = choose(gathered, int_table(near ^ tensor, z ^ 2 ^ tensor, core))
    vision_near = send(vision_near, near_z)

    block = jnp.arange(16, dtype=jnp.int32)
    block_y, block_x = block // 4, (block % 2) * 2 + block // 2 % 2

    def order(this_core):
        across_x, across_y = block_x ^ x, block_y ^ y
        return jnp.where(this_core == 0, across_x * 4 + across_y, across_y * 4 + across_x)

    table = jnp.concatenate(
        [
            int_table(tensor ^ 3, tensor, tensor ^ 1, tensor ^ 2),
            order(1 - core).astype(jnp.int32),
            order(core).astype(jnp.int32),
            int_table(core),
        ]
    )
    grads, other_terms, own_terms = middle(
        from_xc, raw, queries, masked, key_gain, key_proj, value_proj, table
    )
    grads, other_terms, own_terms, vision_near = lax.optimization_barrier(
        (grads, other_terms, own_terms, vision_near)
    )
    core_terms = send(other_terms, to_core)
    terms = add_terms(own_terms, core_terms)
    terms, vision_near, vision_far, grads, feature_near, feature_far = lax.optimization_barrier(
        (terms, vision_near, vision_far, grads, feature_near, feature_far)
    )
    terms = [term.reshape(4, -1, half) for term in terms]
    arrived = [send(terms[i], first_stage(i)) for i in (1, 2, 3)]
    vision_far = send(vision_far, along_z(2))
    grads_z = [send(grads, along_z(i)) for i in (1, 2, 3)]
    vision_pair = send(vision_near, to_core)
    feature_pair = send(feature_near, to_core)
    feature_far_pair = send(feature_far, to_core)
    arrived, vision_far, vision_pair, feature_pair, feature_far_pair = lax.optimization_barrier(
        (arrived, vision_far, vision_pair, feature_pair, feature_far_pair)
    )
    vision_far_pair = send(vision_far, to_core)
    partial = sum([a.astype(f32) for a in arrived], terms[0].astype(f32))
    partial_bf = partial.astype(bf16)
    arrived = [send(partial_bf[i], second_stage(i)) for i in (1, 2, 3)]
    arrived, grads_z, vision_far_pair = lax.optimization_barrier((arrived, grads_z, vision_far_pair))
    token = sum([a.astype(f32) for a in arrived], partial[0]).astype(bf16)
    token = token.reshape(2, -1, half)
    mine = lax.dynamic_index_in_dim(token, core, 0, False)
    partner = send(lax.dynamic_index_in_dim(token, 1 - core, 0, False), to_core)
    token = jnp.where(
        core == 0, jnp.concatenate([mine, partner], 1), jnp.concatenate([partner, mine], 1)
    )
    tokens_z = [send(token, along_z(i)) for i in (1, 2, 3)]

    def ordered(own, by_z, axis):
        near_one = jnp.where(core == 0, by_z[0], by_z[2])
        near_two = jnp.where(core == 0, by_z[2], by_z[0])
        far_own = lax.dynamic_slice_in_dim(by_z[1], core * half, half, axis)
        far_other = lax.dynamic_slice_in_dim(by_z[1], (1 - core) * half, half, axis)
        return [own, near_one, near_two, jnp.concatenate([far_own, far_other], axis)]

    key_total, value_total = weight_grads(
        gathered,
        int_table(z ^ tensor),
        [vision_near, vision_pair, jnp.concatenate([vision_far, vision_far_pair], 0)],
        ordered(grads, grads_z, 0),
    )
    tokens_z, key_total, value_total = lax.optimization_barrier((tokens_z, key_total, value_total))
    projector_total = projector_grad(
        features,
        [feature_near, feature_pair, jnp.concatenate([feature_far, feature_far_pair], 0)],
        ordered(token, tokens_z, 1),
        int_table(z),
    )
    return (key_total[None], value_total[None], projector_total)


def solution(mesh):
    in_specs = (
        P("dp", "tensor"),
        P("dp", None),
        P("dp", "tensor"),
        P("dp", "tensor"),
        P("dp"),
        P("pipe", None, "tensor"),
        P("pipe", None, "tensor"),
        P("pipe", None),
    )
    out_specs = (P("pipe", "dp", "tensor"), P("pipe", "dp", "tensor"), P("dp", ("pipe", "tensor")))
    return jax.shard_map(shards, mesh=mesh, in_specs=in_specs, out_specs=out_specs, check_vma=False)
```

time: 510 us -> 128 us (0.25)
  waiting for transfers between devices: 409 us -> 37.9 us
  matrix products: 52.2 us -> 0 us
  Pallas kernels: 0 us -> 41.8 us
  starting transfers between devices: 0.42 us -> 34.3 us
  local copies, waits for them, and re-layouts: 31.1 us -> 4.71 us
  between operations: 13.9 us -> 0.87 us
    reduce_scatter x4 -> x0, waiting for transfers between devices: 375 us -> none  [the longest x1 137 us: shards(): lax.psum_scatter(contract_rows(key_proj, key_grad) + contract_rows(value_...]
    dot_general x11 -> x0, matrix products: 52.2 us -> none  [the longest x2 13.5 us: contract_first(): lax.dot_general(left, right, (((0,), (0,)), ((), ())), preferred_element_...]
    pallas_call x0 -> x8, Pallas kernels: none -> 41.8 us  [the longest x1 15 us: middle(): pl.pallas_call(kernel, in_specs=[in_smem] + [in_vmem] * 3 + [in_hbm] * 4,...]
    ppermute x0 -> x25, waiting for transfers between devices: none -> 37.9 us  [send(): return lax.ppermute(array, every_axis, exchange_pairs(moved))]
    ppermute x0 -> x25, starting transfers between devices: none -> 34.3 us  [send(): return lax.ppermute(array, every_axis, exchange_pairs(moved))]
    all_gather x1 -> x0, waiting for transfers between devices: 32.5 us -> none  [shards(): gathered = lax.all_gather(vision, 'tensor', axis=1, tiled=True)]
    unnamed x20 -> x24, local copies, waits for them, and re-layouts: 12.6 us -> 4.54 us
    convert_element_type x1 -> x0, local copies, waits for them, and re-layouts: 7.89 us -> none  [local_grads(): probs_bf = attn_probs.astype(jnp.bfloat16)]
  transfers between devices with their start and end apart: 5 -> 25, of which waited for: 5 -> 10; matrix products, arithmetic and copies ran while one was open for 7% -> 6% of each run, Pallas kernels for 0% -> 26%
where the time goes in v1:
time: 128 us; the launch traced here: 127 us
  Pallas kernels  41.8 us (33%)
  waiting for transfers between devices  37.9 us (30%)
  starting transfers between devices  34.3 us (27%)
  other arithmetic  7.76 us (6%)
  local copies, waits for them, and re-layouts  4.71 us (4%)
    ppermute x25, waiting for transfers between devices, send(): return lax.ppermute(array, every_axis, exchange_pairs(moved))  37.9 us
    ppermute x25, starting transfers between devices, send(): return lax.ppermute(array, every_axis, exchange_pairs(moved))  34.3 us
    pallas_call x1, Pallas kernels, middle(): pl.pallas_call(kernel, in_specs=[in_smem] + [in_vmem] * 3 + [in_hbm] * 4,...  15 us
    pallas_call x2, Pallas kernels, project(): pl.pallas_call(kernel, in_specs=[in_smem] + [in_vmem] * n + [in_hbm] * 2...  8.93 us
    pallas_call x1, Pallas kernels, weight_grads(): pl.pallas_call(kernel, grid_spec=pltpu.PrefetchScalarGridSpec(num_scalar_...  6.18 us
    pallas_call x1, Pallas kernels, projector_grad(): pl.pallas_call(kernel, grid_spec=pltpu.PrefetchScalarGridSpec(num_scalar_...  4.82 us
    unnamed x24, local copies, waits for them, and re-layouts  4.54 us
    mul x1, other arithmetic, shards(): masked = ctx_grad * row_mask[:, None].astype(bf16)  3.2 us
  transfers between devices with their start and end apart: 25, of which 10 were waited for; matrix products, arithmetic and copies ran while one was open for 6% of the time, Pallas kernels for 26%

profile of v1, /device:TPU:1, one launch (start us, length us, event | category | flops | bytes accessed | tf_op | source)
XLA Modules:
  0.0 127.3 jit_solution(9465843767796914815)
XLA Ops:
  0.6 1.5 %collective-permute-start.1 = (bf16[256,2048]{1,0:T(8,128)(2,1)}, bf16[256,2048]{1,0:T(8,128)(2,1)S(1)}, u32[]{:S(2)}, u32[]{:S(2)}) collective-permute-start(bf16[256,2048]{1,0:T(8,128)(2,1)} %refs_0_.6), channel_id=1, source_target_pairs={{0,1},{1,0},{4,5},{5,4},{2,3},{3,2},{6,7},{7,6},{8,9},{9,8},{12,13... | collective-permute-start | bytes 3145736 | tf_op jit(solution)/shard_map/ppermute | solution.py:33
  2.1 2.6 %collective-permute-start = (bf16[256,2048]{1,0:T(8,128)(2,1)}, bf16[256,2048]{1,0:T(8,128)(2,1)}, u32[]{:S(2)}, u32[]{:S(2)}) collective-permute-start(bf16[256,2048]{1,0:T(8,128)(2,1)} %refs_0_.6), channel_id=1, source_target_pairs={{0,6},{1,7},{4,2},{5,3},{2,4},{3,5},{6,0},{7,1},{8,14},{9,15},{12,... | collective-permute-start | bytes 3145736 | tf_op jit(solution)/shard_map/ppermute | solution.py:33
  4.8 2.8 %cut_features.1 = (bf16[256,1920]{1,0:T(8,128)(2,1)}, bf16[128,1920]{1,0:T(8,128)(2,1)S(1)}) custom-call(s32[3]{0:T(128)S(1)} %add_add_fusion.table, bf16[256,7680]{1,0:T(8,128)(2,1)} %refs_0_.7, bf16[256,7680]{1,0:T(8,128)(2,1)} %refs_0_.7), custom_call_target="tpu_custom_call" | custom-call | tf_op jit(solution)/shard_map/cut_features/pallas_call | solution.py:94
  7.5 3.8 %collective-permute-start.2 = (bf16[256,1920]{1,0:T(8,128)(2,1)}, bf16[256,1920]{1,0:T(8,128)(2,1)}, u32[]{:S(2)}, u32[]{:S(2)}) collective-permute-start(bf16[256,1920]{1,0:T(8,128)(2,1)} %get-tuple-element.55), channel_id=1, source_target_pairs={{0,32},{1,97},{4,36},{5,101},{2,34},{3,99},{6,38},{7,103},{8,40},{... | collective-permute-start | bytes 2949128 | tf_op jit(solution)/shard_map/ppermute | solution.py:33
  11.4 3.2 %broadcast_multiply_fusion.masked_hbm = bf16[512,2048]{1,0:T(8,128)(2,1)} fusion(bf16[512,2048]{1,0:T(8,128)(2,1)} %param.11, bf16[512]{0:T(512)(128)(2,1)S(1)} %convert_element_type.34), kind=kLoop, calls=%fused_computation.4 | loop fusion | flops 1048576 | bytes 4195328 | tf_op jit(solution)/shard_map/mul | solution.py:400
  14.6 5.1 %project.2.refs_3_ = f32[256,512]{1,0:T(8,128)S(1)} custom-call(s32[2]{0:T(128)S(1)} %pad_add_fusion.table, bf16[256,2048]{1,0:T(8,128)(2,1)S(1)} %copy-done.1, bf16[256,2048]{1,0:T(8,128)(2,1)S(1)} %collective-permute-done.1.refs_1_, bf16[8192,256]{1,0:T(8,128)(2,1)} %bitcast.43, bf16[8192,256]{1,0:T(8,128)(2,1)} %bitcast.46), custom_call_target="tpu_custom_call" | custom-call | tf_op jit(solution)/shard_map/project/pallas_call | solution.py:140
  19.7 0.8 copy-done.4
  20.5 5.3 %collective-permute-done.3 = bf16[128,1920]{1,0:T(8,128)(2,1)} collective-permute-done((bf16[128,1920]{1,0:T(8,128)(2,1)S(1)}, bf16[128,1920]{1,0:T(8,128)(2,1)}, u32[]{:S(2)}, u32[]{:S(2)}) %collective-permute-start.3) | collective-permute-done | bytes 491552 | tf_op jit(solution)/shard_map/ppermute | solution.py:33
  25.8 7.4 %collective-permute-done.2.refs_1_ = bf16[256,1920]{1,0:T(8,128)(2,1)} collective-permute-done((bf16[256,1920]{1,0:T(8,128)(2,1)}, bf16[256,1920]{1,0:T(8,128)(2,1)}, u32[]{:S(2)}, u32[]{:S(2)}) %collective-permute-start.2) | collective-permute-done | bytes 983072 | tf_op jit(solution)/shard_map/ppermute | solution.py:33
  33.2 3.1 %collective-permute-start.4 = (bf16[256,2048]{1,0:T(8,128)(2,1)}, bf16[256,2048]{1,0:T(8,128)(2,1)S(1)}, u32[]{:S(2)}, u32[]{:S(2)}) collective-permute-start(bf16[256,2048]{1,0:T(8,128)(2,1)} %collective-permute-done.refs_0_.refs_2_), channel_id=1, source_target_pairs={{0,1},{1,0},{4,5},{5,4},{2,3},{3,2},{6,7},{7,6},{8,9},{9,8},{12,13... | collective-permute-start | bytes 3145736 | tf_op jit(solution)/shard_map/ppermute | solution.py:33
  36.4 1.0 copy-done.5
  37.5 3.9 %project.3.raw_ref = f32[256,512]{1,0:T(8,128)S(1)} custom-call(s32[1]{0:T(128)} %bitcast.3.table, bf16[256,2048]{1,0:T(8,128)(2,1)} %collective-permute-done.refs_0_.refs_2_, bf16[8192,256]{1,0:T(8,128)(2,1)} %bitcast.44, bf16[8192,256]{1,0:T(8,128)(2,1)} %bitcast.47, f32[256,512]{1,0:T(8,128)S(1)} %copy-done.5), custom_call_target="tpu_custom_call" | custom-call | tf_op jit(solution)/shard_map/project/pallas_call | solution.py:140
  41.4 2.7 %choose.1 = (bf16[256,2048]{1,0:T(8,128)(2,1)}, bf16[128,2048]{1,0:T(8,128)(2,1)}) custom-call(s32[3]{0:T(128)S(1)} %add_add_fusion.1.table, bf16[256,2048]{1,0:T(8,128)(2,1)S(1)} %copy-done.1, bf16[256,2048]{1,0:T(8,128)(2,1)S(1)} %collective-permute-done.1.refs_1_, bf16[256,2048]{1,0:T(8,128)(2,1)} %collective-permute-done.refs_0_.refs_2_, ...), custom_call_target="tpu_custom_call" | custom-call | tf_op jit(solution)/shard_map/choose/pallas_call | solution.py:167
  44.2 1.0 copy-done.3
  45.2 15.0 %middle.1 = (bf16[256,512]{1,0:T(8,128)(2,1)S(1)}, bf16[8192,128]{1,0:T(8,128)(2,1)S(1)}, bf16[8192,128]{1,0:T(8,128)(2,1)S(1)}) custom-call(s32[37]{0:T(128)S(1)} %concatenate.21.table, bf16[256,2048]{1,0:T(8,128)(2,1)S(1)} %collective-permute-done.4.slice_ref.refs_3_, f32[256,512]{1,0:T(8,128)S(1)} %copy-done.3, f32[1,128]{1,0:T(1,128)S(1)} %copy-done.7, ...), custom_call_target="tpu_custom_call" | custom-call | tf_op jit(solution)/shard_map/middle/pallas_call | solution.py:266
  60.2 0.1 collective-permute-start.6
  60.3 4.1 %collective-permute-done.6.other = bf16[8192,128]{1,0:T(8,128)(2,1)S(1)} collective-permute-done((bf16[8192,128]{1,0:T(8,128)(2,1)S(1)}, bf16[8192,128]{1,0:T(8,128)(2,1)S(1)}, u32[]{:S(2)}, u32[]{:S(2)}) %collective-permute-start.6) | collective-permute-done | bytes 2097184 | tf_op jit(solution)/shard_map/ppermute | solution.py:33
  64.5 1.4 %add_terms.1 = (bf16[2048,128]{1,0:T(8,128)(2,1)S(1)}, bf16[2048,128]{1,0:T(8,128)(2,1)S(1)}, bf16[2048,128]{1,0:T(8,128)(2,1)}, bf16[2048,128]{1,0:T(8,128)(2,1)}) custom-call(bf16[8192,128]{1,0:T(8,128)(2,1)S(1)} %get-tuple-element.66.own, bf16[8192,128]{1,0:T(8,128)(2,1)S(1)} %collective-permute-done.6.other), custom_call_target="tpu_custom_call" | custom-call | tf_op jit(solution)/shard_map/add_terms/pallas_call | solution.py:297
  65.9 0.8 copy-done.6
  66.6 1.3 %collective-permute-start.7 = (bf16[4,512,128]{2,1,0:T(8,128)(2,1)S(1)}, bf16[4,512,128]{2,1,0:T(8,128)(2,1)S(1)}, u32[]{:S(2)}, u32[]{:S(2)}) collective-permute-start(bf16[4,512,128]{2,1,0:T(8,128)(2,1)S(1)} %bitcast.42), channel_id=1, source_target_pairs={{0,4},{1,9},{4,0},{5,13},{2,6},{3,11},{6,2},{7,15},{8,12},{9,1},{1... | collective-permute-start | bytes 1572872 | tf_op jit(solution)/shard_map/ppermute | solution.py:33
  67.9 0.5 collective-permute-start.13
  68.4 2.6 %collective-permute-start.8 = (bf16[4,512,128]{2,1,0:T(8,128)(2,1)}, bf16[4,512,128]{2,1,0:T(8,128)(2,1)}, u32[]{:S(2)}, u32[]{:S(2)}) collective-permute-start(bf16[4,512,128]{2,1,0:T(8,128)(2,1)} %bitcast.13), channel_id=1, source_target_pairs={{0,2},{1,17},{4,6},{5,21},{2,0},{3,19},{6,4},{7,23},{8,10},{9,25},... | collective-permute-start | bytes 1572872 | tf_op jit(solution)/shard_map/ppermute | solution.py:33
  71.1 0.8 collective-permute-done.13
  71.8 1.9 %collective-permute-start.9 = (bf16[4,512,128]{2,1,0:T(8,128)(2,1)}, bf16[4,512,128]{2,1,0:T(8,128)(2,1)}, u32[]{:S(2)}, u32[]{:S(2)}) collective-permute-start(bf16[4,512,128]{2,1,0:T(8,128)(2,1)} %bitcast.14), channel_id=1, source_target_pairs={{0,6},{1,25},{4,2},{5,29},{2,4},{3,27},{6,0},{7,31},{8,14},{9,17},... | collective-permute-start | bytes 1572872 | tf_op jit(solution)/shard_map/ppermute | solution.py:33
  73.7 1.2 collective-permute-done.7
  75.0 0.8 copy-done.8
  75.8 1.6 %collective-permute-start.10 = (bf16[128,2048]{1,0:T(8,128)(2,1)}, bf16[128,2048]{1,0:T(8,128)(2,1)}, u32[]{:S(2)}, u32[]{:S(2)}) collective-permute-start(bf16[128,2048]{1,0:T(8,128)(2,1)} %get-tuple-element.81), channel_id=1, source_target_pairs={{0,64},{1,65},{4,68},{5,69},{2,66},{3,67},{6,70},{7,71},{8,72},{9,... | collective-permute-start | bytes 1572872 | tf_op jit(solution)/shard_map/ppermute | solution.py:33
  77.4 5.8 %collective-permute-done.8 = bf16[4,512,128]{2,1,0:T(8,128)(2,1)} collective-permute-done((bf16[4,512,128]{2,1,0:T(8,128)(2,1)}, bf16[4,512,128]{2,1,0:T(8,128)(2,1)}, u32[]{:S(2)}, u32[]{:S(2)}) %collective-permute-start.8) | collective-permute-done | bytes 524320 | tf_op jit(solution)/shard_map/ppermute | solution.py:33
  83.2 2.7 %collective-permute-start.19 = (bf16[256,512]{1,0:T(8,128)(2,1)S(1)}, bf16[256,512]{1,0:T(8,128)(2,1)S(1)}, u32[]{:S(2)}, u32[]{:S(2)}) collective-permute-start(bf16[256,512]{1,0:T(8,128)(2,1)S(1)} %get-tuple-element.88.refs_7_), channel_id=1, source_target_pairs={{0,96},{1,97},{4,100},{5,101},{2,98},{3,99},{6,102},{7,103},{8,104... | collective-permute-start | bytes 786440 | tf_op jit(solution)/shard_map/ppermute | solution.py:33
  85.8 1.5 %collective-permute-done.9 = bf16[4,512,128]{2,1,0:T(8,128)(2,1)} collective-permute-done((bf16[4,512,128]{2,1,0:T(8,128)(2,1)}, bf16[4,512,128]{2,1,0:T(8,128)(2,1)}, u32[]{:S(2)}, u32[]{:S(2)}) %collective-permute-start.9) | collective-permute-done | bytes 524320 | tf_op jit(solution)/shard_map/ppermute | solution.py:33
  87.3 1.4 %collective-permute-start.18 = (bf16[256,512]{1,0:T(8,128)(2,1)S(1)}, bf16[256,512]{1,0:T(8,128)(2,1)S(1)}, u32[]{:S(2)}, u32[]{:S(2)}) collective-permute-start(bf16[256,512]{1,0:T(8,128)(2,1)S(1)} %get-tuple-element.88.refs_7_), channel_id=1, source_target_pairs={{0,64},{1,65},{4,68},{5,69},{2,66},{3,67},{6,70},{7,71},{8,72},{9,... | collective-permute-start | bytes 786440 | tf_op jit(solution)/shard_map/ppermute | solution.py:33
  88.7 1.4 %collective-permute-done.10 = bf16[128,2048]{1,0:T(8,128)(2,1)} collective-permute-done((bf16[128,2048]{1,0:T(8,128)(2,1)}, bf16[128,2048]{1,0:T(8,128)(2,1)}, u32[]{:S(2)}, u32[]{:S(2)}) %collective-permute-start.10) | collective-permute-done | bytes 524320 | tf_op jit(solution)/shard_map/ppermute | solution.py:33
  90.1 1.1 collective-permute-start.17
  91.2 2.6 %collective-permute-start.20 = (bf16[128,2048]{1,0:T(8,128)(2,1)}, bf16[128,2048]{1,0:T(8,128)(2,1)S(1)}, u32[]{:S(2)}, u32[]{:S(2)}) collective-permute-start(bf16[128,2048]{1,0:T(8,128)(2,1)} %collective-permute-done.10), channel_id=1, source_target_pairs={{0,1},{1,0},{4,5},{5,4},{2,3},{3,2},{6,7},{7,6},{8,9},{9,8},{12,13... | collective-permute-start | bytes 1572872 | tf_op jit(solution)/shard_map/ppermute | solution.py:33
  93.8 1.8 %fusion.11 = (bf16[4,512,128]{2,1,0:T(8,128)(2,1)S(1)}, f32[4,512,128]{2,1,0:T(8,128)S(1)}) fusion(bf16[4,512,128]{2,1,0:T(8,128)(2,1)} %collective-permute-done.9, bf16[4,512,128]{2,1,0:T(8,128)(2,1)} %collective-permute-done.8, bf16[4,512,128]{2,1,0:T(8,128)(2,1)} %copy-done.8, bf16[4,512,128]{2,1,0:T(8,128)(2,1)} %bitcast.41), kind=kLoop, calls=%fused_computation.50 | loop fusion | flops 2097152 | bytes 3670016 | tf_op jit(solution)/shard_map/convert_element_type | solution.py:450
  95.7 0.2 collective-permute-start.16
  95.9 6.7 %collective-permute-done.19 = bf16[256,512]{1,0:T(8,128)(2,1)S(1)} collective-permute-done((bf16[256,512]{1,0:T(8,128)(2,1)S(1)}, bf16[256,512]{1,0:T(8,128)(2,1)S(1)}, u32[]{:S(2)}, u32[]{:S(2)}) %collective-permute-start.19) | collective-permute-done | bytes 262176 | tf_op jit(solution)/shard_map/ppermute | solution.py:33
  102.6 0.6 collective-permute-start.15
  103.2 0.2 collective-permute-start.14
  103.4 1.1 pad_maximum_fusion.1.refs_3_
  104.5 3.7 %collective-permute-done.15 = bf16[512,128]{1,0:T(8,128)(2,1)S(1)} collective-permute-done((bf16[512,128]{1,0:T(8,128)(2,1)S(1)}, bf16[512,128]{1,0:T(8,128)(2,1)S(1)}, u32[]{:S(2)}, u32[]{:S(2)}) %collective-permute-start.15) | collective-permute-done | bytes 131104 | tf_op jit(solution)/shard_map/ppermute | solution.py:33
  108.3 3.2 %collective-permute-start.21 = (bf16[256,128]{1,0:T(8,128)(2,1)S(1)}, bf16[256,128]{1,0:T(8,128)(2,1)S(1)}, u32[]{:S(2)}, u32[]{:S(2)}) collective-permute-start(bf16[256,128]{1,0:T(8,128)(2,1)S(1)} %get-tuple-element.121), channel_id=1, source_target_pairs={{0,1},{1,0},{4,5},{5,4},{2,3},{3,2},{6,7},{7,6},{8,9},{9,8},{12,13... | collective-permute-start | bytes 196616 | tf_op jit(solution)/shard_map/ppermute | solution.py:33
  111.5 1.1 pad_maximum_fusion.refs_6_
  112.8 2.7 %collective-permute-start.24 = (bf16[256,256]{1,0:T(8,128)(2,1)S(1)}, bf16[256,256]{1,0:T(8,128)(2,1)S(1)}, u32[]{:S(2)}, u32[]{:S(2)}) collective-permute-start(bf16[256,256]{1,0:T(8,128)(2,1)S(1)} %maximum_select_fusion.refs_4_), channel_id=1, source_target_pairs={{0,96},{1,97},{4,100},{5,101},{2,98},{3,99},{6,102},{7,103},{8,104... | collective-permute-start | bytes 393224 | tf_op jit(solution)/shard_map/ppermute | solution.py:33
  115.5 0.5 collective-permute-start.23
  116.0 0.2 collective-permute-start.22
  116.2 6.2 %weight_grads.1 = (f32[2048,256]{1,0:T(8,128)}, f32[2048,256]{1,0:T(8,128)}) custom-call(s32[1]{0:T(128)} %bitcast.22.table, bf16[256,2048]{1,0:T(8,128)(2,1)S(1)} %copy-done.1, bf16[256,2048]{1,0:T(8,128)(2,1)S(1)} %collective-permute-done.1.refs_1_, bf16[256,2048]{1,0:T(8,128)(2,1)} %collective-permute-done.refs_0_.refs_2_, ...), custom_call_target="tpu_custom_call" | custom-call | tf_op jit(solution)/shard_map/weight_grads/pallas_call | solution.py:330
  122.5 4.8 %projector_grad.1 = f32[1920,256]{1,0:T(8,128)} custom-call(s32[1]{0:T(128)} %bitcast.25.place, bf16[256,7680]{1,0:T(8,128)(2,1)S(1)} %copy-done, bf16[256,1920]{1,0:T(8,128)(2,1)} %collective-permute-done.2.refs_1_, bf16[256,1920]{1,0:T(8,128)(2,1)} %collective-permute-done.12.refs_2_, bf16[256,1920]{1,0:T(8,128)(2,1)S(1)} %pad_maximum_fusion.1.refs_3_, ...), custom_call_target="tpu_custom_call" | custom-call | tf_op jit(solution)/shard_map/projector_grad/pallas_call | solution.py:361
  (54 shorter events, 0.7 us)
Async XLA Ops:
  0.6 14.0 %collective-permute-start.1 = (bf16[256,2048]{1,0:T(8,128)(2,1)}, bf16[256,2048]{1,0:T(8,128)(2,1)S(1)}, u32[]{:S(2)}, u32[]{:S(2)}) collective-permute-start(bf16[256,2048]{1,0:T(8,128)(2,1)} %refs_0_.6), channel_id=1, source_target_pairs={{0,1},{1,0},{4,5},{5,4},{2,3},{3,2},{6,7},{7,6},{8,9},{9,8},{12,13... | collective-permute-start | bytes 3145736 | tf_op jit(solution)/shard_map/ppermute | solution.py:33
  2.1 31.1 %collective-permute-start = (bf16[256,2048]{1,0:T(8,128)(2,1)}, bf16[256,2048]{1,0:T(8,128)(2,1)}, u32[]{:S(2)}, u32[]{:S(2)}) collective-permute-start(bf16[256,2048]{1,0:T(8,128)(2,1)} %refs_0_.6), channel_id=1, source_target_pairs={{0,6},{1,7},{4,2},{5,3},{2,4},{3,5},{6,0},{7,1},{8,14},{9,15},{12,... | collective-permute-start | bytes 3145736 | tf_op jit(solution)/shard_map/ppermute | solution.py:33
  4.8 6.5 %copy-start.11 = (s32[512]{0:T(512)S(1)}, s32[512]{0:T(512)}, u32[]{:S(2)}) copy-start(s32[512]{0:T(512)} %param.12) | copy-start | bytes 6148
  7.5 25.6 %collective-permute-start.2 = (bf16[256,1920]{1,0:T(8,128)(2,1)}, bf16[256,1920]{1,0:T(8,128)(2,1)}, u32[]{:S(2)}, u32[]{:S(2)}) collective-permute-start(bf16[256,1920]{1,0:T(8,128)(2,1)} %get-tuple-element.55), channel_id=1, source_target_pairs={{0,32},{1,97},{4,36},{5,101},{2,34},{3,99},{6,38},{7,103},{8,40},{... | collective-permute-start | bytes 2949128 | tf_op jit(solution)/shard_map/ppermute | solution.py:33
  11.3 14.5 %collective-permute-start.3 = (bf16[128,1920]{1,0:T(8,128)(2,1)S(1)}, bf16[128,1920]{1,0:T(8,128)(2,1)}, u32[]{:S(2)}, u32[]{:S(2)}) collective-permute-start(bf16[128,1920]{1,0:T(8,128)(2,1)S(1)} %get-tuple-element.56), channel_id=1, source_target_pairs={{0,64},{1,65},{4,68},{5,69},{2,66},{3,67},{6,70},{7,71},{8,72},{9,... | collective-permute-start | bytes 1474568 | tf_op jit(solution)/shard_map/ppermute | solution.py:33
  11.4 3.2 %copy-start.1 = (bf16[256,2048]{1,0:T(8,128)(2,1)S(1)}, bf16[256,2048]{1,0:T(8,128)(2,1)}, u32[]{:S(2)}) copy-start(bf16[256,2048]{1,0:T(8,128)(2,1)} %refs_0_.6) | copy-start | bytes 3145732
  19.7 0.8 copy-start.4
  33.2 8.2 %collective-permute-start.4 = (bf16[256,2048]{1,0:T(8,128)(2,1)}, bf16[256,2048]{1,0:T(8,128)(2,1)S(1)}, u32[]{:S(2)}, u32[]{:S(2)}) collective-permute-start(bf16[256,2048]{1,0:T(8,128)(2,1)} %collective-permute-done.refs_0_.refs_2_), channel_id=1, source_target_pairs={{0,1},{1,0},{4,5},{5,4},{2,3},{3,2},{6,7},{7,6},{8,9},{9,8},{12,13... | collective-permute-start | bytes 3145736 | tf_op jit(solution)/shard_map/ppermute | solution.py:33
  36.4 1.0 copy-start.5
  41.3 2.8 %copy-start.2 = (f32[256,512]{1,0:T(8,128)}, f32[256,512]{1,0:T(8,128)S(1)}, u32[]{:S(2)}) copy-start(f32[256,512]{1,0:T(8,128)S(1)} %project.3.raw_ref) | copy-start | bytes 1572868
  41.3 2.9 %copy-start.7 = (f32[1,128]{1,0:T(1,128)S(1)}, f32[1,128]{1,0:T(1,128)}, u32[]{:S(2)}) copy-start(f32[1,128]{1,0:T(1,128)} %gain_ref.1) | copy-start | bytes 1540
  44.1 16.2 %collective-permute-start.5 = (bf16[256,2048]{1,0:T(8,128)(2,1)}, bf16[256,2048]{1,0:T(8,128)(2,1)}, u32[]{:S(2)}, u32[]{:S(2)}) collective-permute-start(bf16[256,2048]{1,0:T(8,128)(2,1)} %get-tuple-element.65), channel_id=1, source_target_pairs={{0,32},{1,97},{4,36},{5,101},{2,34},{3,99},{6,38},{7,103},{8,40},{... | collective-permute-start | bytes 3145736 | tf_op jit(solution)/shard_map/ppermute | solution.py:33
  44.2 1.1 copy-start.3
  60.2 4.2 %collective-permute-start.6 = (bf16[8192,128]{1,0:T(8,128)(2,1)S(1)}, bf16[8192,128]{1,0:T(8,128)(2,1)S(1)}, u32[]{:S(2)}, u32[]{:S(2)}) collective-permute-start(bf16[8192,128]{1,0:T(8,128)(2,1)S(1)} %get-tuple-element.67), channel_id=1, source_target_pairs={{0,1},{1,0},{4,5},{5,4},{2,3},{3,2},{6,7},{7,6},{8,9},{9,8},{12,13... | collective-permute-start | bytes 6291464 | tf_op jit(solution)/shard_map/ppermute | solution.py:33
  65.9 0.8 copy-start.6
  66.6 8.3 %collective-permute-start.7 = (bf16[4,512,128]{2,1,0:T(8,128)(2,1)S(1)}, bf16[4,512,128]{2,1,0:T(8,128)(2,1)S(1)}, u32[]{:S(2)}, u32[]{:S(2)}) collective-permute-start(bf16[4,512,128]{2,1,0:T(8,128)(2,1)S(1)} %bitcast.42), channel_id=1, source_target_pairs={{0,4},{1,9},{4,0},{5,13},{2,6},{3,11},{6,2},{7,15},{8,12},{9,1},{1... | collective-permute-start | bytes 1572872 | tf_op jit(solution)/shard_map/ppermute | solution.py:33
  67.9 23.3 %collective-permute-start.11 = (bf16[256,2048]{1,0:T(8,128)(2,1)}, bf16[256,2048]{1,0:T(8,128)(2,1)}, u32[]{:S(2)}, u32[]{:S(2)}) collective-permute-start(bf16[256,2048]{1,0:T(8,128)(2,1)} %collective-permute-done.5.refs_4_), channel_id=1, source_target_pairs={{0,1},{1,0},{4,5},{5,4},{2,3},{3,2},{6,7},{7,6},{8,9},{9,8},{12,13... | collective-permute-start | bytes 3145736 | tf_op jit(solution)/shard_map/ppermute | solution.py:33
  67.9 3.9 %collective-permute-start.13 = (bf16[128,1920]{1,0:T(8,128)(2,1)}, bf16[128,1920]{1,0:T(8,128)(2,1)S(1)}, u32[]{:S(2)}, u32[]{:S(2)}) collective-permute-start(bf16[128,1920]{1,0:T(8,128)(2,1)} %collective-permute-done.3), channel_id=1, source_target_pairs={{0,1},{1,0},{4,5},{5,4},{2,3},{3,2},{6,7},{7,6},{8,9},{9,8},{12,13... | collective-permute-start | bytes 1474568 | tf_op jit(solution)/shard_map/ppermute | solution.py:33
  68.4 22.8 %collective-permute-start.12 = (bf16[256,1920]{1,0:T(8,128)(2,1)}, bf16[256,1920]{1,0:T(8,128)(2,1)}, u32[]{:S(2)}, u32[]{:S(2)}) collective-permute-start(bf16[256,1920]{1,0:T(8,128)(2,1)} %collective-permute-done.2.refs_1_), channel_id=1, source_target_pairs={{0,1},{1,0},{4,5},{5,4},{2,3},{3,2},{6,7},{7,6},{8,9},{9,8},{12,13... | collective-permute-start | bytes 2949128 | tf_op jit(solution)/shard_map/ppermute | solution.py:33
  68.4 14.7 %collective-permute-start.8 = (bf16[4,512,128]{2,1,0:T(8,128)(2,1)}, bf16[4,512,128]{2,1,0:T(8,128)(2,1)}, u32[]{:S(2)}, u32[]{:S(2)}) collective-permute-start(bf16[4,512,128]{2,1,0:T(8,128)(2,1)} %bitcast.13), channel_id=1, source_target_pairs={{0,2},{1,17},{4,6},{5,21},{2,0},{3,19},{6,4},{7,23},{8,10},{9,25},... | collective-permute-start | bytes 1572872 | tf_op jit(solution)/shard_map/ppermute | solution.py:33
  71.8 3.1 %copy-start.9 = (bf16[128,1920]{1,0:T(8,128)(2,1)}, bf16[128,1920]{1,0:T(8,128)(2,1)S(1)}, u32[]{:S(2)}) copy-start(bf16[128,1920]{1,0:T(8,128)(2,1)S(1)} %collective-permute-done.13) | copy-start | bytes 1474564
  71.8 15.5 %collective-permute-start.9 = (bf16[4,512,128]{2,1,0:T(8,128)(2,1)}, bf16[4,512,128]{2,1,0:T(8,128)(2,1)}, u32[]{:S(2)}, u32[]{:S(2)}) collective-permute-start(bf16[4,512,128]{2,1,0:T(8,128)(2,1)} %bitcast.14), channel_id=1, source_target_pairs={{0,6},{1,25},{4,2},{5,29},{2,4},{3,27},{6,0},{7,31},{8,14},{9,17},... | collective-permute-start | bytes 1572872 | tf_op jit(solution)/shard_map/ppermute | solution.py:33
  75.0 0.9 copy-start.8
  75.8 14.3 %collective-permute-start.10 = (bf16[128,2048]{1,0:T(8,128)(2,1)}, bf16[128,2048]{1,0:T(8,128)(2,1)}, u32[]{:S(2)}, u32[]{:S(2)}) collective-permute-start(bf16[128,2048]{1,0:T(8,128)(2,1)} %get-tuple-element.81), channel_id=1, source_target_pairs={{0,64},{1,65},{4,68},{5,69},{2,66},{3,67},{6,70},{7,71},{8,72},{9,... | collective-permute-start | bytes 1572872 | tf_op jit(solution)/shard_map/ppermute | solution.py:33
  83.2 19.4 %collective-permute-start.19 = (bf16[256,512]{1,0:T(8,128)(2,1)S(1)}, bf16[256,512]{1,0:T(8,128)(2,1)S(1)}, u32[]{:S(2)}, u32[]{:S(2)}) collective-permute-start(bf16[256,512]{1,0:T(8,128)(2,1)S(1)} %get-tuple-element.88.refs_7_), channel_id=1, source_target_pairs={{0,96},{1,97},{4,100},{5,101},{2,98},{3,99},{6,102},{7,103},{8,104... | collective-permute-start | bytes 786440 | tf_op jit(solution)/shard_map/ppermute | solution.py:33
  87.3 15.9 %collective-permute-start.18 = (bf16[256,512]{1,0:T(8,128)(2,1)S(1)}, bf16[256,512]{1,0:T(8,128)(2,1)S(1)}, u32[]{:S(2)}, u32[]{:S(2)}) collective-permute-start(bf16[256,512]{1,0:T(8,128)(2,1)S(1)} %get-tuple-element.88.refs_7_), channel_id=1, source_target_pairs={{0,64},{1,65},{4,68},{5,69},{2,66},{3,67},{6,70},{7,71},{8,72},{9,... | collective-permute-start | bytes 786440 | tf_op jit(solution)/shard_map/ppermute | solution.py:33
  90.1 14.4 %collective-permute-start.17 = (bf16[256,512]{1,0:T(8,128)(2,1)S(1)}, bf16[256,512]{1,0:T(8,128)(2,1)S(1)}, u32[]{:S(2)}, u32[]{:S(2)}) collective-permute-start(bf16[256,512]{1,0:T(8,128)(2,1)S(1)} %get-tuple-element.88.refs_7_), channel_id=1, source_target_pairs={{0,32},{1,33},{4,36},{5,37},{2,34},{3,35},{6,38},{7,39},{8,40},{9,... | collective-permute-start | bytes 786440 | tf_op jit(solution)/shard_map/ppermute | solution.py:33
  91.2 17.0 %collective-permute-start.20 = (bf16[128,2048]{1,0:T(8,128)(2,1)}, bf16[128,2048]{1,0:T(8,128)(2,1)S(1)}, u32[]{:S(2)}, u32[]{:S(2)}) collective-permute-start(bf16[128,2048]{1,0:T(8,128)(2,1)} %collective-permute-done.10), channel_id=1, source_target_pairs={{0,1},{1,0},{4,5},{5,4},{2,3},{3,2},{6,7},{7,6},{8,9},{9,8},{12,13... | collective-permute-start | bytes 1572872 | tf_op jit(solution)/shard_map/ppermute | solution.py:33
  93.8 9.6 %copy-start.10 = (bf16[128,1920]{1,0:T(8,128)(2,1)S(1)}, bf16[128,1920]{1,0:T(8,128)(2,1)}, u32[]{:S(2)}) copy-start(bf16[128,1920]{1,0:T(8,128)(2,1)} %copy-done.9) | copy-start | bytes 1474564
  95.7 8.8 %collective-permute-start.16 = (bf16[512,128]{1,0:T(8,128)(2,1)S(1)}, bf16[512,128]{1,0:T(8,128)(2,1)S(1)}, u32[]{:S(2)}, u32[]{:S(2)}) collective-permute-start(bf16[512,128]{1,0:T(8,128)(2,1)S(1)} %get-tuple-element.111), channel_id=1, source_target_pairs={{0,24},{1,7},{4,28},{5,3},{2,26},{3,5},{6,30},{7,1},{8,16},{9,15},... | collective-permute-start | bytes 393224 | tf_op jit(solution)/shard_map/ppermute | solution.py:33
  102.6 5.6 %collective-permute-start.15 = (bf16[512,128]{1,0:T(8,128)(2,1)S(1)}, bf16[512,128]{1,0:T(8,128)(2,1)S(1)}, u32[]{:S(2)}, u32[]{:S(2)}) collective-permute-start(bf16[512,128]{1,0:T(8,128)(2,1)S(1)} %get-tuple-element.112), channel_id=1, source_target_pairs={{0,16},{1,3},{4,20},{5,7},{2,18},{3,1},{6,22},{7,5},{8,24},{9,11},... | collective-permute-start | bytes 393224 | tf_op jit(solution)/shard_map/ppermute | solution.py:33
  103.2 5.0 %collective-permute-start.14 = (bf16[512,128]{1,0:T(8,128)(2,1)S(1)}, bf16[512,128]{1,0:T(8,128)(2,1)S(1)}, u32[]{:S(2)}, u32[]{:S(2)}) collective-permute-start(bf16[512,128]{1,0:T(8,128)(2,1)S(1)} %get-tuple-element.113), channel_id=1, source_target_pairs={{0,8},{1,5},{4,12},{5,1},{2,10},{3,7},{6,14},{7,3},{8,0},{9,13},{1... | collective-permute-start | bytes 393224 | tf_op jit(solution)/shard_map/ppermute | solution.py:33
  108.3 4.4 %collective-permute-start.21 = (bf16[256,128]{1,0:T(8,128)(2,1)S(1)}, bf16[256,128]{1,0:T(8,128)(2,1)S(1)}, u32[]{:S(2)}, u32[]{:S(2)}) collective-permute-start(bf16[256,128]{1,0:T(8,128)(2,1)S(1)} %get-tuple-element.121), channel_id=1, source_target_pairs={{0,1},{1,0},{4,5},{5,4},{2,3},{3,2},{6,7},{7,6},{8,9},{9,8},{12,13... | collective-permute-start | bytes 196616 | tf_op jit(solution)/shard_map/ppermute | solution.py:33
  112.8 9.6 %collective-permute-start.24 = (bf16[256,256]{1,0:T(8,128)(2,1)S(1)}, bf16[256,256]{1,0:T(8,128)(2,1)S(1)}, u32[]{:S(2)}, u32[]{:S(2)}) collective-permute-start(bf16[256,256]{1,0:T(8,128)(2,1)S(1)} %maximum_select_fusion.refs_4_), channel_id=1, source_target_pairs={{0,96},{1,97},{4,100},{5,101},{2,98},{3,99},{6,102},{7,103},{8,104... | collective-permute-start | bytes 393224 | tf_op jit(solution)/shard_map/ppermute | solution.py:33
  115.5 6.9 %collective-permute-start.23 = (bf16[256,256]{1,0:T(8,128)(2,1)S(1)}, bf16[256,256]{1,0:T(8,128)(2,1)S(1)}, u32[]{:S(2)}, u32[]{:S(2)}) collective-permute-start(bf16[256,256]{1,0:T(8,128)(2,1)S(1)} %maximum_select_fusion.refs_4_), channel_id=1, source_target_pairs={{0,64},{1,65},{4,68},{5,69},{2,66},{3,67},{6,70},{7,71},{8,72},{9,... | collective-permute-start | bytes 393224 | tf_op jit(solution)/shard_map/ppermute | solution.py:33
  116.0 6.4 %collective-permute-start.22 = (bf16[256,256]{1,0:T(8,128)(2,1)S(1)}, bf16[256,256]{1,0:T(8,128)(2,1)S(1)}, u32[]{:S(2)}, u32[]{:S(2)}) collective-permute-start(bf16[256,256]{1,0:T(8,128)(2,1)S(1)} %maximum_select_fusion.refs_4_), channel_id=1, source_target_pairs={{0,32},{1,33},{4,36},{5,37},{2,34},{3,35},{6,38},{7,39},{8,40},{9,... | collective-permute-start | bytes 393224 | tf_op jit(solution)/shard_map/ppermute | solution.py:33
  116.2 6.3 %copy-start = (bf16[256,7680]{1,0:T(8,128)(2,1)S(1)}, bf16[256,7680]{1,0:T(8,128)(2,1)}, u32[]{:S(2)}) copy-start(bf16[256,7680]{1,0:T(8,128)(2,1)} %refs_0_.7) | copy-start | bytes 11796484

commit v2 on v1

v2 whole, which is shorter than its diff:
```python
import jax
import jax.numpy as jnp
from jax import lax
from jax.experimental import pallas as pl
from jax.experimental.pallas import tpu as pltpu
from jax.sharding import PartitionSpec as P

norm_eps = 1e-05
every_axis = ("dp", "pipe", "tensor")
bf16 = jnp.bfloat16
f32 = jnp.float32
head_size = 128
score_scale = head_size**-0.5
log2_e = 1.4426950408889634
megabyte = 2**20


def flat_index(z, y, x, core):
    return z * 32 + y * 8 + (x & 1) * 4 + (x >> 1) * 2 + core


def exchange_pairs(moved):
    pairs = []
    for z in range(4):
        for y in range(4):
            for x in range(4):
                for core in range(2):
                    target = moved(z, y, x, core)
                    if target is not None:
                        pairs.append((flat_index(z, y, x, core), flat_index(*target)))
    return pairs


def send(array, moved):
    return lax.ppermute(array, every_axis, exchange_pairs(moved))


def to_core(z, y, x, core):
    return z, y, x, 1 - core


def to_near_x(z, y, x, core):
    return z, y, x ^ 3, core


def first_stage(k):
    return lambda z, y, x, core: (z, y, x ^ k, core) if core == 0 else (z, y ^ k, x, core)


def second_stage(k):
    return lambda z, y, x, core: (z, y ^ k, x, core) if core == 0 else (z, y, x ^ k, core)


def along_z(k):
    return lambda z, y, x, core: (z ^ k, y, x, core)


def near_z(z, y, x, core):
    return (z ^ 1 if core == 0 else z ^ 3), y, x, core


def vision_near(k):
    return lambda z, y, x, core: None if core == z % 2 else (z ^ k, y, x, core)


def vision_far(z, y, x, core):
    return (z ^ 2, y, x, 1 - core) if core == z % 2 else None


def to_near_y(z, y, x, core):
    return z, y ^ 1, x, core


params = pltpu.CompilerParams(vmem_limit_bytes=14 * megabyte)
small_params = pltpu.CompilerParams(vmem_limit_bytes=4 * megabyte)
large_params = pltpu.CompilerParams(vmem_limit_bytes=26 * megabyte)
def dot(left, right, left_dim=1, right_dim=0):
    return lax.dot_general(
        left, right, (((left_dim,), (right_dim,)), ((), ())), preferred_element_type=f32
    )


at_near, at_far, at_quarter, at_tensor, at_swapped, at_z, at_core = 0, 1, 2, 3, 7, 8, 9
at_own, at_on_parity, at_row_parity, at_other_order, at_own_order = 10, 11, 12, 13, 29

in_vmem = pl.BlockSpec(memory_space=pltpu.VMEM)
in_smem = pl.BlockSpec(memory_space=pltpu.SMEM)


in_hbm = pl.BlockSpec(memory_space=pltpu.HBM)
anywhere = pl.BlockSpec(memory_space=pl.ANY)


def far_away(array):
    return pltpu.with_memory_space_constraint(array, pltpu.HBM)


def chosen_spec(rows, columns, k, place):
    return pl.BlockSpec(
        (rows, columns), lambda i, table: (0, jnp.where(table[place] == k, i, 0))
    )


token_shape = jax.ShapeDtypeStruct((8, 128), f32)


def cut_features(features, table):
    rows, width = features.shape
    width //= 4
    quarter = rows // 4

    def kernel(table, source, near, far, sems):
        def columns(k):
            return pl.ds(pl.multiple_of(table[k] * width, 128), width)

        lines = pl.ds(pl.multiple_of(table[at_quarter] * quarter, quarter), quarter)
        copies = [
            pltpu.make_async_copy(source.at[lines, columns(at_far)], far, sems.at[0]),
            pltpu.make_async_copy(source.at[:, columns(at_near)], near, sems.at[1]),
        ]
        for copy in copies:
            copy.start()
        for copy in copies:
            copy.wait()

    return pl.pallas_call(
        kernel,
        in_specs=[in_smem, in_hbm],
        out_specs=[in_vmem] * 2,
        out_shape=[jax.ShapeDtypeStruct((r, width), bf16) for r in (rows, quarter)],
        scratch_shapes=[pltpu.SemaphoreType.DMA((2,))],
        compiler_params=small_params,
        name="cut_features",
    )(table, far_away(features))


def mask_rows(ctx_grad, mask):
    def kernel(grad_ref, mask_ref, out):
        out[...] = grad_ref[...] * mask_ref[...].astype(bf16)

    rows, width = ctx_grad.shape
    block = pl.BlockSpec((rows, width // 4), lambda i: (0, i))
    return pl.pallas_call(
        kernel,
        grid=(4,),
        in_specs=[block, pl.BlockSpec((rows, 1), lambda i: (0, 0))],
        out_specs=block,
        out_shape=jax.ShapeDtypeStruct(ctx_grad.shape, bf16),
        compiler_params=small_params,
        name="mask_rows",
    )(ctx_grad, mask)


def project(slices, table, key_proj, value_proj):
    rows, width = slices[0].shape
    columns = key_proj.shape[1]
    n = len(slices)

    def kernel(table, *refs):
        slice_refs, projections, (out, done, held, sems) = refs[:n], refs[n : n + 2], refs[n + 2 :]
        done[...] = jnp.zeros_like(done)
        copies = []
        for i in range(n):
            lines = pl.ds(pl.multiple_of(table[at_tensor + i] * width, width), width)
            for j in range(2):
                copy = pltpu.make_async_copy(projections[j].at[lines, :], held.at[i, j], sems.at[i, j])
                copy.start()
                copies.append(copy)
        for j in range(2):
            total = 0.0
            for i in range(n):
                copies[2 * i + j].wait()
                total += dot(slice_refs[i][...], held[i, j])
            out[:, j * columns : (j + 1) * columns] = total

    return pl.pallas_call(
        kernel,
        in_specs=[in_smem] + [in_vmem] * n + [in_hbm] * 2,
        out_specs=[in_vmem] * 2,
        out_shape=[jax.ShapeDtypeStruct((rows, 2 * columns), f32), token_shape],
        scratch_shapes=[pltpu.VMEM((n, 2, width, columns), bf16), pltpu.SemaphoreType.DMA((n, 2))],
        compiler_params=params,
        name="project",
    )(table, *slices, far_away(key_proj), far_away(value_proj))


def choose(own, other, table, after):
    def kernel(table, first, second, *rest):
        one, two, sems = rest[-3:]
        for k, pair in enumerate(((first, second), (second, first))):

            @pl.when(table[at_swapped] == k)
            def _():
                copies = [
                    pltpu.make_async_copy(source, target, sems.at[i])
                    for i, (source, target) in enumerate(zip(pair, (one, two)))
                ]
                for copy in copies:
                    copy.start()
                for copy in copies:
                    copy.wait()

    return pl.pallas_call(
        kernel,
        in_specs=[in_smem] + [in_vmem] * 2 + [anywhere] * len(after),
        out_specs=[in_hbm] * 2,
        out_shape=[pltpu.HBM(own.shape, bf16)] * 2,
        scratch_shapes=[pltpu.SemaphoreType.DMA((2,))],
        compiler_params=small_params,
        name="choose",
    )(table, own, other, *after)


def middle(last_slices, raw, queries, masked, gain, key_proj, value_proj, table):
    vis_rows, width = last_slices[0].shape
    depth, columns = key_proj.shape
    kv_heads = columns // head_size
    text_rows = queries.shape[0]
    group = queries.shape[1] // head_size // kv_heads
    group_width = group * head_size
    half = vis_rows // 2
    blocks = 16
    lines = depth // blocks
    unroll = 4

    def kernel(
        table, slice_one, slice_two, raw_ref, gain_ref, query_ref, masked_ref, key_ref, value_ref,
        grads, other_terms, own_terms,
        keys, values, sums, turned,
    ):
        projected = [raw_ref[:, :columns], raw_ref[:, columns:]]
        for i, slice_ref in enumerate((slice_one, slice_two)):
            place = pl.ds(pl.multiple_of(table[at_tensor + 2 + i] * width, width), width)
            projected[0] += dot(slice_ref[...], key_ref[place, :])
            projected[1] += dot(slice_ref[...], value_ref[place, :])
        key_all, value_all = projected[0], projected[1].astype(bf16)
        for head in range(kv_heads):
            lanes = slice(head * head_size, (head + 1) * head_size)
            key_raw = key_all[:, lanes]
            inv_rms = lax.rsqrt(jnp.mean(key_raw * key_raw, -1, keepdims=True) + norm_eps)
            keys[...] = (key_raw * inv_rms * gain_ref[...]).astype(bf16)
            values[...] = value_all[:, lanes]
            sums[...] = jnp.zeros_like(sums)
            def step(i, carry):
                for j in range(unroll):
                    text = (head * group + i * unroll + j) * head_size
                    text = pl.ds(pl.multiple_of(text, head_size), head_size)
                    query = query_ref[:, text]
                    grad = masked_ref[:, text]
                    exp_scores = jnp.exp2(dot(keys[...], query, 1, 1) * (score_scale * log2_e))
                    prob_grad = dot(values[...], grad, 1, 1)
                    probs = exp_scores * (1.0 / jnp.sum(exp_scores, 0, keepdims=True))
                    row_delta = jnp.sum(probs * prob_grad, 0, keepdims=True)
                    sums[1] += dot(probs.astype(bf16), grad)
                    sums[0] += dot((probs * (prob_grad - row_delta)).astype(bf16), query)
                return carry

            lax.fori_loop(0, group // unroll, step, 0)
            scaled = sums[0] * score_scale * gain_ref[...]
            mean = jnp.mean(scaled * key_raw, -1, keepdims=True)
            key_grad = inv_rms * (scaled - key_raw * inv_rms * inv_rms * mean)
            grads[:, lanes] = key_grad.astype(bf16)
            grads[:, columns + head * head_size : columns + (head + 1) * head_size] = sums[1].astype(bf16)

        for i in range(2):
            here = (table[at_core] + i) % 2 * half
            turned[i * half : (i + 1) * half, :] = grads[pl.ds(pl.multiple_of(here, half), half), :]

        def token_step(i, carry):
            here = pl.ds(pl.multiple_of(i * lines, lines), lines)
            other_place = pl.multiple_of(table[at_other_order + i] * lines, lines)
            own_place = pl.multiple_of(table[at_own_order + i] * lines, lines)
            term = dot(key_ref[here, :], turned[:, :columns], 1, 1)
            term += dot(value_ref[here, :], turned[:, columns:], 1, 1)
            own_terms[pl.ds(own_place, lines), :] = term[:, :half].astype(bf16)
            other_terms[pl.ds(other_place, lines), :] = term[:, half:].astype(bf16)
            return carry

        lax.fori_loop(0, blocks, token_step, 0, unroll=4)

    return pl.pallas_call(
        kernel,
        in_specs=[in_smem] + [in_vmem] * 8,
        out_specs=[in_vmem] * 3,
        out_shape=[jax.ShapeDtypeStruct((vis_rows, 2 * columns), bf16)]
        + [jax.ShapeDtypeStruct((depth, half), bf16)] * 2,
        scratch_shapes=[
            pltpu.VMEM((vis_rows, head_size), bf16),
            pltpu.VMEM((vis_rows, head_size), bf16),
            pltpu.VMEM((2, vis_rows, head_size), f32),
            pltpu.VMEM((vis_rows, 2 * columns), bf16),
        ],
        compiler_params=large_params,
        name="middle",
    )(table, *last_slices, raw, gain, queries, masked, key_proj, value_proj)


def wait_for(array, after):
    return pl.pallas_call(
        lambda *refs: None,
        in_specs=[anywhere] * (1 + len(after)),
        out_specs=anywhere,
        out_shape=jax.ShapeDtypeStruct(array.shape, array.dtype),
        input_output_aliases={0: 0},
        compiler_params=small_params,
        name="wait_for",
    )(array, *after)


def add_terms(own_terms, core_terms, after):
    rows, tokens = own_terms.shape
    part = rows // 4

    def kernel(own, other, *rest):
        for i, out in enumerate(rest[-4:]):
            lines = slice(i * part, (i + 1) * part)
            out[...] = (own[lines, :].astype(f32) + other[lines, :].astype(f32)).astype(bf16)

    return pl.pallas_call(
        kernel,
        in_specs=[in_vmem] * 2 + [anywhere] * len(after),
        out_specs=[in_vmem] * 4,
        out_shape=[jax.ShapeDtypeStruct((part, tokens), bf16)] * 4,
        compiler_params=params,
        name="add_terms",
    )(own_terms, core_terms, *after)


def add_first(parts, after):
    rows, tokens = parts[0].shape
    block = rows // 4

    def kernel(*refs):
        own, *outs = refs[-4:]
        for i, out in enumerate((own, *outs)):
            lines = slice(i * block, (i + 1) * block)
            out[...] = sum(ref[lines, :].astype(f32) for ref in refs[:4]).astype(out.dtype)

    return pl.pallas_call(
        kernel,
        in_specs=[in_vmem] * 4 + [anywhere] * len(after),
        out_specs=[in_vmem] * 4,
        out_shape=[jax.ShapeDtypeStruct((block, tokens), f32)]
        + [jax.ShapeDtypeStruct((block, tokens), bf16)] * 3,
        compiler_params=small_params,
        name="add_first",
    )(*parts, *after)


def add_second(own, arrived, table, after):
    rows, tokens = own.shape
    half = rows // 2

    def kernel(table, *refs):
        for i, out in enumerate(refs[-2:]):
            lines = pl.ds(pl.multiple_of((table[at_core] + i) % 2 * half, half), half)
            out[...] = sum(ref[lines, :].astype(f32) for ref in refs[:4]).astype(bf16)

    return pl.pallas_call(
        kernel,
        in_specs=[in_smem] + [in_vmem] * 4 + [anywhere] * len(after),
        out_specs=[in_vmem] * 2,
        out_shape=[jax.ShapeDtypeStruct((half, tokens), bf16)] * 2,
        compiler_params=small_params,
        name="add_second",
    )(table, own, *arrived, *after)


def weight_grads(gathered, by_z, pairs, table, grads, after):
    rows, width = gathered[0].shape
    columns = grads[0].shape[1] // 2
    steps = 4
    block = width // steps
    choices = [[(at_own, k, v) for k, v in enumerate(gathered)]]
    choices += [
        [(at_on_parity, int(i < 2), by_z[i]), (at_on_parity, int(i == 2), pairs[i])] for i in range(3)
    ]
    flat = sum(choices, [])

    def kernel(table, *refs):
        vision_refs, grad_refs, (key_out, value_out, done, picked) = refs[: len(flat)], refs[len(flat) : -5], refs[-4:]
        done[...] = jnp.zeros_like(done)
        total = 0.0
        at = 0
        for i, options in enumerate(choices):
            for place, value, _ in options:

                @pl.when(table[place] == value)
                def _(ref=vision_refs[at]):
                    picked[i] = ref[...]

                at += 1
        for i in range(4):
            total += dot(picked[i], grad_refs[i][...], 0, 0)
        key_out[...] = total[:, :columns]
        value_out[...] = total[:, columns:]

    return pl.pallas_call(
        kernel,
        grid_spec=pltpu.PrefetchScalarGridSpec(
            num_scalar_prefetch=1,
            grid=(steps,),
            in_specs=[chosen_spec(rows, block, value, place) for place, value, _ in flat]
            + [pl.BlockSpec(g.shape, lambda i, table: (0, 0)) for g in grads]
            + [anywhere],
            out_specs=[pl.BlockSpec((block, columns), lambda i, table: (i, 0))] * 2
            + [pl.BlockSpec(token_shape.shape, lambda i, table: (0, 0))],
            scratch_shapes=[pltpu.VMEM((4, rows, block), bf16)],
        ),
        out_shape=[jax.ShapeDtypeStruct((width, columns), f32)] * 2 + [token_shape],
        compiler_params=params,
        name="weight_grads",
    )(table, *[v for _, _, v in flat], *grads, after)


def join_tokens(mine, partner, table):
    rows, half = mine.shape

    def kernel(table, one, two, out):
        for k, pair in enumerate(((one, two), (two, one))):

            @pl.when(table[at_core] == k)
            def _():
                for i, ref in enumerate(pair):
                    out[:, i * half : (i + 1) * half] = ref[...]

    return pl.pallas_call(
        kernel,
        in_specs=[in_smem] + [in_vmem] * 2,
        out_specs=in_vmem,
        out_shape=jax.ShapeDtypeStruct((rows, 2 * half), bf16),
        compiler_params=small_params,
        name="join_tokens",
    )(table, mine, partner)


def turn_features(features, near, near_pair, far, table, after):
    rows, width = near.shape
    quarter = rows // 4
    steps = 3
    block = width // steps

    def kernel(table, own_ref, near_ref, near_pair_ref, *rest):
        out, done, joined = rest[-3:]
        done[...] = jnp.zeros_like(done)
        for i, ref in enumerate(rest[:4]):
            place = (table[at_core] + i // 2) % 2 * 2 + (table[at_row_parity] + i % 2) % 2
            joined[pl.ds(pl.multiple_of(place * quarter, quarter), quarter), :] = ref[...]
        for i, ref in enumerate((own_ref, near_ref, near_pair_ref, joined)):
            out[:, i * rows : (i + 1) * rows] = ref[...].T

    return pl.pallas_call(
        kernel,
        grid_spec=pltpu.PrefetchScalarGridSpec(
            num_scalar_prefetch=1,
            grid=(steps,),
            in_specs=[pl.BlockSpec((rows, block), lambda i, table: (0, table[at_z] * steps + i))]
            + [pl.BlockSpec((rows, block), lambda i, table: (0, i))] * 2
            + [pl.BlockSpec((quarter, block), lambda i, table: (0, i))] * 4
            + [anywhere],
            out_specs=[
                pl.BlockSpec((block, 4 * rows), lambda i, table: (i, 0)),
                pl.BlockSpec(token_shape.shape, lambda i, table: (0, 0)),
            ],
            scratch_shapes=[pltpu.VMEM((rows, block), bf16)],
        ),
        out_shape=[jax.ShapeDtypeStruct((width, 4 * rows), bf16), token_shape],
        compiler_params=params,
        name="turn_features",
    )(table, far_away(features), near, near_pair, *far, after)


def projector_grad(turned, token, tokens_z, table, after):
    width, depth = turned.shape
    columns = token.shape[0]
    rows = depth // 4
    steps = 3
    block = width // steps

    def kernel(table, feature_ref, *refs):
        out, near = refs[-2:]
        for k, pair in enumerate(((1, 3), (3, 1))):

            @pl.when(table[at_core] == k)
            def _():
                for i in range(2):
                    near[i] = refs[pair[i]][...]

        total = 0.0
        for i, term in enumerate((refs[0][...], near[0], near[1], refs[2][...])):
            total += dot(feature_ref[:, i * rows : (i + 1) * rows], term, 1, 1)
        out[...] = total

    return pl.pallas_call(
        kernel,
        grid_spec=pltpu.PrefetchScalarGridSpec(
            num_scalar_prefetch=1,
            grid=(steps,),
            in_specs=[pl.BlockSpec((block, depth), lambda i, table: (i, 0))]
            + [pl.BlockSpec(token.shape, lambda i, table: (0, 0))] * 4
            + [anywhere],
            out_specs=pl.BlockSpec((block, columns), lambda i, table: (i, 0)),
            scratch_shapes=[pltpu.VMEM((2, *token.shape), bf16)],
        ),
        out_shape=jax.ShapeDtypeStruct((width, columns), f32),
        compiler_params=params,
        name="projector_grad",
    )(table, turned, token, *tokens_z, after)


def integers(z, pipe, tensor):
    y, core = pipe // 2, tensor % 2
    x = (tensor // 2) * 2 + pipe % 2
    on_parity = (core == z % 2).astype(jnp.int32)
    values = [jnp.where(core == 0, z ^ 1, z ^ 3), z ^ 2, 2 * core + y % 2]
    values += [tensor, tensor ^ 1, tensor ^ 2, tensor ^ 3]
    values += [(tensor // 2 == z // 2).astype(jnp.int32) ^ (1 - on_parity), z, core]
    values += [z ^ tensor, on_parity, y % 2]
    for this_core in (1 - core, core):
        for block in range(16):
            across_y, across_x = y ^ (block // 4), x ^ (block % 2 * 2 + block // 2 % 2)
            values.append(
                jnp.where(this_core == 0, across_x * 4 + across_y, across_y * 4 + across_x)
            )
    return jnp.stack(values).astype(jnp.int32)


def shards(vision, features, queries, ctx_grad, row_mask, key_weight, value_weight, key_gain):
    key_proj, value_proj = key_weight[0], value_weight[0]
    table = integers(lax.axis_index("dp"), lax.axis_index("pipe"), lax.axis_index("tensor"))

    from_core = send(vision, to_core)
    from_x = send(vision, to_near_x)

    feature_near, feature_far = cut_features(features, table)
    feature_near = send(feature_near, near_z)
    feature_far = send(feature_far, along_z(2))

    masked = mask_rows(ctx_grad, row_mask[:, None])
    raw, done = project([vision, from_core], table, key_proj, value_proj)
    from_x = wait_for(from_x, [done, masked, feature_near, feature_far])
    from_xc = send(from_x, to_core)
    vision_one, vision_two = choose(vision, from_x, table, [])
    gathered = [vision, from_core, from_x, from_xc]
    by_z = [send(vision_one, vision_near(1)), send(vision_two, vision_near(3))]
    feature_far = [feature_far, send(feature_far, to_near_y)]
    grads, other_terms, own_terms = middle(
        [from_x, from_xc], raw, queries, masked, key_gain, key_proj, value_proj, table
    )

    core_terms = send(wait_for(other_terms, by_z + feature_far), to_core)
    by_z.append(send(vision_one, vision_far))
    feature_far += [send(part, to_core) for part in feature_far]
    terms = add_terms(own_terms, core_terms, feature_far)
    arrived = [send(terms[i], first_stage(i)) for i in (1, 2, 3)]
    feature_near = wait_for(feature_near, [terms[0]])
    feature_pair = send(feature_near, to_core)
    own, *partial = add_first([terms[0], *arrived], [by_z[2], feature_pair])
    grads = wait_for(grads, [own])
    grads_z = {i: send(grads, along_z(i)) for i in (1, 2, 3)}
    arrived = [send(partial[i - 1], second_stage(i)) for i in (1, 2, 3)]
    turned, done = turn_features(features, feature_near, feature_pair, feature_far, table, own)
    mine, other = add_second(own, arrived, table, [done, *grads_z.values()])
    token = join_tokens(mine, send(other, to_core), table)
    tokens_z = [send(token, along_z(i)) for i in (1, 2, 3)]

    by_z = [wait_for(array, [token]) for array in by_z]
    pairs = [send(array, to_core) for array in by_z]
    key_total, value_total, done = weight_grads(
        gathered, by_z, pairs, table, [grads, *(grads_z[i] for i in (1, 3, 2))], token
    )
    projector_total = projector_grad(turned, token, tokens_z, table, done)
    return (key_total[None], value_total[None], projector_total)


def solution(mesh):
    in_specs = (
        P("dp", "tensor"),
        P("dp", None),
        P("dp", "tensor"),
        P("dp", "tensor"),
        P("dp"),
        P("pipe", None, "tensor"),
        P("pipe", None, "tensor"),
        P("pipe", None),
    )
    out_specs = (P("pipe", "dp", "tensor"), P("pipe", "dp", "tensor"), P("dp", ("pipe", "tensor")))
    return jax.shard_map(shards, mesh=mesh, in_specs=in_specs, out_specs=out_specs, check_vma=False)
```

time: 128 us -> 114 us (0.89)
  other arithmetic: 7.76 us -> 0 us
  waiting for transfers between devices: 37.9 us -> 31.6 us
  starting transfers between devices: 34.3 us -> 38.2 us
  Pallas kernels: 41.8 us -> 38.6 us
    ppermute x25 -> x29, waiting for transfers between devices: 37.9 us -> 31.6 us  [send(): return lax.ppermute(array, every_axis, exchange_pairs(moved))]
    ppermute x25 -> x29, starting transfers between devices: 34.3 us -> 38.2 us  [send(): return lax.ppermute(array, every_axis, exchange_pairs(moved))]
    mul x1 -> x0, other arithmetic: 3.2 us -> none  [shards(): masked = ctx_grad * row_mask[:, None].astype(bf16)]
    concatenate x3 -> x0, other arithmetic: 2.26 us -> none  [the longest x1 1.14 us: shards(): jnp.concatenate([vision_far, vision_far_pair], 0)]
    convert_element_type x3 -> x0, other arithmetic: 1.91 us -> none  [the longest x1 1.85 us: shards(): partial_bf = partial.astype(bf16)]
    pallas_call x1, Pallas kernels: 4.82 us -> 3.36 us  [projector_grad(): pl.pallas_call(kernel, grid_spec=pltpu.PrefetchScalarGridSpec(num_scalar_...]
    pallas_call x6 -> x17, Pallas kernels: 30.8 us -> 29.4 us  [the longest x1 13.2 us: middle(): pl.pallas_call(kernel, in_specs=[in_smem] + [in_vmem] * 8, out_specs=[in_...]
    unnamed x24 -> x18, local copies, waits for them, and re-layouts: 4.54 us -> 3.5 us
  transfers between devices with their start and end apart: 25 -> 29, of which waited for: 10 -> 11; matrix products, arithmetic and copies ran while one was open for 6% -> 1% of each run, Pallas kernels for 26% -> 30%
where the time goes in v2:
time: 114 us
  Pallas kernels  38.6 us (34%)
  starting transfers between devices  38.2 us (34%)
  waiting for transfers between devices  31.6 us (28%)
  local copies, waits for them, and re-layouts  4.53 us (4%)
    ppermute x29, starting transfers between devices, send(): return lax.ppermute(array, every_axis, exchange_pairs(moved))  38.2 us
    ppermute x29, waiting for transfers between devices, send(): return lax.ppermute(array, every_axis, exchange_pairs(moved))  31.6 us
    pallas_call x1, Pallas kernels, middle(): pl.pallas_call(kernel, in_specs=[in_smem] + [in_vmem] * 8, out_specs=[in_...  13.2 us
    pallas_call x1, Pallas kernels, weight_grads(): pl.pallas_call(kernel, grid_spec=pltpu.PrefetchScalarGridSpec(num_scalar_...  5.89 us
    pallas_call x1, Pallas kernels, project(): pl.pallas_call(kernel, in_specs=[in_smem] + [in_vmem] * n + [in_hbm] * 2,...  5.33 us
    unnamed x18, local copies, waits for them, and re-layouts  3.5 us
    pallas_call x1, Pallas kernels, turn_features(): pl.pallas_call(kernel, grid_spec=pltpu.PrefetchScalarGridSpec(num_scalar_...  3.37 us
    pallas_call x1, Pallas kernels, projector_grad(): pl.pallas_call(kernel, grid_spec=pltpu.PrefetchScalarGridSpec(num_scalar_...  3.36 us
  transfers between devices with their start and end apart: 29, of which 11 were waited for; matrix products, arithmetic and copies ran while one was open for 1% of the time, Pallas kernels for 30%

profile of v2, /device:TPU:1, one launch (start us, length us, event | category | flops | bytes accessed | tf_op | source)
XLA Modules:
  0.0 113.8 jit_solution(16326885281541524221)
XLA Ops:
  0.6 1.5 %collective-permute-start = (bf16[256,2048]{1,0:T(8,128)(2,1)}, bf16[256,2048]{1,0:T(8,128)(2,1)S(1)}, u32[]{:S(2)}, u32[]{:S(2)}) collective-permute-start(bf16[256,2048]{1,0:T(8,128)(2,1)} %refs_0_.3), channel_id=1, source_target_pairs={{0,1},{1,0},{4,5},{5,4},{2,3},{3,2},{6,7},{7,6},{8,9},{9,8},{12,13... | collective-permute-start | bytes 3145736 | tf_op jit(solution)/shard_map/ppermute | solution.py:35
  2.1 2.6 %collective-permute-start.1 = (bf16[256,2048]{1,0:T(8,128)(2,1)}, bf16[256,2048]{1,0:T(8,128)(2,1)S(1)}, u32[]{:S(2)}, u32[]{:S(2)}) collective-permute-start(bf16[256,2048]{1,0:T(8,128)(2,1)} %refs_0_.3), channel_id=1, source_target_pairs={{0,6},{1,7},{4,2},{5,3},{2,4},{3,5},{6,0},{7,1},{8,14},{9,15},{12,... | collective-permute-start | bytes 3145736 | tf_op jit(solution)/shard_map/ppermute | solution.py:35
  4.9 2.9 %cut_features.1 = (bf16[256,1920]{1,0:T(8,128)(2,1)}, bf16[64,1920]{1,0:T(8,128)(2,1)}) custom-call(s32[45]{0:T(128)S(1)} %stack.183.table, bf16[256,7680]{1,0:T(8,128)(2,1)} %own_ref.1), custom_call_target="tpu_custom_call" | custom-call | tf_op jit(solution)/shard_map/cut_features/pallas_call | solution.py:126
  7.8 3.8 %collective-permute-start.2 = (bf16[256,1920]{1,0:T(8,128)(2,1)}, bf16[256,1920]{1,0:T(8,128)(2,1)S(1)}, u32[]{:S(2)}, u32[]{:S(2)}) collective-permute-start(bf16[256,1920]{1,0:T(8,128)(2,1)} %get-tuple-element.28), channel_id=1, source_target_pairs={{0,32},{1,97},{4,36},{5,101},{2,34},{3,99},{6,38},{7,103},{8,40},{... | collective-permute-start | bytes 2949128 | tf_op jit(solution)/shard_map/ppermute | solution.py:35
  11.7 0.9 copy.18.mask_ref
  12.5 1.6 %copy-done.3 = bf16[512,2048]{1,0:T(8,128)(2,1)S(1)} copy-done((bf16[512,2048]{1,0:T(8,128)(2,1)S(1)}, bf16[512,2048]{1,0:T(8,128)(2,1)}, u32[]{:S(2)}) %copy-start.3) | copy-done | bytes 2097176
  14.1 0.9 copy-done.5
  15.1 0.8 mask_rows.1.refs_2_.masked_ref
  15.9 0.4 copy-done.2
  16.3 5.3 %project.1 = (f32[256,512]{1,0:T(8,128)S(1)}, f32[8,128]{1,0:T(8,128)S(1)}) custom-call(s32[45]{0:T(128)S(1)} %stack.183.table, bf16[256,2048]{1,0:T(8,128)(2,1)S(1)} %copy-done.2, bf16[256,2048]{1,0:T(8,128)(2,1)S(1)} %collective-permute-done.refs_1_, bf16[8192,256]{1,0:T(8,128)(2,1)} %bitcast.50, bf16[8192,256]{1,0:T(8,128)(2,1)} %bitcast.52), custom_call_target="tpu_custom_call" | custom-call | tf_op jit(solution)/shard_map/project/pallas_call | solution.py:176
  21.6 6.6 %collective-permute-done.2.refs_3_.refs_0_ = bf16[256,1920]{1,0:T(8,128)(2,1)S(1)} collective-permute-done((bf16[256,1920]{1,0:T(8,128)(2,1)}, bf16[256,1920]{1,0:T(8,128)(2,1)S(1)}, u32[]{:S(2)}, u32[]{:S(2)}) %collective-permute-start.2) | collective-permute-done | bytes 983072 | tf_op jit(solution)/shard_map/ppermute | solution.py:35
  28.3 3.1 %collective-permute-start.4 = (bf16[256,2048]{1,0:T(8,128)(2,1)S(1)}, bf16[256,2048]{1,0:T(8,128)(2,1)S(1)}, u32[]{:S(2)}, u32[]{:S(2)}) collective-permute-start(bf16[256,2048]{1,0:T(8,128)(2,1)S(1)} %wait_for.7.second.slice_one.refs_2_), channel_id=1, source_target_pairs={{0,1},{1,0},{4,5},{5,4},{2,3},{3,2},{6,7},{7,6},{8,9},{9,8},{12,13... | collective-permute-start | bytes 3145736 | tf_op jit(solution)/shard_map/ppermute | solution.py:35
  31.4 1.9 %choose.1 = (bf16[256,2048]{1,0:T(8,128)(2,1)}, bf16[256,2048]{1,0:T(8,128)(2,1)}) custom-call(s32[45]{0:T(128)S(1)} %stack.183.table, bf16[256,2048]{1,0:T(8,128)(2,1)S(1)} %copy-done.2, bf16[256,2048]{1,0:T(8,128)(2,1)S(1)} %wait_for.7.second.slice_one.refs_2_), custom_call_target="tpu_custom_call" | custom-call | tf_op jit(solution)/shard_map/choose/pallas_call | solution.py:203
  33.3 1.5 %collective-permute-start.5 = (bf16[256,2048]{1,0:T(8,128)(2,1)}, bf16[256,2048]{1,0:T(8,128)(2,1)S(1)}, u32[]{:S(2)}, u32[]{:S(2)}) collective-permute-start(bf16[256,2048]{1,0:T(8,128)(2,1)} %get-tuple-element.30), channel_id=1, source_target_pairs={{1,33},{5,37},{3,35},{7,39},{9,41},{13,45},{11,43},{15,47},{17,49}... | collective-permute-start | bytes 3145736 | tf_op jit(solution)/shard_map/ppermute | solution.py:35
  34.8 3.4 %collective-permute-start.6 = (bf16[256,2048]{1,0:T(8,128)(2,1)}, bf16[256,2048]{1,0:T(8,128)(2,1)S(1)}, u32[]{:S(2)}, u32[]{:S(2)}) collective-permute-start(bf16[256,2048]{1,0:T(8,128)(2,1)} %get-tuple-element.34), channel_id=1, source_target_pairs={{1,97},{5,101},{3,99},{7,103},{9,105},{13,109},{11,107},{15,111},{... | collective-permute-start | bytes 3145736 | tf_op jit(solution)/shard_map/ppermute | solution.py:35
  38.2 1.4 %collective-permute-start.7 = (bf16[64,1920]{1,0:T(8,128)(2,1)S(1)}, bf16[64,1920]{1,0:T(8,128)(2,1)S(1)}, u32[]{:S(2)}, u32[]{:S(2)}) collective-permute-start(bf16[64,1920]{1,0:T(8,128)(2,1)S(1)} %collective-permute-done.3.refs_4_.refs_3_.rest_0_), channel_id=1, source_target_pairs={{0,8},{1,9},{4,12},{5,13},{2,10},{3,11},{6,14},{7,15},{8,0},{9,1},... | collective-permute-start | bytes 737288 | tf_op jit(solution)/shard_map/ppermute | solution.py:35
  39.6 13.2 %middle.1 = (bf16[256,512]{1,0:T(8,128)(2,1)S(1)}, bf16[8192,128]{1,0:T(8,128)(2,1)S(1)}, bf16[8192,128]{1,0:T(8,128)(2,1)S(1)}) custom-call(s32[45]{0:T(128)S(1)} %stack.183.table, bf16[256,2048]{1,0:T(8,128)(2,1)S(1)} %wait_for.7.second.slice_one.refs_2_, bf16[256,2048]{1,0:T(8,128)(2,1)S(1)} %collective-permute-done.4.slice_two.refs_3_, ...), custom_call_target="tpu_custom_call" | custom-call | tf_op jit(solution)/shard_map/middle/pallas_call | solution.py:281
  52.9 0.5 collective-permute-start.9
  53.5 0.5 copy-done.8
  54.1 1.3 %collective-permute-start.14 = (bf16[256,2048]{1,0:T(8,128)(2,1)S(1)}, bf16[256,2048]{1,0:T(8,128)(2,1)S(1)}, u32[]{:S(2)}, u32[]{:S(2)}) collective-permute-start(bf16[256,2048]{1,0:T(8,128)(2,1)S(1)} %copy-done.8), channel_id=1, source_target_pairs={{0,65},{4,69},{2,67},{6,71},{8,73},{12,77},{10,75},{14,79},{16,81}... | collective-permute-start | bytes 3145736 | tf_op jit(solution)/shard_map/ppermute | solution.py:35
  55.3 2.1 %collective-permute-done.9.rest_2_ = bf16[64,1920]{1,0:T(8,128)(2,1)S(1)} collective-permute-done((bf16[64,1920]{1,0:T(8,128)(2,1)S(1)}, bf16[64,1920]{1,0:T(8,128)(2,1)S(1)}, u32[]{:S(2)}, u32[]{:S(2)}) %collective-permute-start.9) | collective-permute-done | bytes 245792 | tf_op jit(solution)/shard_map/ppermute | solution.py:35
  57.4 0.4 collective-permute-done.10.rest_3_
  57.8 0.5 add_terms.1
  58.5 1.1 collective-permute-start.11
  59.6 2.6 %collective-permute-start.12 = (bf16[2048,128]{1,0:T(8,128)(2,1)S(1)}, bf16[2048,128]{1,0:T(8,128)(2,1)S(1)}, u32[]{:S(2)}, u32[]{:S(2)}) collective-permute-start(bf16[2048,128]{1,0:T(8,128)(2,1)S(1)} %get-tuple-element.37), channel_id=1, source_target_pairs={{0,2},{1,17},{4,6},{5,21},{2,0},{3,19},{6,4},{7,23},{8,10},{9,25},... | collective-permute-start | bytes 1572872 | tf_op jit(solution)/shard_map/ppermute | solution.py:35
  62.4 9.6 %collective-permute-done.14.refs_4_.refs_0_ = bf16[256,2048]{1,0:T(8,128)(2,1)S(1)} collective-permute-done((bf16[256,2048]{1,0:T(8,128)(2,1)S(1)}, bf16[256,2048]{1,0:T(8,128)(2,1)S(1)}, u32[]{:S(2)}, u32[]{:S(2)}) %collective-permute-start.14) | collective-permute-done | bytes 1048608 | tf_op jit(solution)/shard_map/ppermute | solution.py:35
  72.0 2.8 %collective-permute-done.12.refs_2_ = bf16[2048,128]{1,0:T(8,128)(2,1)S(1)} collective-permute-done((bf16[2048,128]{1,0:T(8,128)(2,1)S(1)}, bf16[2048,128]{1,0:T(8,128)(2,1)S(1)}, u32[]{:S(2)}, u32[]{:S(2)}) %collective-permute-start.12) | collective-permute-done | bytes 524320 | tf_op jit(solution)/shard_map/ppermute | solution.py:35
  74.8 2.6 %collective-permute-done.13.refs_3_ = bf16[2048,128]{1,0:T(8,128)(2,1)S(1)} collective-permute-done((bf16[2048,128]{1,0:T(8,128)(2,1)S(1)}, bf16[2048,128]{1,0:T(8,128)(2,1)S(1)}, u32[]{:S(2)}, u32[]{:S(2)}) %collective-permute-start.13) | collective-permute-done | bytes 524320 | tf_op jit(solution)/shard_map/ppermute | solution.py:35
  77.4 0.3 add_first.1
  77.8 2.1 %collective-permute-start.20 = (bf16[256,512]{1,0:T(8,128)(2,1)S(1)}, bf16[256,512]{1,0:T(8,128)(2,1)S(1)}, u32[]{:S(2)}, u32[]{:S(2)}) collective-permute-start(bf16[256,512]{1,0:T(8,128)(2,1)S(1)} %wait_for.10.refs_10_), channel_id=1, source_target_pairs={{0,64},{1,65},{4,68},{5,69},{2,66},{3,67},{6,70},{7,71},{8,72},{9,... | collective-permute-start | bytes 786440 | tf_op jit(solution)/shard_map/ppermute | solution.py:35
  80.0 1.7 %collective-permute-start.21 = (bf16[256,512]{1,0:T(8,128)(2,1)S(1)}, bf16[256,512]{1,0:T(8,128)(2,1)S(1)}, u32[]{:S(2)}, u32[]{:S(2)}) collective-permute-start(bf16[256,512]{1,0:T(8,128)(2,1)S(1)} %wait_for.10.refs_10_), channel_id=1, source_target_pairs={{0,96},{1,97},{4,100},{5,101},{2,98},{3,99},{6,102},{7,103},{8,104... | collective-permute-start | bytes 786440 | tf_op jit(solution)/shard_map/ppermute | solution.py:35
  81.7 2.6 %collective-permute-start.17 = (bf16[512,128]{1,0:T(8,128)(2,1)S(1)}, bf16[512,128]{1,0:T(8,128)(2,1)S(1)}, u32[]{:S(2)}, u32[]{:S(2)}) collective-permute-start(bf16[512,128]{1,0:T(8,128)(2,1)S(1)} %get-tuple-element.41), channel_id=1, source_target_pairs={{0,16},{1,3},{4,20},{5,7},{2,18},{3,1},{6,22},{7,5},{8,24},{9,11},... | collective-permute-start | bytes 393224 | tf_op jit(solution)/shard_map/ppermute | solution.py:35
  84.3 1.1 collective-permute-start.18
  85.5 3.4 %turn_features.1 = (bf16[1920,1024]{1,0:T(8,128)(2,1)S(1)}, f32[8,128]{1,0:T(8,128)S(1)}) custom-call(s32[45]{0:T(128)S(1)} %stack.183.table, bf16[256,7680]{1,0:T(8,128)(2,1)} %own_ref.1, bf16[256,1920]{1,0:T(8,128)(2,1)S(1)} %wait_for.9.near_ref, bf16[256,1920]{1,0:T(8,128)(2,1)S(1)} %collective-permute-done.15.refs_5_.near_pair_ref, ...), custom_call_target="tpu_custom_call" | custom-call | tf_op jit(solution)/shard_map/turn_features/pallas_call | solution.py:452
  88.8 0.8 collective-permute-done.18.refs_3_
  89.7 3.7 %collective-permute-done.21.refs_7_.refs_12_ = bf16[256,512]{1,0:T(8,128)(2,1)S(1)} collective-permute-done((bf16[256,512]{1,0:T(8,128)(2,1)S(1)}, bf16[256,512]{1,0:T(8,128)(2,1)S(1)}, u32[]{:S(2)}, u32[]{:S(2)}) %collective-permute-start.21) | collective-permute-done | bytes 262176 | tf_op jit(solution)/shard_map/ppermute | solution.py:35
  93.4 0.6 add_second.1
  94.0 2.3 %collective-permute-start.22 = (bf16[256,128]{1,0:T(8,128)(2,1)S(1)}, bf16[256,128]{1,0:T(8,128)(2,1)S(1)}, u32[]{:S(2)}, u32[]{:S(2)}) collective-permute-start(bf16[256,128]{1,0:T(8,128)(2,1)S(1)} %get-tuple-element.46), channel_id=1, source_target_pairs={{0,1},{1,0},{4,5},{5,4},{2,3},{3,2},{6,7},{7,6},{8,9},{9,8},{12,13... | collective-permute-start | bytes 196616 | tf_op jit(solution)/shard_map/ppermute | solution.py:35
  96.2 0.9 collective-permute-done.22.two
  97.1 0.6 join_tokens.1.refs_1_.refs_14_.refs_0_
  97.7 0.4 collective-permute-start.25
  98.3 0.4 collective-permute-start.23
  98.7 2.9 %collective-permute-start.27 = (bf16[256,256]{1,0:T(8,128)(2,1)S(1)}, bf16[256,256]{1,0:T(8,128)(2,1)S(1)}, u32[]{:S(2)}, u32[]{:S(2)}) collective-permute-start(bf16[256,256]{1,0:T(8,128)(2,1)S(1)} %join_tokens.1.refs_1_.refs_14_.refs_0_), channel_id=1, source_target_pairs={{0,64},{1,65},{4,68},{5,69},{2,66},{3,67},{6,70},{7,71},{8,72},{9,... | collective-permute-start | bytes 393224 | tf_op jit(solution)/shard_map/ppermute | solution.py:35
  101.6 1.0 collective-permute-start.28
  102.5 0.9 collective-permute-done.23.refs_5_
  103.5 5.9 %weight_grads.1 = (f32[2048,256]{1,0:T(8,128)}, f32[2048,256]{1,0:T(8,128)}, f32[8,128]{1,0:T(8,128)S(1)}) custom-call(s32[45]{0:T(128)S(1)} %stack.183.table, bf16[256,2048]{1,0:T(8,128)(2,1)S(1)} %copy-done.2, bf16[256,2048]{1,0:T(8,128)(2,1)S(1)} %collective-permute-done.refs_1_, bf16[256,2048]{1,0:T(8,128)(2,1)S(1)} %wait_for.7.second.slice_one.refs_2_, ...), custom_call_target="tpu_custom_call" | custom-call | tf_op jit(solution)/shard_map/weight_grads/pallas_call | solution.py:398
  109.4 1.1 collective-permute-done.28.refs_3_
  110.4 3.4 %projector_grad.1 = f32[1920,256]{1,0:T(8,128)} custom-call(s32[45]{0:T(128)S(1)} %stack.183.table, bf16[1920,1024]{1,0:T(8,128)(2,1)S(1)} %get-tuple-element.49.feature_ref, bf16[256,256]{1,0:T(8,128)(2,1)S(1)} %join_tokens.1.refs_1_.refs_14_.refs_0_, bf16[256,256]{1,0:T(8,128)(2,1)S(1)} %collective-permute-done.26.refs_1_, ...), custom_call_target="tpu_custom_call" | custom-call | tf_op jit(solution)/shard_map/projector_grad/pallas_call | solution.py:494
  (49 shorter events, 1.1 us)
Async XLA Ops:
  0.6 15.2 %collective-permute-start = (bf16[256,2048]{1,0:T(8,128)(2,1)}, bf16[256,2048]{1,0:T(8,128)(2,1)S(1)}, u32[]{:S(2)}, u32[]{:S(2)}) collective-permute-start(bf16[256,2048]{1,0:T(8,128)(2,1)} %refs_0_.3), channel_id=1, source_target_pairs={{0,1},{1,0},{4,5},{5,4},{2,3},{3,2},{6,7},{7,6},{8,9},{9,8},{12,13... | collective-permute-start | bytes 3145736 | tf_op jit(solution)/shard_map/ppermute | solution.py:35
  2.1 26.1 %collective-permute-start.1 = (bf16[256,2048]{1,0:T(8,128)(2,1)}, bf16[256,2048]{1,0:T(8,128)(2,1)S(1)}, u32[]{:S(2)}, u32[]{:S(2)}) collective-permute-start(bf16[256,2048]{1,0:T(8,128)(2,1)} %refs_0_.3), channel_id=1, source_target_pairs={{0,6},{1,7},{4,2},{5,3},{2,4},{3,5},{6,0},{7,1},{8,14},{9,15},{12,... | collective-permute-start | bytes 3145736 | tf_op jit(solution)/shard_map/ppermute | solution.py:35
  4.7 6.9 %copy-start.7 = (s32[512]{0:T(512)S(1)}, s32[512]{0:T(512)}, u32[]{:S(2)}) copy-start(s32[512]{0:T(512)} %param.12) | copy-start | bytes 6148
  7.8 20.5 %collective-permute-start.2 = (bf16[256,1920]{1,0:T(8,128)(2,1)}, bf16[256,1920]{1,0:T(8,128)(2,1)S(1)}, u32[]{:S(2)}, u32[]{:S(2)}) collective-permute-start(bf16[256,1920]{1,0:T(8,128)(2,1)} %get-tuple-element.28), channel_id=1, source_target_pairs={{0,32},{1,97},{4,36},{5,101},{2,34},{3,99},{6,38},{7,103},{8,40},{... | collective-permute-start | bytes 2949128 | tf_op jit(solution)/shard_map/ppermute | solution.py:35
  11.6 10.0 %collective-permute-start.3 = (bf16[64,1920]{1,0:T(8,128)(2,1)}, bf16[64,1920]{1,0:T(8,128)(2,1)S(1)}, u32[]{:S(2)}, u32[]{:S(2)}) collective-permute-start(bf16[64,1920]{1,0:T(8,128)(2,1)} %get-tuple-element.29), channel_id=1, source_target_pairs={{0,64},{1,65},{4,68},{5,69},{2,66},{3,67},{6,70},{7,71},{8,72},{9,... | collective-permute-start | bytes 737288 | tf_op jit(solution)/shard_map/ppermute | solution.py:35
  12.5 1.6 %copy-start.3 = (bf16[512,2048]{1,0:T(8,128)(2,1)S(1)}, bf16[512,2048]{1,0:T(8,128)(2,1)}, u32[]{:S(2)}) copy-start(bf16[512,2048]{1,0:T(8,128)(2,1)} %grad_ref.1) | copy-start | bytes 6291460
  14.1 0.9 copy-start.5
  15.1 1.2 %copy-start.2 = (bf16[256,2048]{1,0:T(8,128)(2,1)S(1)}, bf16[256,2048]{1,0:T(8,128)(2,1)}, u32[]{:S(2)}) copy-start(bf16[256,2048]{1,0:T(8,128)(2,1)} %refs_0_.3) | copy-start | bytes 3145732
  16.3 23.3 %copy-start.1 = (bf16[1,8192,256]{2,1,0:T(8,128)(2,1)S(1)}, bf16[1,8192,256]{2,1,0:T(8,128)(2,1)}, u32[]{:S(2)}) copy-start(bf16[1,8192,256]{2,1,0:T(8,128)(2,1)} %param.14) | copy-start | bytes 12582916
  28.3 11.3 %copy-start = (bf16[1,8192,256]{2,1,0:T(8,128)(2,1)S(1)}, bf16[1,8192,256]{2,1,0:T(8,128)(2,1)}, u32[]{:S(2)}) copy-start(bf16[1,8192,256]{2,1,0:T(8,128)(2,1)} %param.13) | copy-start | bytes 12582916
  28.3 11.3 %copy-start.4 = (bf16[512,2048]{1,0:T(8,128)(2,1)S(1)}, bf16[512,2048]{1,0:T(8,128)(2,1)}, u32[]{:S(2)}) copy-start(bf16[512,2048]{1,0:T(8,128)(2,1)} %query_ref.1) | copy-start | bytes 6291460
  28.3 11.3 %copy-start.6 = (f32[1,128]{1,0:T(1,128)S(1)}, f32[1,128]{1,0:T(1,128)}, u32[]{:S(2)}) copy-start(f32[1,128]{1,0:T(1,128)} %gain_ref.1) | copy-start | bytes 1540
  28.3 11.3 %collective-permute-start.4 = (bf16[256,2048]{1,0:T(8,128)(2,1)S(1)}, bf16[256,2048]{1,0:T(8,128)(2,1)S(1)}, u32[]{:S(2)}, u32[]{:S(2)}) collective-permute-start(bf16[256,2048]{1,0:T(8,128)(2,1)S(1)} %wait_for.7.second.slice_one.refs_2_), channel_id=1, source_target_pairs={{0,1},{1,0},{4,5},{5,4},{2,3},{3,2},{6,7},{7,6},{8,9},{9,8},{12,13... | collective-permute-start | bytes 3145736 | tf_op jit(solution)/shard_map/ppermute | solution.py:35
  33.3 19.5 %collective-permute-start.5 = (bf16[256,2048]{1,0:T(8,128)(2,1)}, bf16[256,2048]{1,0:T(8,128)(2,1)S(1)}, u32[]{:S(2)}, u32[]{:S(2)}) collective-permute-start(bf16[256,2048]{1,0:T(8,128)(2,1)} %get-tuple-element.30), channel_id=1, source_target_pairs={{1,33},{5,37},{3,35},{7,39},{9,41},{13,45},{11,43},{15,47},{17,49}... | collective-permute-start | bytes 3145736 | tf_op jit(solution)/shard_map/ppermute | solution.py:35
  34.8 18.0 %collective-permute-start.6 = (bf16[256,2048]{1,0:T(8,128)(2,1)}, bf16[256,2048]{1,0:T(8,128)(2,1)S(1)}, u32[]{:S(2)}, u32[]{:S(2)}) collective-permute-start(bf16[256,2048]{1,0:T(8,128)(2,1)} %get-tuple-element.34), channel_id=1, source_target_pairs={{1,97},{5,101},{3,99},{7,103},{9,105},{13,109},{11,107},{15,111},{... | collective-permute-start | bytes 3145736 | tf_op jit(solution)/shard_map/ppermute | solution.py:35
  38.2 14.6 %collective-permute-start.7 = (bf16[64,1920]{1,0:T(8,128)(2,1)S(1)}, bf16[64,1920]{1,0:T(8,128)(2,1)S(1)}, u32[]{:S(2)}, u32[]{:S(2)}) collective-permute-start(bf16[64,1920]{1,0:T(8,128)(2,1)S(1)} %collective-permute-done.3.refs_4_.refs_3_.rest_0_), channel_id=1, source_target_pairs={{0,8},{1,9},{4,12},{5,13},{2,10},{3,11},{6,14},{7,15},{8,0},{9,1},... | collective-permute-start | bytes 737288 | tf_op jit(solution)/shard_map/ppermute | solution.py:35
  52.8 1.2 %copy-start.8 = (bf16[256,2048]{1,0:T(8,128)(2,1)S(1)}, bf16[256,2048]{1,0:T(8,128)(2,1)}, u32[]{:S(2)}) copy-start(bf16[256,2048]{1,0:T(8,128)(2,1)} %get-tuple-element.30) | copy-start | bytes 3145732
  52.8 4.9 %collective-permute-start.8 = (bf16[8192,128]{1,0:T(8,128)(2,1)S(1)}, bf16[8192,128]{1,0:T(8,128)(2,1)S(1)}, u32[]{:S(2)}, u32[]{:S(2)}) collective-permute-start(bf16[8192,128]{1,0:T(8,128)(2,1)S(1)} %wait_for.8), channel_id=1, source_target_pairs={{0,1},{1,0},{4,5},{5,4},{2,3},{3,2},{6,7},{7,6},{8,9},{9,8},{12,13... | collective-permute-start | bytes 6291464 | tf_op jit(solution)/shard_map/ppermute | solution.py:35
  52.9 4.5 %collective-permute-start.9 = (bf16[64,1920]{1,0:T(8,128)(2,1)S(1)}, bf16[64,1920]{1,0:T(8,128)(2,1)S(1)}, u32[]{:S(2)}, u32[]{:S(2)}) collective-permute-start(bf16[64,1920]{1,0:T(8,128)(2,1)S(1)} %collective-permute-done.3.refs_4_.refs_3_.rest_0_), channel_id=1, source_target_pairs={{0,1},{1,0},{4,5},{5,4},{2,3},{3,2},{6,7},{7,6},{8,9},{9,8},{12,13... | collective-permute-start | bytes 737288 | tf_op jit(solution)/shard_map/ppermute | solution.py:35
  53.4 4.4 %collective-permute-start.10 = (bf16[64,1920]{1,0:T(8,128)(2,1)S(1)}, bf16[64,1920]{1,0:T(8,128)(2,1)S(1)}, u32[]{:S(2)}, u32[]{:S(2)}) collective-permute-start(bf16[64,1920]{1,0:T(8,128)(2,1)S(1)} %collective-permute-done.7.refs_4_.rest_1_), channel_id=1, source_target_pairs={{0,1},{1,0},{4,5},{5,4},{2,3},{3,2},{6,7},{7,6},{8,9},{9,8},{12,13... | collective-permute-start | bytes 737288 | tf_op jit(solution)/shard_map/ppermute | solution.py:35
  54.1 17.9 %collective-permute-start.14 = (bf16[256,2048]{1,0:T(8,128)(2,1)S(1)}, bf16[256,2048]{1,0:T(8,128)(2,1)S(1)}, u32[]{:S(2)}, u32[]{:S(2)}) collective-permute-start(bf16[256,2048]{1,0:T(8,128)(2,1)S(1)} %copy-done.8), channel_id=1, source_target_pairs={{0,65},{4,69},{2,67},{6,71},{8,73},{12,77},{10,75},{14,79},{16,81}... | collective-permute-start | bytes 3145736 | tf_op jit(solution)/shard_map/ppermute | solution.py:35
  58.3 19.1 %collective-permute-start.15 = (bf16[256,1920]{1,0:T(8,128)(2,1)S(1)}, bf16[256,1920]{1,0:T(8,128)(2,1)S(1)}, u32[]{:S(2)}, u32[]{:S(2)}) collective-permute-start(bf16[256,1920]{1,0:T(8,128)(2,1)S(1)} %wait_for.9.near_ref), channel_id=1, source_target_pairs={{0,1},{1,0},{4,5},{5,4},{2,3},{3,2},{6,7},{7,6},{8,9},{9,8},{12,13... | collective-permute-start | bytes 2949128 | tf_op jit(solution)/shard_map/ppermute | solution.py:35
  58.5 13.5 %collective-permute-start.11 = (bf16[2048,128]{1,0:T(8,128)(2,1)S(1)}, bf16[2048,128]{1,0:T(8,128)(2,1)S(1)}, u32[]{:S(2)}, u32[]{:S(2)}) collective-permute-start(bf16[2048,128]{1,0:T(8,128)(2,1)S(1)} %get-tuple-element.36), channel_id=1, source_target_pairs={{0,4},{1,9},{4,0},{5,13},{2,6},{3,11},{6,2},{7,15},{8,12},{9,1},{1... | collective-permute-start | bytes 1572872 | tf_op jit(solution)/shard_map/ppermute | solution.py:35
  59.6 15.1 %collective-permute-start.12 = (bf16[2048,128]{1,0:T(8,128)(2,1)S(1)}, bf16[2048,128]{1,0:T(8,128)(2,1)S(1)}, u32[]{:S(2)}, u32[]{:S(2)}) collective-permute-start(bf16[2048,128]{1,0:T(8,128)(2,1)S(1)} %get-tuple-element.37), channel_id=1, source_target_pairs={{0,2},{1,17},{4,6},{5,21},{2,0},{3,19},{6,4},{7,23},{8,10},{9,25},... | collective-permute-start | bytes 1572872 | tf_op jit(solution)/shard_map/ppermute | solution.py:35
  62.2 15.2 %collective-permute-start.13 = (bf16[2048,128]{1,0:T(8,128)(2,1)S(1)}, bf16[2048,128]{1,0:T(8,128)(2,1)S(1)}, u32[]{:S(2)}, u32[]{:S(2)}) collective-permute-start(bf16[2048,128]{1,0:T(8,128)(2,1)S(1)} %get-tuple-element.38), channel_id=1, source_target_pairs={{0,6},{1,25},{4,2},{5,29},{2,4},{3,27},{6,0},{7,31},{8,14},{9,17},... | collective-permute-start | bytes 1572872 | tf_op jit(solution)/shard_map/ppermute | solution.py:35
  77.6 6.7 %collective-permute-start.16 = (bf16[512,128]{1,0:T(8,128)(2,1)S(1)}, bf16[512,128]{1,0:T(8,128)(2,1)S(1)}, u32[]{:S(2)}, u32[]{:S(2)}) collective-permute-start(bf16[512,128]{1,0:T(8,128)(2,1)S(1)} %get-tuple-element.40), channel_id=1, source_target_pairs={{0,8},{1,5},{4,12},{5,1},{2,10},{3,7},{6,14},{7,3},{8,0},{9,13},{1... | collective-permute-start | bytes 393224 | tf_op jit(solution)/shard_map/ppermute | solution.py:35
  77.8 11.9 %collective-permute-start.19 = (bf16[256,512]{1,0:T(8,128)(2,1)S(1)}, bf16[256,512]{1,0:T(8,128)(2,1)S(1)}, u32[]{:S(2)}, u32[]{:S(2)}) collective-permute-start(bf16[256,512]{1,0:T(8,128)(2,1)S(1)} %wait_for.10.refs_10_), channel_id=1, source_target_pairs={{0,32},{1,33},{4,36},{5,37},{2,34},{3,35},{6,38},{7,39},{8,40},{9,... | collective-permute-start | bytes 786440 | tf_op jit(solution)/shard_map/ppermute | solution.py:35
  77.8 11.8 %collective-permute-start.20 = (bf16[256,512]{1,0:T(8,128)(2,1)S(1)}, bf16[256,512]{1,0:T(8,128)(2,1)S(1)}, u32[]{:S(2)}, u32[]{:S(2)}) collective-permute-start(bf16[256,512]{1,0:T(8,128)(2,1)S(1)} %wait_for.10.refs_10_), channel_id=1, source_target_pairs={{0,64},{1,65},{4,68},{5,69},{2,66},{3,67},{6,70},{7,71},{8,72},{9,... | collective-permute-start | bytes 786440 | tf_op jit(solution)/shard_map/ppermute | solution.py:35
  80.0 13.4 %collective-permute-start.21 = (bf16[256,512]{1,0:T(8,128)(2,1)S(1)}, bf16[256,512]{1,0:T(8,128)(2,1)S(1)}, u32[]{:S(2)}, u32[]{:S(2)}) collective-permute-start(bf16[256,512]{1,0:T(8,128)(2,1)S(1)} %wait_for.10.refs_10_), channel_id=1, source_target_pairs={{0,96},{1,97},{4,100},{5,101},{2,98},{3,99},{6,102},{7,103},{8,104... | collective-permute-start | bytes 786440 | tf_op jit(solution)/shard_map/ppermute | solution.py:35
  81.7 7.1 %collective-permute-start.17 = (bf16[512,128]{1,0:T(8,128)(2,1)S(1)}, bf16[512,128]{1,0:T(8,128)(2,1)S(1)}, u32[]{:S(2)}, u32[]{:S(2)}) collective-permute-start(bf16[512,128]{1,0:T(8,128)(2,1)S(1)} %get-tuple-element.41), channel_id=1, source_target_pairs={{0,16},{1,3},{4,20},{5,7},{2,18},{3,1},{6,22},{7,5},{8,24},{9,11},... | collective-permute-start | bytes 393224 | tf_op jit(solution)/shard_map/ppermute | solution.py:35
  84.3 5.3 %collective-permute-start.18 = (bf16[512,128]{1,0:T(8,128)(2,1)S(1)}, bf16[512,128]{1,0:T(8,128)(2,1)S(1)}, u32[]{:S(2)}, u32[]{:S(2)}) collective-permute-start(bf16[512,128]{1,0:T(8,128)(2,1)S(1)} %get-tuple-element.42), channel_id=1, source_target_pairs={{0,24},{1,7},{4,28},{5,3},{2,26},{3,5},{6,30},{7,1},{8,16},{9,15},... | collective-permute-start | bytes 393224 | tf_op jit(solution)/shard_map/ppermute | solution.py:35
  94.0 3.2 %collective-permute-start.22 = (bf16[256,128]{1,0:T(8,128)(2,1)S(1)}, bf16[256,128]{1,0:T(8,128)(2,1)S(1)}, u32[]{:S(2)}, u32[]{:S(2)}) collective-permute-start(bf16[256,128]{1,0:T(8,128)(2,1)S(1)} %get-tuple-element.46), channel_id=1, source_target_pairs={{0,1},{1,0},{4,5},{5,4},{2,3},{3,2},{6,7},{7,6},{8,9},{9,8},{12,13... | collective-permute-start | bytes 196616 | tf_op jit(solution)/shard_map/ppermute | solution.py:35
  97.7 3.8 %collective-permute-start.25 = (bf16[256,2048]{1,0:T(8,128)(2,1)S(1)}, bf16[256,2048]{1,0:T(8,128)(2,1)S(1)}, u32[]{:S(2)}, u32[]{:S(2)}) collective-permute-start(bf16[256,2048]{1,0:T(8,128)(2,1)S(1)} %wait_for.13.refs_8_), channel_id=1, source_target_pairs={{0,1},{1,0},{4,5},{5,4},{2,3},{3,2},{6,7},{7,6},{8,9},{9,8},{12,13... | collective-permute-start | bytes 3145736 | tf_op jit(solution)/shard_map/ppermute | solution.py:35
  98.2 4.4 %collective-permute-start.24 = (bf16[256,2048]{1,0:T(8,128)(2,1)S(1)}, bf16[256,2048]{1,0:T(8,128)(2,1)S(1)}, u32[]{:S(2)}, u32[]{:S(2)}) collective-permute-start(bf16[256,2048]{1,0:T(8,128)(2,1)S(1)} %wait_for.12.refs_6_), channel_id=1, source_target_pairs={{0,1},{1,0},{4,5},{5,4},{2,3},{3,2},{6,7},{7,6},{8,9},{9,8},{12,13... | collective-permute-start | bytes 3145736 | tf_op jit(solution)/shard_map/ppermute | solution.py:35
  98.3 5.1 %collective-permute-start.23 = (bf16[256,2048]{1,0:T(8,128)(2,1)S(1)}, bf16[256,2048]{1,0:T(8,128)(2,1)S(1)}, u32[]{:S(2)}, u32[]{:S(2)}) collective-permute-start(bf16[256,2048]{1,0:T(8,128)(2,1)S(1)} %wait_for.11.refs_4_), channel_id=1, source_target_pairs={{0,1},{1,0},{4,5},{5,4},{2,3},{3,2},{6,7},{7,6},{8,9},{9,8},{12,13... | collective-permute-start | bytes 3145736 | tf_op jit(solution)/shard_map/ppermute | solution.py:35
  98.7 10.7 %collective-permute-start.26 = (bf16[256,256]{1,0:T(8,128)(2,1)S(1)}, bf16[256,256]{1,0:T(8,128)(2,1)S(1)}, u32[]{:S(2)}, u32[]{:S(2)}) collective-permute-start(bf16[256,256]{1,0:T(8,128)(2,1)S(1)} %join_tokens.1.refs_1_.refs_14_.refs_0_), channel_id=1, source_target_pairs={{0,32},{1,33},{4,36},{5,37},{2,34},{3,35},{6,38},{7,39},{8,40},{9,... | collective-permute-start | bytes 393224 | tf_op jit(solution)/shard_map/ppermute | solution.py:35
  98.7 10.7 %collective-permute-start.27 = (bf16[256,256]{1,0:T(8,128)(2,1)S(1)}, bf16[256,256]{1,0:T(8,128)(2,1)S(1)}, u32[]{:S(2)}, u32[]{:S(2)}) collective-permute-start(bf16[256,256]{1,0:T(8,128)(2,1)S(1)} %join_tokens.1.refs_1_.refs_14_.refs_0_), channel_id=1, source_target_pairs={{0,64},{1,65},{4,68},{5,69},{2,66},{3,67},{6,70},{7,71},{8,72},{9,... | collective-permute-start | bytes 393224 | tf_op jit(solution)/shard_map/ppermute | solution.py:35
  101.6 8.9 %collective-permute-start.28 = (bf16[256,256]{1,0:T(8,128)(2,1)S(1)}, bf16[256,256]{1,0:T(8,128)(2,1)S(1)}, u32[]{:S(2)}, u32[]{:S(2)}) collective-permute-start(bf16[256,256]{1,0:T(8,128)(2,1)S(1)} %join_tokens.1.refs_1_.refs_14_.refs_0_), channel_id=1, source_target_pairs={{0,96},{1,97},{4,100},{5,101},{2,98},{3,99},{6,102},{7,103},{8,104... | collective-permute-start | bytes 393224 | tf_op jit(solution)/shard_map/ppermute | solution.py:35

commit v3 on v2

--- a/solution.py
+++ b/solution.py
@@ -184,31 +184,23 @@
     )(table, *slices, far_away(key_proj), far_away(value_proj))
 
 
-def choose(own, other, table, after):
-    def kernel(table, first, second, *rest):
-        one, two, sems = rest[-3:]
-        for k, pair in enumerate(((first, second), (second, first))):
+def choose(own, other, table):
+    def kernel(table, first, second, one, two):
+        for k, (a, b) in enumerate(((first, second), (second, first))):
 
             @pl.when(table[at_swapped] == k)
             def _():
-                copies = [
-                    pltpu.make_async_copy(source, target, sems.at[i])
-                    for i, (source, target) in enumerate(zip(pair, (one, two)))
-                ]
-                for copy in copies:
-                    copy.start()
-                for copy in copies:
-                    copy.wait()
-
-    return pl.pallas_call(
-        kernel,
-        in_specs=[in_smem] + [in_vmem] * 2 + [anywhere] * len(after),
-        out_specs=[in_hbm] * 2,
-        out_shape=[pltpu.HBM(own.shape, bf16)] * 2,
-        scratch_shapes=[pltpu.SemaphoreType.DMA((2,))],
+                one[...] = a[...]
+                two[...] = b[...]
+
+    return pl.pallas_call(
+        kernel,
+        in_specs=[in_smem] + [in_vmem] * 2,
+        out_specs=[in_vmem] * 2,
+        out_shape=[jax.ShapeDtypeStruct(own.shape, bf16)] * 2,
         compiler_params=small_params,
         name="choose",
-    )(table, own, other, *after)
+    )(table, own, other)
 
 
 def middle(last_slices, raw, queries, masked, gain, key_proj, value_proj, table):
@@ -221,7 +213,7 @@
     half = vis_rows // 2
     blocks = 16
     lines = depth // blocks
-    unroll = 4
+    unroll = 8
 
     def kernel(
         table, slice_one, slice_two, raw_ref, gain_ref, query_ref, masked_ref, key_ref, value_ref,
@@ -352,15 +344,16 @@
     half = rows // 2
 
     def kernel(table, *refs):
-        for i, out in enumerate(refs[-2:]):
+        for i in range(2):
             lines = pl.ds(pl.multiple_of((table[at_core] + i) % 2 * half, half), half)
-            out[...] = sum(ref[lines, :].astype(f32) for ref in refs[:4]).astype(bf16)
+            total = sum(ref[lines, :].astype(f32) for ref in refs[:4]).astype(bf16)
+            refs[-1][i * half : (i + 1) * half, :] = total
 
     return pl.pallas_call(
         kernel,
         in_specs=[in_smem] + [in_vmem] * 4 + [anywhere] * len(after),
-        out_specs=[in_vmem] * 2,
-        out_shape=[jax.ShapeDtypeStruct((half, tokens), bf16)] * 2,
+        out_specs=in_vmem,
+        out_shape=jax.ShapeDtypeStruct((rows, tokens), bf16),
         compiler_params=small_params,
         name="add_second",
     )(table, own, *arrived, *after)
@@ -411,27 +404,6 @@
         compiler_params=params,
         name="weight_grads",
     )(table, *[v for _, _, v in flat], *grads, after)
-
-
-def join_tokens(mine, partner, table):
-    rows, half = mine.shape
-
-    def kernel(table, one, two, out):
-        for k, pair in enumerate(((one, two), (two, one))):
-
-            @pl.when(table[at_core] == k)
-            def _():
-                for i, ref in enumerate(pair):
-                    out[:, i * half : (i + 1) * half] = ref[...]
-
-    return pl.pallas_call(
-        kernel,
-        in_specs=[in_smem] + [in_vmem] * 2,
-        out_specs=in_vmem,
-        out_shape=jax.ShapeDtypeStruct((rows, 2 * half), bf16),
-        compiler_params=small_params,
-        name="join_tokens",
-    )(table, mine, partner)
 
 
 def turn_features(features, near, near_pair, far, table, after):
@@ -470,25 +442,26 @@
     )(table, far_away(features), near, near_pair, *far, after)
 
 
-def projector_grad(turned, token, tokens_z, table, after):
+def projector_grad(turned, tokens, partners, table, after):
     width, depth = turned.shape
-    columns = token.shape[0]
-    rows = depth // 4
+    rows, half = tokens[0].shape
+    columns = rows // 2
     steps = 3
     block = width // steps
 
     def kernel(table, feature_ref, *refs):
-        out, near = refs[-2:]
-        for k, pair in enumerate(((1, 3), (3, 1))):
+        out, joined = refs[-2:]
+        for k in range(2):
 
             @pl.when(table[at_core] == k)
             def _():
-                for i in range(2):
-                    near[i] = refs[pair[i]][...]
+                for i, image in enumerate((0, 1, 3, 2) if k == 0 else (0, 3, 1, 2)):
+                    joined[i, :, k * half : (k + 1) * half] = refs[image][:columns, :]
+                    joined[i, :, (1 - k) * half : (2 - k) * half] = refs[4 + image][columns:, :]
 
         total = 0.0
-        for i, term in enumerate((refs[0][...], near[0], near[1], refs[2][...])):
-            total += dot(feature_ref[:, i * rows : (i + 1) * rows], term, 1, 1)
+        for i in range(4):
+            total += dot(feature_ref[:, i * 2 * half : (i + 1) * 2 * half], joined[i], 1, 1)
         out[...] = total
 
     return pl.pallas_call(
@@ -497,15 +470,15 @@
             num_scalar_prefetch=1,
             grid=(steps,),
             in_specs=[pl.BlockSpec((block, depth), lambda i, table: (i, 0))]
-            + [pl.BlockSpec(token.shape, lambda i, table: (0, 0))] * 4
+            + [pl.BlockSpec((rows, half), lambda i, table: (0, 0))] * 8
             + [anywhere],
             out_specs=pl.BlockSpec((block, columns), lambda i, table: (i, 0)),
-            scratch_shapes=[pltpu.VMEM((2, *token.shape), bf16)],
+            scratch_shapes=[pltpu.VMEM((4, columns, 2 * half), bf16)],
         ),
         out_shape=jax.ShapeDtypeStruct((width, columns), f32),
         compiler_params=params,
         name="projector_grad",
-    )(table, turned, token, *tokens_z, after)
+    )(table, turned, *tokens, *partners, after)
 
 
 def integers(z, pipe, tensor):
@@ -540,7 +513,7 @@
     raw, done = project([vision, from_core], table, key_proj, value_proj)
     from_x = wait_for(from_x, [done, masked, feature_near, feature_far])
     from_xc = send(from_x, to_core)
-    vision_one, vision_two = choose(vision, from_x, table, [])
+    vision_one, vision_two = choose(vision, from_x, table)
     gathered = [vision, from_core, from_x, from_xc]
     by_z = [send(vision_one, vision_near(1)), send(vision_two, vision_near(3))]
     feature_far = [feature_far, send(feature_far, to_near_y)]
@@ -553,23 +526,22 @@
     feature_far += [send(part, to_core) for part in feature_far]
     terms = add_terms(own_terms, core_terms, feature_far)
     arrived = [send(terms[i], first_stage(i)) for i in (1, 2, 3)]
-    feature_near = wait_for(feature_near, [terms[0]])
+    grads_z = {i: send(grads, along_z(i)) for i in (1, 2, 3)}
+    own, *partial = add_first([terms[0], *arrived], [by_z[2], grads_z[2]])
+    arrived = [send(partial[i - 1], second_stage(i)) for i in (1, 2, 3)]
+    feature_near = wait_for(feature_near, [own])
     feature_pair = send(feature_near, to_core)
-    own, *partial = add_first([terms[0], *arrived], [by_z[2], feature_pair])
-    grads = wait_for(grads, [own])
-    grads_z = {i: send(grads, along_z(i)) for i in (1, 2, 3)}
-    arrived = [send(partial[i - 1], second_stage(i)) for i in (1, 2, 3)]
     turned, done = turn_features(features, feature_near, feature_pair, feature_far, table, own)
-    mine, other = add_second(own, arrived, table, [done, *grads_z.values()])
-    token = join_tokens(mine, send(other, to_core), table)
-    tokens_z = [send(token, along_z(i)) for i in (1, 2, 3)]
-
+    token = add_second(own, arrived, table, [done, grads_z[1], grads_z[3]])
+    tokens = [token, *(send(token, along_z(i)) for i in (1, 2, 3))]
     by_z = [wait_for(array, [token]) for array in by_z]
     pairs = [send(array, to_core) for array in by_z]
     key_total, value_total, done = weight_grads(
         gathered, by_z, pairs, table, [grads, *(grads_z[i] for i in (1, 3, 2))], token
     )
-    projector_total = projector_grad(turned, token, tokens_z, table, done)
+    tokens[1:] = [wait_for(array, [done]) for array in tokens[1:]]
+    partners = [send(array, to_core) for array in tokens]
+    projector_total = projector_grad(turned, tokens, partners, table, done)
     return (key_total[None], value_total[None], projector_total)
 
 

time: 114 us -> 108 us (0.947)
  waiting for transfers between devices: 31.6 us -> 22.9 us
  starting transfers between devices: 38.2 us -> 44.2 us
  Pallas kernels: 38.6 us -> 36.2 us
    ppermute x29 -> x32, waiting for transfers between devices: 31.6 us -> 22.9 us  [send(): return lax.ppermute(array, every_axis, exchange_pairs(moved))]
    ppermute x29 -> x32, starting transfers between devices: 38.2 us -> 44.2 us  [send(): return lax.ppermute(array, every_axis, exchange_pairs(moved))]
    pallas_call x2 -> x1, Pallas kernels: 2.45 us -> 0.69 us  [choose(): pl.pallas_call(kernel, in_specs=[in_smem] + [in_vmem] * 2, out_specs=[in_...]
    unnamed x18 -> x16, local copies, waits for them, and re-layouts: 3.5 us -> 2.97 us
  transfers between devices with their start and end apart: 29 -> 32, of which waited for: 11 -> 11; matrix products, arithmetic and copies ran while one was open for 1% -> 1% of each run, Pallas kernels for 30% -> 29%
where the time goes in v3:
time: 108 us
  starting transfers between devices  44.2 us (41%)
  Pallas kernels  36.2 us (34%)
  waiting for transfers between devices  22.9 us (21%)
  local copies, waits for them, and re-layouts  4 us (4%)
    ppermute x32, starting transfers between devices, send(): return lax.ppermute(array, every_axis, exchange_pairs(moved))  44.2 us
    ppermute x32, waiting for transfers between devices, send(): return lax.ppermute(array, every_axis, exchange_pairs(moved))  22.9 us
    pallas_call x1, Pallas kernels, middle(): pl.pallas_call(kernel, in_specs=[in_smem] + [in_vmem] * 8, out_specs=[in_...  12.3 us
    pallas_call x1, Pallas kernels, weight_grads(): pl.pallas_call(kernel, grid_spec=pltpu.PrefetchScalarGridSpec(num_scalar_...  5.91 us
    pallas_call x1, Pallas kernels, project(): pl.pallas_call(kernel, in_specs=[in_smem] + [in_vmem] * n + [in_hbm] * 2,...  5.33 us
    pallas_call x1, Pallas kernels, projector_grad(): pl.pallas_call(kernel, grid_spec=pltpu.PrefetchScalarGridSpec(num_scalar_...  3.52 us
    pallas_call x1, Pallas kernels, turn_features(): pl.pallas_call(kernel, grid_spec=pltpu.PrefetchScalarGridSpec(num_scalar_...  3.37 us
    unnamed x16, local copies, waits for them, and re-layouts  2.97 us
  transfers between devices with their start and end apart: 32, of which 11 were waited for; matrix products, arithmetic and copies ran while one was open for 1% of the time, Pallas kernels for 29%

profile of v3, /device:TPU:1, one launch (start us, length us, event | category | flops | bytes accessed | tf_op | source)
XLA Modules:
  0.0 108.1 jit_solution(7793200769198853539)
XLA Ops:
  0.6 1.5 %collective-permute-start = (bf16[256,2048]{1,0:T(8,128)(2,1)}, bf16[256,2048]{1,0:T(8,128)(2,1)S(1)}, u32[]{:S(2)}, u32[]{:S(2)}) collective-permute-start(bf16[256,2048]{1,0:T(8,128)(2,1)} %refs_0_.3), channel_id=1, source_target_pairs={{0,1},{1,0},{4,5},{5,4},{2,3},{3,2},{6,7},{7,6},{8,9},{9,8},{12,13... | collective-permute-start | bytes 3145736 | tf_op jit(solution)/shard_map/ppermute | solution.py:35
  2.1 2.6 %collective-permute-start.1 = (bf16[256,2048]{1,0:T(8,128)(2,1)}, bf16[256,2048]{1,0:T(8,128)(2,1)S(1)}, u32[]{:S(2)}, u32[]{:S(2)}) collective-permute-start(bf16[256,2048]{1,0:T(8,128)(2,1)} %refs_0_.3), channel_id=1, source_target_pairs={{0,6},{1,7},{4,2},{5,3},{2,4},{3,5},{6,0},{7,1},{8,14},{9,15},{12,... | collective-permute-start | bytes 3145736 | tf_op jit(solution)/shard_map/ppermute | solution.py:35
  4.9 2.9 %cut_features.1 = (bf16[256,1920]{1,0:T(8,128)(2,1)}, bf16[64,1920]{1,0:T(8,128)(2,1)}) custom-call(s32[45]{0:T(128)S(1)} %stack.183.table, bf16[256,7680]{1,0:T(8,128)(2,1)} %own_ref.1), custom_call_target="tpu_custom_call" | custom-call | tf_op jit(solution)/shard_map/cut_features/pallas_call | solution.py:126
  7.8 3.8 %collective-permute-start.2 = (bf16[256,1920]{1,0:T(8,128)(2,1)}, bf16[256,1920]{1,0:T(8,128)(2,1)S(1)}, u32[]{:S(2)}, u32[]{:S(2)}) collective-permute-start(bf16[256,1920]{1,0:T(8,128)(2,1)} %get-tuple-element.26), channel_id=1, source_target_pairs={{0,32},{1,97},{4,36},{5,101},{2,34},{3,99},{6,38},{7,103},{8,40},{... | collective-permute-start | bytes 2949128 | tf_op jit(solution)/shard_map/ppermute | solution.py:35
  11.7 0.9 copy.20.mask_ref
  12.5 1.6 %copy-done.3 = bf16[512,2048]{1,0:T(8,128)(2,1)S(1)} copy-done((bf16[512,2048]{1,0:T(8,128)(2,1)S(1)}, bf16[512,2048]{1,0:T(8,128)(2,1)}, u32[]{:S(2)}) %copy-start.3) | copy-done | bytes 2097176
  14.1 0.9 copy-done.5
  15.1 0.8 mask_rows.1.refs_2_.masked_ref
  15.9 0.4 copy-done.2
  16.3 5.3 %project.1 = (f32[256,512]{1,0:T(8,128)S(1)}, f32[8,128]{1,0:T(8,128)S(1)}) custom-call(s32[45]{0:T(128)S(1)} %stack.183.table, bf16[256,2048]{1,0:T(8,128)(2,1)S(1)} %copy-done.2, bf16[256,2048]{1,0:T(8,128)(2,1)S(1)} %collective-permute-done.refs_1_, bf16[8192,256]{1,0:T(8,128)(2,1)} %bitcast.50, bf16[8192,256]{1,0:T(8,128)(2,1)} %bitcast.52), custom_call_target="tpu_custom_call" | custom-call | tf_op jit(solution)/shard_map/project/pallas_call | solution.py:176
  21.6 6.6 %collective-permute-done.2.refs_3_.refs_0_ = bf16[256,1920]{1,0:T(8,128)(2,1)S(1)} collective-permute-done((bf16[256,1920]{1,0:T(8,128)(2,1)}, bf16[256,1920]{1,0:T(8,128)(2,1)S(1)}, u32[]{:S(2)}, u32[]{:S(2)}) %collective-permute-start.2) | collective-permute-done | bytes 983072 | tf_op jit(solution)/shard_map/ppermute | solution.py:35
  28.3 3.1 %collective-permute-start.4 = (bf16[256,2048]{1,0:T(8,128)(2,1)S(1)}, bf16[256,2048]{1,0:T(8,128)(2,1)S(1)}, u32[]{:S(2)}, u32[]{:S(2)}) collective-permute-start(bf16[256,2048]{1,0:T(8,128)(2,1)S(1)} %wait_for.9.second.slice_one.refs_2_), channel_id=1, source_target_pairs={{0,1},{1,0},{4,5},{5,4},{2,3},{3,2},{6,7},{7,6},{8,9},{9,8},{12,13... | collective-permute-start | bytes 3145736 | tf_op jit(solution)/shard_map/ppermute | solution.py:35
  31.4 0.7 choose.1
  32.1 1.6 %collective-permute-start.5 = (bf16[256,2048]{1,0:T(8,128)(2,1)S(1)}, bf16[256,2048]{1,0:T(8,128)(2,1)S(1)}, u32[]{:S(2)}, u32[]{:S(2)}) collective-permute-start(bf16[256,2048]{1,0:T(8,128)(2,1)S(1)} %get-tuple-element.28), channel_id=1, source_target_pairs={{1,33},{5,37},{3,35},{7,39},{9,41},{13,45},{11,43},{15,47},{17,49}... | collective-permute-start | bytes 3145736 | tf_op jit(solution)/shard_map/ppermute | solution.py:35
  33.7 3.4 %collective-permute-start.6 = (bf16[256,2048]{1,0:T(8,128)(2,1)S(1)}, bf16[256,2048]{1,0:T(8,128)(2,1)S(1)}, u32[]{:S(2)}, u32[]{:S(2)}) collective-permute-start(bf16[256,2048]{1,0:T(8,128)(2,1)S(1)} %get-tuple-element.32), channel_id=1, source_target_pairs={{1,97},{5,101},{3,99},{7,103},{9,105},{13,109},{11,107},{15,111},{... | collective-permute-start | bytes 3145736 | tf_op jit(solution)/shard_map/ppermute | solution.py:35
  37.2 1.6 %collective-permute-start.7 = (bf16[64,1920]{1,0:T(8,128)(2,1)S(1)}, bf16[64,1920]{1,0:T(8,128)(2,1)S(1)}, u32[]{:S(2)}, u32[]{:S(2)}) collective-permute-start(bf16[64,1920]{1,0:T(8,128)(2,1)S(1)} %collective-permute-done.3.refs_4_.refs_3_.rest_0_), channel_id=1, source_target_pairs={{0,8},{1,9},{4,12},{5,13},{2,10},{3,11},{6,14},{7,15},{8,0},{9,1},... | collective-permute-start | bytes 737288 | tf_op jit(solution)/shard_map/ppermute | solution.py:35
  38.8 12.3 %middle.1 = (bf16[256,512]{1,0:T(8,128)(2,1)S(1)}, bf16[8192,128]{1,0:T(8,128)(2,1)S(1)}, bf16[8192,128]{1,0:T(8,128)(2,1)S(1)}) custom-call(s32[45]{0:T(128)S(1)} %stack.183.table, bf16[256,2048]{1,0:T(8,128)(2,1)S(1)} %wait_for.9.second.slice_one.refs_2_, bf16[256,2048]{1,0:T(8,128)(2,1)S(1)} %collective-permute-done.4.slice_two.refs_3_, ...), custom_call_target="tpu_custom_call" | custom-call | tf_op jit(solution)/shard_map/middle/pallas_call | solution.py:273
  51.1 0.5 collective-permute-start.8
  51.6 1.3 %collective-permute-start.14 = (bf16[256,2048]{1,0:T(8,128)(2,1)S(1)}, bf16[256,2048]{1,0:T(8,128)(2,1)S(1)}, u32[]{:S(2)}, u32[]{:S(2)}) collective-permute-start(bf16[256,2048]{1,0:T(8,128)(2,1)S(1)} %get-tuple-element.28), channel_id=1, source_target_pairs={{0,65},{4,69},{2,67},{6,71},{8,73},{12,77},{10,75},{14,79},{16,81}... | collective-permute-start | bytes 3145736 | tf_op jit(solution)/shard_map/ppermute | solution.py:35
  52.9 2.0 %collective-permute-start.9 = (bf16[64,1920]{1,0:T(8,128)(2,1)S(1)}, bf16[64,1920]{1,0:T(8,128)(2,1)S(1)}, u32[]{:S(2)}, u32[]{:S(2)}) collective-permute-start(bf16[64,1920]{1,0:T(8,128)(2,1)S(1)} %collective-permute-done.3.refs_4_.refs_3_.rest_0_), channel_id=1, source_target_pairs={{0,1},{1,0},{4,5},{5,4},{2,3},{3,2},{6,7},{7,6},{8,9},{9,8},{12,13... | collective-permute-start | bytes 737288 | tf_op jit(solution)/shard_map/ppermute | solution.py:35
  55.0 1.0 collective-permute-done.9.rest_2_
  56.0 0.4 collective-permute-done.10.rest_3_
  56.4 0.5 add_terms.1
  56.9 1.2 %collective-permute-start.11 = (bf16[2048,128]{1,0:T(8,128)(2,1)S(1)}, bf16[2048,128]{1,0:T(8,128)(2,1)S(1)}, u32[]{:S(2)}, u32[]{:S(2)}) collective-permute-start(bf16[2048,128]{1,0:T(8,128)(2,1)S(1)} %get-tuple-element.34), channel_id=1, source_target_pairs={{0,4},{1,9},{4,0},{5,13},{2,6},{3,11},{6,2},{7,15},{8,12},{9,1},{1... | collective-permute-start | bytes 1572872 | tf_op jit(solution)/shard_map/ppermute | solution.py:35
  58.1 2.6 %collective-permute-start.12 = (bf16[2048,128]{1,0:T(8,128)(2,1)S(1)}, bf16[2048,128]{1,0:T(8,128)(2,1)S(1)}, u32[]{:S(2)}, u32[]{:S(2)}) collective-permute-start(bf16[2048,128]{1,0:T(8,128)(2,1)S(1)} %get-tuple-element.35), channel_id=1, source_target_pairs={{0,2},{1,17},{4,6},{5,21},{2,0},{3,19},{6,4},{7,23},{8,10},{9,25},... | collective-permute-start | bytes 1572872 | tf_op jit(solution)/shard_map/ppermute | solution.py:35
  60.8 2.2 %collective-permute-start.15 = (bf16[256,512]{1,0:T(8,128)(2,1)S(1)}, bf16[256,512]{1,0:T(8,128)(2,1)S(1)}, u32[]{:S(2)}, u32[]{:S(2)}) collective-permute-start(bf16[256,512]{1,0:T(8,128)(2,1)S(1)} %get-tuple-element.37.refs_10_), channel_id=1, source_target_pairs={{0,64},{1,65},{4,68},{5,69},{2,66},{3,67},{6,70},{7,71},{8,72},{9,... | collective-permute-start | bytes 786440 | tf_op jit(solution)/shard_map/ppermute | solution.py:35
  63.0 9.3 %collective-permute-done.14.refs_4_.refs_0_ = bf16[256,2048]{1,0:T(8,128)(2,1)S(1)} collective-permute-done((bf16[256,2048]{1,0:T(8,128)(2,1)S(1)}, bf16[256,2048]{1,0:T(8,128)(2,1)S(1)}, u32[]{:S(2)}, u32[]{:S(2)}) %collective-permute-start.14) | collective-permute-done | bytes 1048608 | tf_op jit(solution)/shard_map/ppermute | solution.py:35
  72.3 0.9 collective-permute-done.12.refs_2_
  73.2 2.6 %collective-permute-done.13.refs_3_ = bf16[2048,128]{1,0:T(8,128)(2,1)S(1)} collective-permute-done((bf16[2048,128]{1,0:T(8,128)(2,1)S(1)}, bf16[2048,128]{1,0:T(8,128)(2,1)S(1)}, u32[]{:S(2)}, u32[]{:S(2)}) %collective-permute-start.13) | collective-permute-done | bytes 524320 | tf_op jit(solution)/shard_map/ppermute | solution.py:35
  76.1 1.8 %collective-permute-start.19 = (bf16[256,1920]{1,0:T(8,128)(2,1)S(1)}, bf16[256,1920]{1,0:T(8,128)(2,1)S(1)}, u32[]{:S(2)}, u32[]{:S(2)}) collective-permute-start(bf16[256,1920]{1,0:T(8,128)(2,1)S(1)} %wait_for.11.near_ref), channel_id=1, source_target_pairs={{0,1},{1,0},{4,5},{5,4},{2,3},{3,2},{6,7},{7,6},{8,9},{9,8},{12,13... | collective-permute-start | bytes 2949128 | tf_op jit(solution)/shard_map/ppermute | solution.py:35
  78.1 1.8 %collective-permute-start.21 = (bf16[256,512]{1,0:T(8,128)(2,1)S(1)}, bf16[256,512]{1,0:T(8,128)(2,1)S(1)}, u32[]{:S(2)}, u32[]{:S(2)}) collective-permute-start(bf16[256,512]{1,0:T(8,128)(2,1)S(1)} %get-tuple-element.37.refs_10_), channel_id=1, source_target_pairs={{0,96},{1,97},{4,100},{5,101},{2,98},{3,99},{6,102},{7,103},{8,104... | collective-permute-start | bytes 786440 | tf_op jit(solution)/shard_map/ppermute | solution.py:35
  79.9 1.8 %collective-permute-start.17 = (bf16[512,128]{1,0:T(8,128)(2,1)S(1)}, bf16[512,128]{1,0:T(8,128)(2,1)S(1)}, u32[]{:S(2)}, u32[]{:S(2)}) collective-permute-start(bf16[512,128]{1,0:T(8,128)(2,1)S(1)} %get-tuple-element.40), channel_id=1, source_target_pairs={{0,16},{1,3},{4,20},{5,7},{2,18},{3,1},{6,22},{7,5},{8,24},{9,11},... | collective-permute-start | bytes 393224 | tf_op jit(solution)/shard_map/ppermute | solution.py:35
  81.7 2.1 %collective-permute-start.18 = (bf16[512,128]{1,0:T(8,128)(2,1)S(1)}, bf16[512,128]{1,0:T(8,128)(2,1)S(1)}, u32[]{:S(2)}, u32[]{:S(2)}) collective-permute-start(bf16[512,128]{1,0:T(8,128)(2,1)S(1)} %get-tuple-element.41), channel_id=1, source_target_pairs={{0,24},{1,7},{4,28},{5,3},{2,26},{3,5},{6,30},{7,1},{8,16},{9,15},... | collective-permute-start | bytes 393224 | tf_op jit(solution)/shard_map/ppermute | solution.py:35
  83.8 3.4 %turn_features.1 = (bf16[1920,1024]{1,0:T(8,128)(2,1)S(1)}, f32[8,128]{1,0:T(8,128)S(1)}) custom-call(s32[45]{0:T(128)S(1)} %stack.183.table, bf16[256,7680]{1,0:T(8,128)(2,1)} %own_ref.1, bf16[256,1920]{1,0:T(8,128)(2,1)S(1)} %wait_for.11.near_ref, bf16[256,1920]{1,0:T(8,128)(2,1)S(1)} %collective-permute-done.19.near_pair_ref, ...), custom_call_target="tpu_custom_call" | custom-call | tf_op jit(solution)/shard_map/turn_features/pallas_call | solution.py:424
  87.2 0.6 add_second.1.refs_1_.refs_14_.refs_0_
  87.9 3.6 %collective-permute-start.24 = (bf16[256,2048]{1,0:T(8,128)(2,1)S(1)}, bf16[256,2048]{1,0:T(8,128)(2,1)S(1)}, u32[]{:S(2)}, u32[]{:S(2)}) collective-permute-start(bf16[256,2048]{1,0:T(8,128)(2,1)S(1)} %wait_for.14.refs_8_), channel_id=1, source_target_pairs={{0,1},{1,0},{4,5},{5,4},{2,3},{3,2},{6,7},{7,6},{8,9},{9,8},{12,13... | collective-permute-start | bytes 3145736 | tf_op jit(solution)/shard_map/ppermute | solution.py:35
  91.6 0.4 collective-permute-start.22
  92.0 1.4 %collective-permute-start.27 = (bf16[512,128]{1,0:T(8,128)(2,1)S(1)}, bf16[512,128]{1,0:T(8,128)(2,1)S(1)}, u32[]{:S(2)}, u32[]{:S(2)}) collective-permute-start(bf16[512,128]{1,0:T(8,128)(2,1)S(1)} %add_second.1.refs_1_.refs_14_.refs_0_), channel_id=1, source_target_pairs={{0,96},{1,97},{4,100},{5,101},{2,98},{3,99},{6,102},{7,103},{8,104... | collective-permute-start | bytes 393224 | tf_op jit(solution)/shard_map/ppermute | solution.py:35
  93.4 0.4 collective-permute-done.24.refs_9_
  93.8 1.5 %collective-permute-start.25 = (bf16[512,128]{1,0:T(8,128)(2,1)S(1)}, bf16[512,128]{1,0:T(8,128)(2,1)S(1)}, u32[]{:S(2)}, u32[]{:S(2)}) collective-permute-start(bf16[512,128]{1,0:T(8,128)(2,1)S(1)} %add_second.1.refs_1_.refs_14_.refs_0_), channel_id=1, source_target_pairs={{0,32},{1,33},{4,36},{5,37},{2,34},{3,35},{6,38},{7,39},{8,40},{9,... | collective-permute-start | bytes 393224 | tf_op jit(solution)/shard_map/ppermute | solution.py:35
  95.3 0.9 collective-permute-start.28
  96.2 0.6 collective-permute-done.22.refs_5_
  96.8 5.9 %weight_grads.1 = (f32[2048,256]{1,0:T(8,128)}, f32[2048,256]{1,0:T(8,128)}, f32[8,128]{1,0:T(8,128)S(1)}) custom-call(s32[45]{0:T(128)S(1)} %stack.183.table, bf16[256,2048]{1,0:T(8,128)(2,1)S(1)} %copy-done.2, bf16[256,2048]{1,0:T(8,128)(2,1)S(1)} %collective-permute-done.refs_1_, bf16[256,2048]{1,0:T(8,128)(2,1)S(1)} %wait_for.9.second.slice_one.refs_2_, ...), custom_call_target="tpu_custom_call" | custom-call | tf_op jit(solution)/shard_map/weight_grads/pallas_call | solution.py:391
  102.7 0.4 collective-permute-start.31
  103.2 0.4 collective-permute-start.29
  103.6 0.5 collective-permute-done.31.refs_7_
  104.0 0.4 collective-permute-done.30.refs_6_
  104.6 3.5 %projector_grad.1 = f32[1920,256]{1,0:T(8,128)} custom-call(s32[45]{0:T(128)S(1)} %stack.183.table, bf16[1920,1024]{1,0:T(8,128)(2,1)S(1)} %get-tuple-element.45.feature_ref, bf16[512,128]{1,0:T(8,128)(2,1)S(1)} %add_second.1.refs_1_.refs_14_.refs_0_, bf16[512,128]{1,0:T(8,128)(2,1)S(1)} %wait_for.15.refs_1_, bf16[512,128]{1,0:T(8,128)(2,1)S(1)} %wait_for.16.refs_2_, ...), custom_call_target="tpu_custom_call" | custom-call | tf_op jit(solution)/shard_map/projector_grad/pallas_call | solution.py:467
  (54 shorter events, 1.5 us)
Async XLA Ops:
  0.6 15.2 %collective-permute-start = (bf16[256,2048]{1,0:T(8,128)(2,1)}, bf16[256,2048]{1,0:T(8,128)(2,1)S(1)}, u32[]{:S(2)}, u32[]{:S(2)}) collective-permute-start(bf16[256,2048]{1,0:T(8,128)(2,1)} %refs_0_.3), channel_id=1, source_target_pairs={{0,1},{1,0},{4,5},{5,4},{2,3},{3,2},{6,7},{7,6},{8,9},{9,8},{12,13... | collective-permute-start | bytes 3145736 | tf_op jit(solution)/shard_map/ppermute | solution.py:35
  2.1 26.1 %collective-permute-start.1 = (bf16[256,2048]{1,0:T(8,128)(2,1)}, bf16[256,2048]{1,0:T(8,128)(2,1)S(1)}, u32[]{:S(2)}, u32[]{:S(2)}) collective-permute-start(bf16[256,2048]{1,0:T(8,128)(2,1)} %refs_0_.3), channel_id=1, source_target_pairs={{0,6},{1,7},{4,2},{5,3},{2,4},{3,5},{6,0},{7,1},{8,14},{9,15},{12,... | collective-permute-start | bytes 3145736 | tf_op jit(solution)/shard_map/ppermute | solution.py:35
  4.7 6.9 %copy-start.7 = (s32[512]{0:T(512)S(1)}, s32[512]{0:T(512)}, u32[]{:S(2)}) copy-start(s32[512]{0:T(512)} %param.12) | copy-start | bytes 6148
  7.8 20.5 %collective-permute-start.2 = (bf16[256,1920]{1,0:T(8,128)(2,1)}, bf16[256,1920]{1,0:T(8,128)(2,1)S(1)}, u32[]{:S(2)}, u32[]{:S(2)}) collective-permute-start(bf16[256,1920]{1,0:T(8,128)(2,1)} %get-tuple-element.26), channel_id=1, source_target_pairs={{0,32},{1,97},{4,36},{5,101},{2,34},{3,99},{6,38},{7,103},{8,40},{... | collective-permute-start | bytes 2949128 | tf_op jit(solution)/shard_map/ppermute | solution.py:35
  11.6 10.0 %collective-permute-start.3 = (bf16[64,1920]{1,0:T(8,128)(2,1)}, bf16[64,1920]{1,0:T(8,128)(2,1)S(1)}, u32[]{:S(2)}, u32[]{:S(2)}) collective-permute-start(bf16[64,1920]{1,0:T(8,128)(2,1)} %get-tuple-element.27), channel_id=1, source_target_pairs={{0,64},{1,65},{4,68},{5,69},{2,66},{3,67},{6,70},{7,71},{8,72},{9,... | collective-permute-start | bytes 737288 | tf_op jit(solution)/shard_map/ppermute | solution.py:35
  12.5 1.6 %copy-start.3 = (bf16[512,2048]{1,0:T(8,128)(2,1)S(1)}, bf16[512,2048]{1,0:T(8,128)(2,1)}, u32[]{:S(2)}) copy-start(bf16[512,2048]{1,0:T(8,128)(2,1)} %grad_ref.1) | copy-start | bytes 6291460
  14.1 0.9 copy-start.5
  15.1 1.2 %copy-start.2 = (bf16[256,2048]{1,0:T(8,128)(2,1)S(1)}, bf16[256,2048]{1,0:T(8,128)(2,1)}, u32[]{:S(2)}) copy-start(bf16[256,2048]{1,0:T(8,128)(2,1)} %refs_0_.3) | copy-start | bytes 3145732
  16.3 22.4 %copy-start.1 = (bf16[1,8192,256]{2,1,0:T(8,128)(2,1)S(1)}, bf16[1,8192,256]{2,1,0:T(8,128)(2,1)}, u32[]{:S(2)}) copy-start(bf16[1,8192,256]{2,1,0:T(8,128)(2,1)} %param.14) | copy-start | bytes 12582916
  28.3 10.5 %copy-start = (bf16[1,8192,256]{2,1,0:T(8,128)(2,1)S(1)}, bf16[1,8192,256]{2,1,0:T(8,128)(2,1)}, u32[]{:S(2)}) copy-start(bf16[1,8192,256]{2,1,0:T(8,128)(2,1)} %param.13) | copy-start | bytes 12582916
  28.3 10.5 %copy-start.4 = (bf16[512,2048]{1,0:T(8,128)(2,1)S(1)}, bf16[512,2048]{1,0:T(8,128)(2,1)}, u32[]{:S(2)}) copy-start(bf16[512,2048]{1,0:T(8,128)(2,1)} %query_ref.1) | copy-start | bytes 6291460
  28.3 10.5 %copy-start.6 = (f32[1,128]{1,0:T(1,128)S(1)}, f32[1,128]{1,0:T(1,128)}, u32[]{:S(2)}) copy-start(f32[1,128]{1,0:T(1,128)} %gain_ref.1) | copy-start | bytes 1540
  28.3 10.4 %collective-permute-start.4 = (bf16[256,2048]{1,0:T(8,128)(2,1)S(1)}, bf16[256,2048]{1,0:T(8,128)(2,1)S(1)}, u32[]{:S(2)}, u32[]{:S(2)}) collective-permute-start(bf16[256,2048]{1,0:T(8,128)(2,1)S(1)} %wait_for.9.second.slice_one.refs_2_), channel_id=1, source_target_pairs={{0,1},{1,0},{4,5},{5,4},{2,3},{3,2},{6,7},{7,6},{8,9},{9,8},{12,13... | collective-permute-start | bytes 3145736 | tf_op jit(solution)/shard_map/ppermute | solution.py:35
  32.1 19.0 %collective-permute-start.5 = (bf16[256,2048]{1,0:T(8,128)(2,1)S(1)}, bf16[256,2048]{1,0:T(8,128)(2,1)S(1)}, u32[]{:S(2)}, u32[]{:S(2)}) collective-permute-start(bf16[256,2048]{1,0:T(8,128)(2,1)S(1)} %get-tuple-element.28), channel_id=1, source_target_pairs={{1,33},{5,37},{3,35},{7,39},{9,41},{13,45},{11,43},{15,47},{17,49}... | collective-permute-start | bytes 3145736 | tf_op jit(solution)/shard_map/ppermute | solution.py:35
  33.7 17.3 %collective-permute-start.6 = (bf16[256,2048]{1,0:T(8,128)(2,1)S(1)}, bf16[256,2048]{1,0:T(8,128)(2,1)S(1)}, u32[]{:S(2)}, u32[]{:S(2)}) collective-permute-start(bf16[256,2048]{1,0:T(8,128)(2,1)S(1)} %get-tuple-element.32), channel_id=1, source_target_pairs={{1,97},{5,101},{3,99},{7,103},{9,105},{13,109},{11,107},{15,111},{... | collective-permute-start | bytes 3145736 | tf_op jit(solution)/shard_map/ppermute | solution.py:35
  37.2 13.9 %collective-permute-start.7 = (bf16[64,1920]{1,0:T(8,128)(2,1)S(1)}, bf16[64,1920]{1,0:T(8,128)(2,1)S(1)}, u32[]{:S(2)}, u32[]{:S(2)}) collective-permute-start(bf16[64,1920]{1,0:T(8,128)(2,1)S(1)} %collective-permute-done.3.refs_4_.refs_3_.rest_0_), channel_id=1, source_target_pairs={{0,8},{1,9},{4,12},{5,13},{2,10},{3,11},{6,14},{7,15},{8,0},{9,1},... | collective-permute-start | bytes 737288 | tf_op jit(solution)/shard_map/ppermute | solution.py:35
  51.1 5.3 %collective-permute-start.8 = (bf16[8192,128]{1,0:T(8,128)(2,1)S(1)}, bf16[8192,128]{1,0:T(8,128)(2,1)S(1)}, u32[]{:S(2)}, u32[]{:S(2)}) collective-permute-start(bf16[8192,128]{1,0:T(8,128)(2,1)S(1)} %wait_for.10), channel_id=1, source_target_pairs={{0,1},{1,0},{4,5},{5,4},{2,3},{3,2},{6,7},{7,6},{8,9},{9,8},{12,13... | collective-permute-start | bytes 6291464 | tf_op jit(solution)/shard_map/ppermute | solution.py:35
  51.6 20.7 %collective-permute-start.14 = (bf16[256,2048]{1,0:T(8,128)(2,1)S(1)}, bf16[256,2048]{1,0:T(8,128)(2,1)S(1)}, u32[]{:S(2)}, u32[]{:S(2)}) collective-permute-start(bf16[256,2048]{1,0:T(8,128)(2,1)S(1)} %get-tuple-element.28), channel_id=1, source_target_pairs={{0,65},{4,69},{2,67},{6,71},{8,73},{12,77},{10,75},{14,79},{16,81}... | collective-permute-start | bytes 3145736 | tf_op jit(solution)/shard_map/ppermute | solution.py:35
  52.9 3.1 %collective-permute-start.9 = (bf16[64,1920]{1,0:T(8,128)(2,1)S(1)}, bf16[64,1920]{1,0:T(8,128)(2,1)S(1)}, u32[]{:S(2)}, u32[]{:S(2)}) collective-permute-start(bf16[64,1920]{1,0:T(8,128)(2,1)S(1)} %collective-permute-done.3.refs_4_.refs_3_.rest_0_), channel_id=1, source_target_pairs={{0,1},{1,0},{4,5},{5,4},{2,3},{3,2},{6,7},{7,6},{8,9},{9,8},{12,13... | collective-permute-start | bytes 737288 | tf_op jit(solution)/shard_map/ppermute | solution.py:35
  54.9 1.5 %collective-permute-start.10 = (bf16[64,1920]{1,0:T(8,128)(2,1)S(1)}, bf16[64,1920]{1,0:T(8,128)(2,1)S(1)}, u32[]{:S(2)}, u32[]{:S(2)}) collective-permute-start(bf16[64,1920]{1,0:T(8,128)(2,1)S(1)} %collective-permute-done.7.refs_4_.rest_1_), channel_id=1, source_target_pairs={{0,1},{1,0},{4,5},{5,4},{2,3},{3,2},{6,7},{7,6},{8,9},{9,8},{12,13... | collective-permute-start | bytes 737288 | tf_op jit(solution)/shard_map/ppermute | solution.py:35
  56.9 15.4 %collective-permute-start.11 = (bf16[2048,128]{1,0:T(8,128)(2,1)S(1)}, bf16[2048,128]{1,0:T(8,128)(2,1)S(1)}, u32[]{:S(2)}, u32[]{:S(2)}) collective-permute-start(bf16[2048,128]{1,0:T(8,128)(2,1)S(1)} %get-tuple-element.34), channel_id=1, source_target_pairs={{0,4},{1,9},{4,0},{5,13},{2,6},{3,11},{6,2},{7,15},{8,12},{9,1},{1... | collective-permute-start | bytes 1572872 | tf_op jit(solution)/shard_map/ppermute | solution.py:35
  58.1 15.1 %collective-permute-start.12 = (bf16[2048,128]{1,0:T(8,128)(2,1)S(1)}, bf16[2048,128]{1,0:T(8,128)(2,1)S(1)}, u32[]{:S(2)}, u32[]{:S(2)}) collective-permute-start(bf16[2048,128]{1,0:T(8,128)(2,1)S(1)} %get-tuple-element.35), channel_id=1, source_target_pairs={{0,2},{1,17},{4,6},{5,21},{2,0},{3,19},{6,4},{7,23},{8,10},{9,25},... | collective-permute-start | bytes 1572872 | tf_op jit(solution)/shard_map/ppermute | solution.py:35
  60.7 15.2 %collective-permute-start.13 = (bf16[2048,128]{1,0:T(8,128)(2,1)S(1)}, bf16[2048,128]{1,0:T(8,128)(2,1)S(1)}, u32[]{:S(2)}, u32[]{:S(2)}) collective-permute-start(bf16[2048,128]{1,0:T(8,128)(2,1)S(1)} %get-tuple-element.36), channel_id=1, source_target_pairs={{0,6},{1,25},{4,2},{5,29},{2,4},{3,27},{6,0},{7,31},{8,14},{9,17},... | collective-permute-start | bytes 1572872 | tf_op jit(solution)/shard_map/ppermute | solution.py:35
  60.8 11.5 %collective-permute-start.15 = (bf16[256,512]{1,0:T(8,128)(2,1)S(1)}, bf16[256,512]{1,0:T(8,128)(2,1)S(1)}, u32[]{:S(2)}, u32[]{:S(2)}) collective-permute-start(bf16[256,512]{1,0:T(8,128)(2,1)S(1)} %get-tuple-element.37.refs_10_), channel_id=1, source_target_pairs={{0,64},{1,65},{4,68},{5,69},{2,66},{3,67},{6,70},{7,71},{8,72},{9,... | collective-permute-start | bytes 786440 | tf_op jit(solution)/shard_map/ppermute | solution.py:35
  76.1 5.6 %collective-permute-start.19 = (bf16[256,1920]{1,0:T(8,128)(2,1)S(1)}, bf16[256,1920]{1,0:T(8,128)(2,1)S(1)}, u32[]{:S(2)}, u32[]{:S(2)}) collective-permute-start(bf16[256,1920]{1,0:T(8,128)(2,1)S(1)} %wait_for.11.near_ref), channel_id=1, source_target_pairs={{0,1},{1,0},{4,5},{5,4},{2,3},{3,2},{6,7},{7,6},{8,9},{9,8},{12,13... | collective-permute-start | bytes 2949128 | tf_op jit(solution)/shard_map/ppermute | solution.py:35
  77.9 9.3 %collective-permute-start.20 = (bf16[256,512]{1,0:T(8,128)(2,1)S(1)}, bf16[256,512]{1,0:T(8,128)(2,1)S(1)}, u32[]{:S(2)}, u32[]{:S(2)}) collective-permute-start(bf16[256,512]{1,0:T(8,128)(2,1)S(1)} %get-tuple-element.37.refs_10_), channel_id=1, source_target_pairs={{0,32},{1,33},{4,36},{5,37},{2,34},{3,35},{6,38},{7,39},{8,40},{9,... | collective-permute-start | bytes 786440 | tf_op jit(solution)/shard_map/ppermute | solution.py:35
  78.1 9.0 %collective-permute-start.21 = (bf16[256,512]{1,0:T(8,128)(2,1)S(1)}, bf16[256,512]{1,0:T(8,128)(2,1)S(1)}, u32[]{:S(2)}, u32[]{:S(2)}) collective-permute-start(bf16[256,512]{1,0:T(8,128)(2,1)S(1)} %get-tuple-element.37.refs_10_), channel_id=1, source_target_pairs={{0,96},{1,97},{4,100},{5,101},{2,98},{3,99},{6,102},{7,103},{8,104... | collective-permute-start | bytes 786440 | tf_op jit(solution)/shard_map/ppermute | solution.py:35
  79.9 7.3 %collective-permute-start.16 = (bf16[512,128]{1,0:T(8,128)(2,1)S(1)}, bf16[512,128]{1,0:T(8,128)(2,1)S(1)}, u32[]{:S(2)}, u32[]{:S(2)}) collective-permute-start(bf16[512,128]{1,0:T(8,128)(2,1)S(1)} %get-tuple-element.39), channel_id=1, source_target_pairs={{0,8},{1,5},{4,12},{5,1},{2,10},{3,7},{6,14},{7,3},{8,0},{9,13},{1... | collective-permute-start | bytes 393224 | tf_op jit(solution)/shard_map/ppermute | solution.py:35
  79.9 7.3 %collective-permute-start.17 = (bf16[512,128]{1,0:T(8,128)(2,1)S(1)}, bf16[512,128]{1,0:T(8,128)(2,1)S(1)}, u32[]{:S(2)}, u32[]{:S(2)}) collective-permute-start(bf16[512,128]{1,0:T(8,128)(2,1)S(1)} %get-tuple-element.40), channel_id=1, source_target_pairs={{0,16},{1,3},{4,20},{5,7},{2,18},{3,1},{6,22},{7,5},{8,24},{9,11},... | collective-permute-start | bytes 393224 | tf_op jit(solution)/shard_map/ppermute | solution.py:35
  81.7 5.5 %collective-permute-start.18 = (bf16[512,128]{1,0:T(8,128)(2,1)S(1)}, bf16[512,128]{1,0:T(8,128)(2,1)S(1)}, u32[]{:S(2)}, u32[]{:S(2)}) collective-permute-start(bf16[512,128]{1,0:T(8,128)(2,1)S(1)} %get-tuple-element.41), channel_id=1, source_target_pairs={{0,24},{1,7},{4,28},{5,3},{2,26},{3,5},{6,30},{7,1},{8,16},{9,15},... | collective-permute-start | bytes 393224 | tf_op jit(solution)/shard_map/ppermute | solution.py:35
  87.9 5.9 %collective-permute-start.24 = (bf16[256,2048]{1,0:T(8,128)(2,1)S(1)}, bf16[256,2048]{1,0:T(8,128)(2,1)S(1)}, u32[]{:S(2)}, u32[]{:S(2)}) collective-permute-start(bf16[256,2048]{1,0:T(8,128)(2,1)S(1)} %wait_for.14.refs_8_), channel_id=1, source_target_pairs={{0,1},{1,0},{4,5},{5,4},{2,3},{3,2},{6,7},{7,6},{8,9},{9,8},{12,13... | collective-permute-start | bytes 3145736 | tf_op jit(solution)/shard_map/ppermute | solution.py:35
  91.5 3.8 %collective-permute-start.23 = (bf16[256,2048]{1,0:T(8,128)(2,1)S(1)}, bf16[256,2048]{1,0:T(8,128)(2,1)S(1)}, u32[]{:S(2)}, u32[]{:S(2)}) collective-permute-start(bf16[256,2048]{1,0:T(8,128)(2,1)S(1)} %wait_for.13.refs_6_), channel_id=1, source_target_pairs={{0,1},{1,0},{4,5},{5,4},{2,3},{3,2},{6,7},{7,6},{8,9},{9,8},{12,13... | collective-permute-start | bytes 3145736 | tf_op jit(solution)/shard_map/ppermute | solution.py:35
  91.6 5.2 %collective-permute-start.22 = (bf16[256,2048]{1,0:T(8,128)(2,1)S(1)}, bf16[256,2048]{1,0:T(8,128)(2,1)S(1)}, u32[]{:S(2)}, u32[]{:S(2)}) collective-permute-start(bf16[256,2048]{1,0:T(8,128)(2,1)S(1)} %wait_for.12.refs_4_), channel_id=1, source_target_pairs={{0,1},{1,0},{4,5},{5,4},{2,3},{3,2},{6,7},{7,6},{8,9},{9,8},{12,13... | collective-permute-start | bytes 3145736 | tf_op jit(solution)/shard_map/ppermute | solution.py:35
  92.0 10.7 %collective-permute-start.27 = (bf16[512,128]{1,0:T(8,128)(2,1)S(1)}, bf16[512,128]{1,0:T(8,128)(2,1)S(1)}, u32[]{:S(2)}, u32[]{:S(2)}) collective-permute-start(bf16[512,128]{1,0:T(8,128)(2,1)S(1)} %add_second.1.refs_1_.refs_14_.refs_0_), channel_id=1, source_target_pairs={{0,96},{1,97},{4,100},{5,101},{2,98},{3,99},{6,102},{7,103},{8,104... | collective-permute-start | bytes 393224 | tf_op jit(solution)/shard_map/ppermute | solution.py:35
  93.4 9.7 %collective-permute-start.26 = (bf16[512,128]{1,0:T(8,128)(2,1)S(1)}, bf16[512,128]{1,0:T(8,128)(2,1)S(1)}, u32[]{:S(2)}, u32[]{:S(2)}) collective-permute-start(bf16[512,128]{1,0:T(8,128)(2,1)S(1)} %add_second.1.refs_1_.refs_14_.refs_0_), channel_id=1, source_target_pairs={{0,64},{1,65},{4,68},{5,69},{2,66},{3,67},{6,70},{7,71},{8,72},{9,... | collective-permute-start | bytes 393224 | tf_op jit(solution)/shard_map/ppermute | solution.py:35
  93.8 9.4 %collective-permute-start.25 = (bf16[512,128]{1,0:T(8,128)(2,1)S(1)}, bf16[512,128]{1,0:T(8,128)(2,1)S(1)}, u32[]{:S(2)}, u32[]{:S(2)}) collective-permute-start(bf16[512,128]{1,0:T(8,128)(2,1)S(1)} %add_second.1.refs_1_.refs_14_.refs_0_), channel_id=1, source_target_pairs={{0,32},{1,33},{4,36},{5,37},{2,34},{3,35},{6,38},{7,39},{8,40},{9,... | collective-permute-start | bytes 393224 | tf_op jit(solution)/shard_map/ppermute | solution.py:35
  95.3 8.3 %collective-permute-start.28 = (bf16[512,128]{1,0:T(8,128)(2,1)S(1)}, bf16[512,128]{1,0:T(8,128)(2,1)S(1)}, u32[]{:S(2)}, u32[]{:S(2)}) collective-permute-start(bf16[512,128]{1,0:T(8,128)(2,1)S(1)} %add_second.1.refs_1_.refs_14_.refs_0_), channel_id=1, source_target_pairs={{0,1},{1,0},{4,5},{5,4},{2,3},{3,2},{6,7},{7,6},{8,9},{9,8},{12,13... | collective-permute-start | bytes 393224 | tf_op jit(solution)/shard_map/ppermute | solution.py:35
  102.7 1.4 %collective-permute-start.31 = (bf16[512,128]{1,0:T(8,128)(2,1)S(1)}, bf16[512,128]{1,0:T(8,128)(2,1)S(1)}, u32[]{:S(2)}, u32[]{:S(2)}) collective-permute-start(bf16[512,128]{1,0:T(8,128)(2,1)S(1)} %wait_for.17.refs_3_), channel_id=1, source_target_pairs={{0,1},{1,0},{4,5},{5,4},{2,3},{3,2},{6,7},{7,6},{8,9},{9,8},{12,13... | collective-permute-start | bytes 393224 | tf_op jit(solution)/shard_map/ppermute | solution.py:35
  103.1 1.3 %collective-permute-start.30 = (bf16[512,128]{1,0:T(8,128)(2,1)S(1)}, bf16[512,128]{1,0:T(8,128)(2,1)S(1)}, u32[]{:S(2)}, u32[]{:S(2)}) collective-permute-start(bf16[512,128]{1,0:T(8,128)(2,1)S(1)} %wait_for.16.refs_2_), channel_id=1, source_target_pairs={{0,1},{1,0},{4,5},{5,4},{2,3},{3,2},{6,7},{7,6},{8,9},{9,8},{12,13... | collective-permute-start | bytes 393224 | tf_op jit(solution)/shard_map/ppermute | solution.py:35
  103.2 1.4 %collective-permute-start.29 = (bf16[512,128]{1,0:T(8,128)(2,1)S(1)}, bf16[512,128]{1,0:T(8,128)(2,1)S(1)}, u32[]{:S(2)}, u32[]{:S(2)}) collective-permute-start(bf16[512,128]{1,0:T(8,128)(2,1)S(1)} %wait_for.15.refs_1_), channel_id=1, source_target_pairs={{0,1},{1,0},{4,5},{5,4},{2,3},{3,2},{6,7},{7,6},{8,9},{9,8},{12,13... | collective-permute-start | bytes 393224 | tf_op jit(solution)/shard_map/ppermute | solution.py:35

commit v4 on v3

--- a/solution.py
+++ b/solution.py
@@ -362,7 +362,7 @@
 def weight_grads(gathered, by_z, pairs, table, grads, after):
     rows, width = gathered[0].shape
     columns = grads[0].shape[1] // 2
-    steps = 4
+    steps = 2
     block = width // steps
     choices = [[(at_own, k, v) for k, v in enumerate(gathered)]]
     choices += [
@@ -401,7 +401,7 @@
             scratch_shapes=[pltpu.VMEM((4, rows, block), bf16)],
         ),
         out_shape=[jax.ShapeDtypeStruct((width, columns), f32)] * 2 + [token_shape],
-        compiler_params=params,
+        compiler_params=large_params,
         name="weight_grads",
     )(table, *[v for _, _, v in flat], *grads, after)
 
@@ -409,7 +409,7 @@
 def turn_features(features, near, near_pair, far, table, after):
     rows, width = near.shape
     quarter = rows // 4
-    steps = 3
+    steps = 1
     block = width // steps
 
     def kernel(table, own_ref, near_ref, near_pair_ref, *rest):
@@ -437,7 +437,7 @@
             scratch_shapes=[pltpu.VMEM((rows, block), bf16)],
         ),
         out_shape=[jax.ShapeDtypeStruct((width, 4 * rows), bf16), token_shape],
-        compiler_params=params,
+        compiler_params=large_params,
         name="turn_features",
     )(table, far_away(features), near, near_pair, *far, after)
 
@@ -446,36 +446,40 @@
     width, depth = turned.shape
     rows, half = tokens[0].shape
     columns = rows // 2
-    steps = 3
+    steps = 5
     block = width // steps
 
     def kernel(table, feature_ref, *refs):
-        out, joined = refs[-2:]
+        out, joined, total, sems = refs[-4:]
         for k in range(2):
 
             @pl.when(table[at_core] == k)
             def _():
                 for i, image in enumerate((0, 1, 3, 2) if k == 0 else (0, 3, 1, 2)):
-                    joined[i, :, k * half : (k + 1) * half] = refs[image][:columns, :]
-                    joined[i, :, (1 - k) * half : (2 - k) * half] = refs[4 + image][columns:, :]
-
-        total = 0.0
-        for i in range(4):
-            total += dot(feature_ref[:, i * 2 * half : (i + 1) * 2 * half], joined[i], 1, 1)
-        out[...] = total
-
-    return pl.pallas_call(
-        kernel,
-        grid_spec=pltpu.PrefetchScalarGridSpec(
-            num_scalar_prefetch=1,
-            grid=(steps,),
-            in_specs=[pl.BlockSpec((block, depth), lambda i, table: (i, 0))]
-            + [pl.BlockSpec((rows, half), lambda i, table: (0, 0))] * 8
-            + [anywhere],
-            out_specs=pl.BlockSpec((block, columns), lambda i, table: (i, 0)),
-            scratch_shapes=[pltpu.VMEM((4, columns, 2 * half), bf16)],
-        ),
-        out_shape=jax.ShapeDtypeStruct((width, columns), f32),
+                    joined[:, (2 * i + k) * half : (2 * i + k + 1) * half] = refs[image][:columns, :]
+                    joined[:, (2 * i + 1 - k) * half : (2 * i + 2 - k) * half] = refs[4 + image][
+                        columns:, :
+                    ]
+
+        copies = []
+        for step in range(steps):
+            lines = pl.ds(step * block, block)
+            total[lines, :] = dot(feature_ref[lines, :], joined[...], 1, 1)
+            copies.append(pltpu.make_async_copy(total.at[lines, :], out.at[lines, :], sems.at[step]))
+            copies[-1].start()
+        for copy in copies:
+            copy.wait()
+
+    return pl.pallas_call(
+        kernel,
+        in_specs=[in_smem] + [in_vmem] * 9 + [anywhere],
+        out_specs=in_hbm,
+        out_shape=pltpu.HBM((width, columns), f32),
+        scratch_shapes=[
+            pltpu.VMEM((columns, depth), bf16),
+            pltpu.VMEM((width, columns), f32),
+            pltpu.SemaphoreType.DMA((steps,)),
+        ],
         compiler_params=params,
         name="projector_grad",
     )(table, turned, *tokens, *partners, after)
@@ -525,10 +529,10 @@
     by_z.append(send(vision_one, vision_far))
     feature_far += [send(part, to_core) for part in feature_far]
     terms = add_terms(own_terms, core_terms, feature_far)
-    arrived = [send(terms[i], first_stage(i)) for i in (1, 2, 3)]
+    arrived = [send(terms[i], first_stage(i)) for i in (2, 1, 3)]
     grads_z = {i: send(grads, along_z(i)) for i in (1, 2, 3)}
     own, *partial = add_first([terms[0], *arrived], [by_z[2], grads_z[2]])
-    arrived = [send(partial[i - 1], second_stage(i)) for i in (1, 2, 3)]
+    arrived = [send(partial[i - 1], second_stage(i)) for i in (2, 1, 3)]
     feature_near = wait_for(feature_near, [own])
     feature_pair = send(feature_near, to_core)
     turned, done = turn_features(features, feature_near, feature_pair, feature_far, table, own)

time: 108 us -> 104 us (0.963)
  starting transfers between devices: 44.2 us -> 42.6 us
  Pallas kernels: 36.2 us -> 34.8 us
  waiting for transfers between devices: 22.9 us -> 21.7 us
    ppermute x32, starting transfers between devices: 44.2 us -> 42.6 us  [send(): return lax.ppermute(array, every_axis, exchange_pairs(moved))]
    ppermute x32, waiting for transfers between devices: 22.9 us -> 21.7 us  [send(): return lax.ppermute(array, every_axis, exchange_pairs(moved))]
  transfers between devices with their start and end apart: 32 -> 32, of which waited for: 11 -> 12; matrix products, arithmetic and copies ran while one was open for 1% -> 1% of each run, Pallas kernels for 29% -> 30%
where the time goes in v4:
time: 104 us
  starting transfers between devices  42.6 us (41%)
  Pallas kernels  34.8 us (33%)
  waiting for transfers between devices  21.7 us (21%)
  local copies, waits for them, and re-layouts  4 us (4%)
    ppermute x32, starting transfers between devices, send(): return lax.ppermute(array, every_axis, exchange_pairs(moved))  42.6 us
    ppermute x32, waiting for transfers between devices, send(): return lax.ppermute(array, every_axis, exchange_pairs(moved))  21.7 us
    pallas_call x1, Pallas kernels, middle(): pl.pallas_call(kernel, in_specs=[in_smem] + [in_vmem] * 8, out_specs=[in_...  12.3 us
    pallas_call x1, Pallas kernels, weight_grads(): pl.pallas_call(kernel, grid_spec=pltpu.PrefetchScalarGridSpec(num_scalar_...  5.64 us
    pallas_call x1, Pallas kernels, project(): pl.pallas_call(kernel, in_specs=[in_smem] + [in_vmem] * n + [in_hbm] * 2,...  5.33 us
    unnamed x16, local copies, waits for them, and re-layouts  2.97 us
    pallas_call x1, Pallas kernels, turn_features(): pl.pallas_call(kernel, grid_spec=pltpu.PrefetchScalarGridSpec(num_scalar_...  2.94 us
    pallas_call x1, Pallas kernels, cut_features(): pl.pallas_call(kernel, in_specs=[in_smem, in_hbm], out_specs=[in_vmem] *...  2.92 us
  transfers between devices with their start and end apart: 32, of which 12 were waited for; matrix products, arithmetic and copies ran while one was open for 1% of the time, Pallas kernels for 30%

profile of v4, /device:TPU:1, one launch (start us, length us, event | category | flops | bytes accessed | tf_op | source)
XLA Modules:
  0.0 104.1 jit_solution(3935503240679061904)
XLA Ops:
  0.6 1.5 %collective-permute-start = (bf16[256,2048]{1,0:T(8,128)(2,1)}, bf16[256,2048]{1,0:T(8,128)(2,1)S(1)}, u32[]{:S(2)}, u32[]{:S(2)}) collective-permute-start(bf16[256,2048]{1,0:T(8,128)(2,1)} %refs_0_.3), channel_id=1, source_target_pairs={{0,1},{1,0},{4,5},{5,4},{2,3},{3,2},{6,7},{7,6},{8,9},{9,8},{12,13... | collective-permute-start | bytes 3145736 | tf_op jit(solution)/shard_map/ppermute | solution.py:35
  2.1 2.6 %collective-permute-start.1 = (bf16[256,2048]{1,0:T(8,128)(2,1)}, bf16[256,2048]{1,0:T(8,128)(2,1)S(1)}, u32[]{:S(2)}, u32[]{:S(2)}) collective-permute-start(bf16[256,2048]{1,0:T(8,128)(2,1)} %refs_0_.3), channel_id=1, source_target_pairs={{0,6},{1,7},{4,2},{5,3},{2,4},{3,5},{6,0},{7,1},{8,14},{9,15},{12,... | collective-permute-start | bytes 3145736 | tf_op jit(solution)/shard_map/ppermute | solution.py:35
  4.9 2.9 %cut_features.1 = (bf16[256,1920]{1,0:T(8,128)(2,1)}, bf16[64,1920]{1,0:T(8,128)(2,1)}) custom-call(s32[45]{0:T(128)S(1)} %stack.183.table, bf16[256,7680]{1,0:T(8,128)(2,1)} %own_ref.1), custom_call_target="tpu_custom_call" | custom-call | tf_op jit(solution)/shard_map/cut_features/pallas_call | solution.py:126
  7.8 3.8 %collective-permute-start.2 = (bf16[256,1920]{1,0:T(8,128)(2,1)}, bf16[256,1920]{1,0:T(8,128)(2,1)S(1)}, u32[]{:S(2)}, u32[]{:S(2)}) collective-permute-start(bf16[256,1920]{1,0:T(8,128)(2,1)} %get-tuple-element.26), channel_id=1, source_target_pairs={{0,32},{1,97},{4,36},{5,101},{2,34},{3,99},{6,38},{7,103},{8,40},{... | collective-permute-start | bytes 2949128 | tf_op jit(solution)/shard_map/ppermute | solution.py:35
  11.7 0.9 copy.20.mask_ref
  12.5 1.6 %copy-done.3 = bf16[512,2048]{1,0:T(8,128)(2,1)S(1)} copy-done((bf16[512,2048]{1,0:T(8,128)(2,1)S(1)}, bf16[512,2048]{1,0:T(8,128)(2,1)}, u32[]{:S(2)}) %copy-start.3) | copy-done | bytes 2097176
  14.1 0.9 copy-done.5
  15.1 0.8 mask_rows.1.refs_2_.masked_ref
  15.9 0.4 copy-done.2
  16.3 5.3 %project.1 = (f32[256,512]{1,0:T(8,128)S(1)}, f32[8,128]{1,0:T(8,128)S(1)}) custom-call(s32[45]{0:T(128)S(1)} %stack.183.table, bf16[256,2048]{1,0:T(8,128)(2,1)S(1)} %copy-done.2, bf16[256,2048]{1,0:T(8,128)(2,1)S(1)} %collective-permute-done.refs_1_, bf16[8192,256]{1,0:T(8,128)(2,1)} %bitcast.50, bf16[8192,256]{1,0:T(8,128)(2,1)} %bitcast.52), custom_call_target="tpu_custom_call" | custom-call | tf_op jit(solution)/shard_map/project/pallas_call | solution.py:176
  21.6 6.6 %collective-permute-done.2.refs_3_.refs_0_ = bf16[256,1920]{1,0:T(8,128)(2,1)S(1)} collective-permute-done((bf16[256,1920]{1,0:T(8,128)(2,1)}, bf16[256,1920]{1,0:T(8,128)(2,1)S(1)}, u32[]{:S(2)}, u32[]{:S(2)}) %collective-permute-start.2) | collective-permute-done | bytes 983072 | tf_op jit(solution)/shard_map/ppermute | solution.py:35
  28.3 3.1 %collective-permute-start.4 = (bf16[256,2048]{1,0:T(8,128)(2,1)S(1)}, bf16[256,2048]{1,0:T(8,128)(2,1)S(1)}, u32[]{:S(2)}, u32[]{:S(2)}) collective-permute-start(bf16[256,2048]{1,0:T(8,128)(2,1)S(1)} %wait_for.9.second.slice_one.refs_2_), channel_id=1, source_target_pairs={{0,1},{1,0},{4,5},{5,4},{2,3},{3,2},{6,7},{7,6},{8,9},{9,8},{12,13... | collective-permute-start | bytes 3145736 | tf_op jit(solution)/shard_map/ppermute | solution.py:35
  31.4 0.7 choose.1
  32.1 1.6 %collective-permute-start.5 = (bf16[256,2048]{1,0:T(8,128)(2,1)S(1)}, bf16[256,2048]{1,0:T(8,128)(2,1)S(1)}, u32[]{:S(2)}, u32[]{:S(2)}) collective-permute-start(bf16[256,2048]{1,0:T(8,128)(2,1)S(1)} %get-tuple-element.28), channel_id=1, source_target_pairs={{1,33},{5,37},{3,35},{7,39},{9,41},{13,45},{11,43},{15,47},{17,49}... | collective-permute-start | bytes 3145736 | tf_op jit(solution)/shard_map/ppermute | solution.py:35
  33.7 3.4 %collective-permute-start.6 = (bf16[256,2048]{1,0:T(8,128)(2,1)S(1)}, bf16[256,2048]{1,0:T(8,128)(2,1)S(1)}, u32[]{:S(2)}, u32[]{:S(2)}) collective-permute-start(bf16[256,2048]{1,0:T(8,128)(2,1)S(1)} %get-tuple-element.32), channel_id=1, source_target_pairs={{1,97},{5,101},{3,99},{7,103},{9,105},{13,109},{11,107},{15,111},{... | collective-permute-start | bytes 3145736 | tf_op jit(solution)/shard_map/ppermute | solution.py:35
  37.2 1.6 %collective-permute-start.7 = (bf16[64,1920]{1,0:T(8,128)(2,1)S(1)}, bf16[64,1920]{1,0:T(8,128)(2,1)S(1)}, u32[]{:S(2)}, u32[]{:S(2)}) collective-permute-start(bf16[64,1920]{1,0:T(8,128)(2,1)S(1)} %collective-permute-done.3.refs_4_.refs_3_.rest_0_), channel_id=1, source_target_pairs={{0,8},{1,9},{4,12},{5,13},{2,10},{3,11},{6,14},{7,15},{8,0},{9,1},... | collective-permute-start | bytes 737288 | tf_op jit(solution)/shard_map/ppermute | solution.py:35
  38.8 12.3 %middle.1 = (bf16[256,512]{1,0:T(8,128)(2,1)S(1)}, bf16[8192,128]{1,0:T(8,128)(2,1)S(1)}, bf16[8192,128]{1,0:T(8,128)(2,1)S(1)}) custom-call(s32[45]{0:T(128)S(1)} %stack.183.table, bf16[256,2048]{1,0:T(8,128)(2,1)S(1)} %wait_for.9.second.slice_one.refs_2_, bf16[256,2048]{1,0:T(8,128)(2,1)S(1)} %collective-permute-done.4.slice_two.refs_3_, ...), custom_call_target="tpu_custom_call" | custom-call | tf_op jit(solution)/shard_map/middle/pallas_call | solution.py:273
  51.1 0.5 collective-permute-start.8
  51.6 1.3 %collective-permute-start.14 = (bf16[256,2048]{1,0:T(8,128)(2,1)S(1)}, bf16[256,2048]{1,0:T(8,128)(2,1)S(1)}, u32[]{:S(2)}, u32[]{:S(2)}) collective-permute-start(bf16[256,2048]{1,0:T(8,128)(2,1)S(1)} %get-tuple-element.28), channel_id=1, source_target_pairs={{0,65},{4,69},{2,67},{6,71},{8,73},{12,77},{10,75},{14,79},{16,81}... | collective-permute-start | bytes 3145736 | tf_op jit(solution)/shard_map/ppermute | solution.py:35
  52.9 2.0 %collective-permute-start.9 = (bf16[64,1920]{1,0:T(8,128)(2,1)S(1)}, bf16[64,1920]{1,0:T(8,128)(2,1)S(1)}, u32[]{:S(2)}, u32[]{:S(2)}) collective-permute-start(bf16[64,1920]{1,0:T(8,128)(2,1)S(1)} %collective-permute-done.3.refs_4_.refs_3_.rest_0_), channel_id=1, source_target_pairs={{0,1},{1,0},{4,5},{5,4},{2,3},{3,2},{6,7},{7,6},{8,9},{9,8},{12,13... | collective-permute-start | bytes 737288 | tf_op jit(solution)/shard_map/ppermute | solution.py:35
  55.0 1.0 %collective-permute-done.9.rest_2_ = bf16[64,1920]{1,0:T(8,128)(2,1)S(1)} collective-permute-done((bf16[64,1920]{1,0:T(8,128)(2,1)S(1)}, bf16[64,1920]{1,0:T(8,128)(2,1)S(1)}, u32[]{:S(2)}, u32[]{:S(2)}) %collective-permute-start.9) | collective-permute-done | bytes 245792 | tf_op jit(solution)/shard_map/ppermute | solution.py:35
  56.4 0.5 add_terms.1
  56.9 2.8 %collective-permute-start.11 = (bf16[2048,128]{1,0:T(8,128)(2,1)S(1)}, bf16[2048,128]{1,0:T(8,128)(2,1)S(1)}, u32[]{:S(2)}, u32[]{:S(2)}) collective-permute-start(bf16[2048,128]{1,0:T(8,128)(2,1)S(1)} %get-tuple-element.34), channel_id=1, source_target_pairs={{0,2},{1,17},{4,6},{5,21},{2,0},{3,19},{6,4},{7,23},{8,10},{9,25},... | collective-permute-start | bytes 1572872 | tf_op jit(solution)/shard_map/ppermute | solution.py:35
  59.7 0.4 collective-permute-start.12
  60.1 0.4 collective-permute-start.13
  60.5 2.3 %collective-permute-start.15 = (bf16[256,512]{1,0:T(8,128)(2,1)S(1)}, bf16[256,512]{1,0:T(8,128)(2,1)S(1)}, u32[]{:S(2)}, u32[]{:S(2)}) collective-permute-start(bf16[256,512]{1,0:T(8,128)(2,1)S(1)} %get-tuple-element.37.refs_10_), channel_id=1, source_target_pairs={{0,64},{1,65},{4,68},{5,69},{2,66},{3,67},{6,70},{7,71},{8,72},{9,... | collective-permute-start | bytes 786440 | tf_op jit(solution)/shard_map/ppermute | solution.py:35
  62.8 9.2 %collective-permute-done.14.refs_4_.refs_0_ = bf16[256,2048]{1,0:T(8,128)(2,1)S(1)} collective-permute-done((bf16[256,2048]{1,0:T(8,128)(2,1)S(1)}, bf16[256,2048]{1,0:T(8,128)(2,1)S(1)}, u32[]{:S(2)}, u32[]{:S(2)}) %collective-permute-start.14) | collective-permute-done | bytes 1048608 | tf_op jit(solution)/shard_map/ppermute | solution.py:35
  72.0 0.6 collective-permute-done.12.refs_2_
  72.9 3.0 %collective-permute-start.19 = (bf16[256,1920]{1,0:T(8,128)(2,1)S(1)}, bf16[256,1920]{1,0:T(8,128)(2,1)S(1)}, u32[]{:S(2)}, u32[]{:S(2)}) collective-permute-start(bf16[256,1920]{1,0:T(8,128)(2,1)S(1)} %wait_for.11.near_ref), channel_id=1, source_target_pairs={{0,1},{1,0},{4,5},{5,4},{2,3},{3,2},{6,7},{7,6},{8,9},{9,8},{12,13... | collective-permute-start | bytes 2949128 | tf_op jit(solution)/shard_map/ppermute | solution.py:35
  75.9 1.2 %collective-permute-start.21 = (bf16[256,512]{1,0:T(8,128)(2,1)S(1)}, bf16[256,512]{1,0:T(8,128)(2,1)S(1)}, u32[]{:S(2)}, u32[]{:S(2)}) collective-permute-start(bf16[256,512]{1,0:T(8,128)(2,1)S(1)} %get-tuple-element.37.refs_10_), channel_id=1, source_target_pairs={{0,96},{1,97},{4,100},{5,101},{2,98},{3,99},{6,102},{7,103},{8,104... | collective-permute-start | bytes 786440 | tf_op jit(solution)/shard_map/ppermute | solution.py:35
  77.0 1.5 %collective-permute-start.16 = (bf16[512,128]{1,0:T(8,128)(2,1)S(1)}, bf16[512,128]{1,0:T(8,128)(2,1)S(1)}, u32[]{:S(2)}, u32[]{:S(2)}) collective-permute-start(bf16[512,128]{1,0:T(8,128)(2,1)S(1)} %get-tuple-element.39), channel_id=1, source_target_pairs={{0,16},{1,3},{4,20},{5,7},{2,18},{3,1},{6,22},{7,5},{8,24},{9,11},... | collective-permute-start | bytes 393224 | tf_op jit(solution)/shard_map/ppermute | solution.py:35
  78.6 1.5 %collective-permute-start.17 = (bf16[512,128]{1,0:T(8,128)(2,1)S(1)}, bf16[512,128]{1,0:T(8,128)(2,1)S(1)}, u32[]{:S(2)}, u32[]{:S(2)}) collective-permute-start(bf16[512,128]{1,0:T(8,128)(2,1)S(1)} %get-tuple-element.40), channel_id=1, source_target_pairs={{0,8},{1,5},{4,12},{5,1},{2,10},{3,7},{6,14},{7,3},{8,0},{9,13},{1... | collective-permute-start | bytes 393224 | tf_op jit(solution)/shard_map/ppermute | solution.py:35
  80.3 2.9 %turn_features.1 = (bf16[1920,1024]{1,0:T(8,128)(2,1)S(1)}, f32[8,128]{1,0:T(8,128)S(1)}) custom-call(s32[45]{0:T(128)S(1)} %stack.183.table, bf16[256,7680]{1,0:T(8,128)(2,1)} %own_ref.1, bf16[256,1920]{1,0:T(8,128)(2,1)S(1)} %wait_for.11.near_ref, bf16[256,1920]{1,0:T(8,128)(2,1)S(1)} %collective-permute-done.19.near_pair_ref, ...), custom_call_target="tpu_custom_call" | custom-call | tf_op jit(solution)/shard_map/turn_features/pallas_call | solution.py:424
  83.2 0.5 collective-permute-done.20.refs_5_.refs_11_
  83.8 1.1 %collective-permute-done.21.refs_6_.refs_12_ = bf16[256,512]{1,0:T(8,128)(2,1)S(1)} collective-permute-done((bf16[256,512]{1,0:T(8,128)(2,1)S(1)}, bf16[256,512]{1,0:T(8,128)(2,1)S(1)}, u32[]{:S(2)}, u32[]{:S(2)}) %collective-permute-start.21) | collective-permute-done | bytes 262176 | tf_op jit(solution)/shard_map/ppermute | solution.py:35
  84.8 0.6 collective-permute-done.18.refs_3_
  85.4 0.6 add_second.1.refs_1_.refs_14_.refs_0_
  86.1 2.2 %collective-permute-start.24 = (bf16[256,2048]{1,0:T(8,128)(2,1)S(1)}, bf16[256,2048]{1,0:T(8,128)(2,1)S(1)}, u32[]{:S(2)}, u32[]{:S(2)}) collective-permute-start(bf16[256,2048]{1,0:T(8,128)(2,1)S(1)} %wait_for.14.refs_8_), channel_id=1, source_target_pairs={{0,1},{1,0},{4,5},{5,4},{2,3},{3,2},{6,7},{7,6},{8,9},{9,8},{12,13... | collective-permute-start | bytes 3145736 | tf_op jit(solution)/shard_map/ppermute | solution.py:35
  88.3 0.4 collective-permute-start.22
  88.7 1.6 %collective-permute-start.27 = (bf16[512,128]{1,0:T(8,128)(2,1)S(1)}, bf16[512,128]{1,0:T(8,128)(2,1)S(1)}, u32[]{:S(2)}, u32[]{:S(2)}) collective-permute-start(bf16[512,128]{1,0:T(8,128)(2,1)S(1)} %add_second.1.refs_1_.refs_14_.refs_0_), channel_id=1, source_target_pairs={{0,96},{1,97},{4,100},{5,101},{2,98},{3,99},{6,102},{7,103},{8,104... | collective-permute-start | bytes 393224 | tf_op jit(solution)/shard_map/ppermute | solution.py:35
  90.3 0.8 collective-permute-start.26
  91.1 0.9 collective-permute-start.25
  92.0 0.9 collective-permute-start.28
  92.9 0.6 collective-permute-done.22.refs_5_
  93.5 5.6 %weight_grads.1 = (f32[2048,256]{1,0:T(8,128)}, f32[2048,256]{1,0:T(8,128)}, f32[8,128]{1,0:T(8,128)S(1)}) custom-call(s32[45]{0:T(128)S(1)} %stack.183.table, bf16[256,2048]{1,0:T(8,128)(2,1)S(1)} %copy-done.2, bf16[256,2048]{1,0:T(8,128)(2,1)S(1)} %collective-permute-done.refs_1_, bf16[256,2048]{1,0:T(8,128)(2,1)S(1)} %wait_for.9.second.slice_one.refs_2_, ...), custom_call_target="tpu_custom_call" | custom-call | tf_op jit(solution)/shard_map/weight_grads/pallas_call | solution.py:391
  99.2 0.4 collective-permute-start.31
  100.1 0.5 collective-permute-done.31.refs_7_
  101.1 2.9 %projector_grad.1 = f32[1920,256]{1,0:T(8,128)} custom-call(s32[45]{0:T(128)S(1)} %stack.183.table, bf16[1920,1024]{1,0:T(8,128)(2,1)S(1)} %get-tuple-element.45.feature_ref, bf16[512,128]{1,0:T(8,128)(2,1)S(1)} %add_second.1.refs_1_.refs_14_.refs_0_, bf16[512,128]{1,0:T(8,128)(2,1)S(1)} %wait_for.15.refs_1_, bf16[512,128]{1,0:T(8,128)(2,1)S(1)} %wait_for.16.refs_2_, ...), custom_call_target="tpu_custom_call" | custom-call | tf_op jit(solution)/shard_map/projector_grad/pallas_call | solution.py:473
  (54 shorter events, 2.3 us)
Async XLA Ops:
  0.6 15.2 %collective-permute-start = (bf16[256,2048]{1,0:T(8,128)(2,1)}, bf16[256,2048]{1,0:T(8,128)(2,1)S(1)}, u32[]{:S(2)}, u32[]{:S(2)}) collective-permute-start(bf16[256,2048]{1,0:T(8,128)(2,1)} %refs_0_.3), channel_id=1, source_target_pairs={{0,1},{1,0},{4,5},{5,4},{2,3},{3,2},{6,7},{7,6},{8,9},{9,8},{12,13... | collective-permute-start | bytes 3145736 | tf_op jit(solution)/shard_map/ppermute | solution.py:35
  2.1 26.1 %collective-permute-start.1 = (bf16[256,2048]{1,0:T(8,128)(2,1)}, bf16[256,2048]{1,0:T(8,128)(2,1)S(1)}, u32[]{:S(2)}, u32[]{:S(2)}) collective-permute-start(bf16[256,2048]{1,0:T(8,128)(2,1)} %refs_0_.3), channel_id=1, source_target_pairs={{0,6},{1,7},{4,2},{5,3},{2,4},{3,5},{6,0},{7,1},{8,14},{9,15},{12,... | collective-permute-start | bytes 3145736 | tf_op jit(solution)/shard_map/ppermute | solution.py:35
  4.7 6.9 %copy-start.7 = (s32[512]{0:T(512)S(1)}, s32[512]{0:T(512)}, u32[]{:S(2)}) copy-start(s32[512]{0:T(512)} %param.12) | copy-start | bytes 6148
  7.8 20.5 %collective-permute-start.2 = (bf16[256,1920]{1,0:T(8,128)(2,1)}, bf16[256,1920]{1,0:T(8,128)(2,1)S(1)}, u32[]{:S(2)}, u32[]{:S(2)}) collective-permute-start(bf16[256,1920]{1,0:T(8,128)(2,1)} %get-tuple-element.26), channel_id=1, source_target_pairs={{0,32},{1,97},{4,36},{5,101},{2,34},{3,99},{6,38},{7,103},{8,40},{... | collective-permute-start | bytes 2949128 | tf_op jit(solution)/shard_map/ppermute | solution.py:35
  11.6 10.0 %collective-permute-start.3 = (bf16[64,1920]{1,0:T(8,128)(2,1)}, bf16[64,1920]{1,0:T(8,128)(2,1)S(1)}, u32[]{:S(2)}, u32[]{:S(2)}) collective-permute-start(bf16[64,1920]{1,0:T(8,128)(2,1)} %get-tuple-element.27), channel_id=1, source_target_pairs={{0,64},{1,65},{4,68},{5,69},{2,66},{3,67},{6,70},{7,71},{8,72},{9,... | collective-permute-start | bytes 737288 | tf_op jit(solution)/shard_map/ppermute | solution.py:35
  12.5 1.6 %copy-start.3 = (bf16[512,2048]{1,0:T(8,128)(2,1)S(1)}, bf16[512,2048]{1,0:T(8,128)(2,1)}, u32[]{:S(2)}) copy-start(bf16[512,2048]{1,0:T(8,128)(2,1)} %grad_ref.1) | copy-start | bytes 6291460
  14.1 0.9 copy-start.5
  15.1 1.2 %copy-start.2 = (bf16[256,2048]{1,0:T(8,128)(2,1)S(1)}, bf16[256,2048]{1,0:T(8,128)(2,1)}, u32[]{:S(2)}) copy-start(bf16[256,2048]{1,0:T(8,128)(2,1)} %refs_0_.3) | copy-start | bytes 3145732
  16.3 22.4 %copy-start.1 = (bf16[1,8192,256]{2,1,0:T(8,128)(2,1)S(1)}, bf16[1,8192,256]{2,1,0:T(8,128)(2,1)}, u32[]{:S(2)}) copy-start(bf16[1,8192,256]{2,1,0:T(8,128)(2,1)} %param.14) | copy-start | bytes 12582916
  28.3 10.5 %copy-start = (bf16[1,8192,256]{2,1,0:T(8,128)(2,1)S(1)}, bf16[1,8192,256]{2,1,0:T(8,128)(2,1)}, u32[]{:S(2)}) copy-start(bf16[1,8192,256]{2,1,0:T(8,128)(2,1)} %param.13) | copy-start | bytes 12582916
  28.3 10.5 %copy-start.4 = (bf16[512,2048]{1,0:T(8,128)(2,1)S(1)}, bf16[512,2048]{1,0:T(8,128)(2,1)}, u32[]{:S(2)}) copy-start(bf16[512,2048]{1,0:T(8,128)(2,1)} %query_ref.1) | copy-start | bytes 6291460
  28.3 10.5 %copy-start.6 = (f32[1,128]{1,0:T(1,128)S(1)}, f32[1,128]{1,0:T(1,128)}, u32[]{:S(2)}) copy-start(f32[1,128]{1,0:T(1,128)} %gain_ref.1) | copy-start | bytes 1540
  28.3 10.4 %collective-permute-start.4 = (bf16[256,2048]{1,0:T(8,128)(2,1)S(1)}, bf16[256,2048]{1,0:T(8,128)(2,1)S(1)}, u32[]{:S(2)}, u32[]{:S(2)}) collective-permute-start(bf16[256,2048]{1,0:T(8,128)(2,1)S(1)} %wait_for.9.second.slice_one.refs_2_), channel_id=1, source_target_pairs={{0,1},{1,0},{4,5},{5,4},{2,3},{3,2},{6,7},{7,6},{8,9},{9,8},{12,13... | collective-permute-start | bytes 3145736 | tf_op jit(solution)/shard_map/ppermute | solution.py:35
  32.1 19.0 %collective-permute-start.5 = (bf16[256,2048]{1,0:T(8,128)(2,1)S(1)}, bf16[256,2048]{1,0:T(8,128)(2,1)S(1)}, u32[]{:S(2)}, u32[]{:S(2)}) collective-permute-start(bf16[256,2048]{1,0:T(8,128)(2,1)S(1)} %get-tuple-element.28), channel_id=1, source_target_pairs={{1,33},{5,37},{3,35},{7,39},{9,41},{13,45},{11,43},{15,47},{17,49}... | collective-permute-start | bytes 3145736 | tf_op jit(solution)/shard_map/ppermute | solution.py:35
  33.7 17.3 %collective-permute-start.6 = (bf16[256,2048]{1,0:T(8,128)(2,1)S(1)}, bf16[256,2048]{1,0:T(8,128)(2,1)S(1)}, u32[]{:S(2)}, u32[]{:S(2)}) collective-permute-start(bf16[256,2048]{1,0:T(8,128)(2,1)S(1)} %get-tuple-element.32), channel_id=1, source_target_pairs={{1,97},{5,101},{3,99},{7,103},{9,105},{13,109},{11,107},{15,111},{... | collective-permute-start | bytes 3145736 | tf_op jit(solution)/shard_map/ppermute | solution.py:35
  37.2 13.9 %collective-permute-start.7 = (bf16[64,1920]{1,0:T(8,128)(2,1)S(1)}, bf16[64,1920]{1,0:T(8,128)(2,1)S(1)}, u32[]{:S(2)}, u32[]{:S(2)}) collective-permute-start(bf16[64,1920]{1,0:T(8,128)(2,1)S(1)} %collective-permute-done.3.refs_4_.refs_3_.rest_0_), channel_id=1, source_target_pairs={{0,8},{1,9},{4,12},{5,13},{2,10},{3,11},{6,14},{7,15},{8,0},{9,1},... | collective-permute-start | bytes 737288 | tf_op jit(solution)/shard_map/ppermute | solution.py:35
  51.1 5.3 %collective-permute-start.8 = (bf16[8192,128]{1,0:T(8,128)(2,1)S(1)}, bf16[8192,128]{1,0:T(8,128)(2,1)S(1)}, u32[]{:S(2)}, u32[]{:S(2)}) collective-permute-start(bf16[8192,128]{1,0:T(8,128)(2,1)S(1)} %wait_for.10), channel_id=1, source_target_pairs={{0,1},{1,0},{4,5},{5,4},{2,3},{3,2},{6,7},{7,6},{8,9},{9,8},{12,13... | collective-permute-start | bytes 6291464 | tf_op jit(solution)/shard_map/ppermute | solution.py:35
  51.6 20.4 %collective-permute-start.14 = (bf16[256,2048]{1,0:T(8,128)(2,1)S(1)}, bf16[256,2048]{1,0:T(8,128)(2,1)S(1)}, u32[]{:S(2)}, u32[]{:S(2)}) collective-permute-start(bf16[256,2048]{1,0:T(8,128)(2,1)S(1)} %get-tuple-element.28), channel_id=1, source_target_pairs={{0,65},{4,69},{2,67},{6,71},{8,73},{12,77},{10,75},{14,79},{16,81}... | collective-permute-start | bytes 3145736 | tf_op jit(solution)/shard_map/ppermute | solution.py:35
  52.9 3.1 %collective-permute-start.9 = (bf16[64,1920]{1,0:T(8,128)(2,1)S(1)}, bf16[64,1920]{1,0:T(8,128)(2,1)S(1)}, u32[]{:S(2)}, u32[]{:S(2)}) collective-permute-start(bf16[64,1920]{1,0:T(8,128)(2,1)S(1)} %collective-permute-done.3.refs_4_.refs_3_.rest_0_), channel_id=1, source_target_pairs={{0,1},{1,0},{4,5},{5,4},{2,3},{3,2},{6,7},{7,6},{8,9},{9,8},{12,13... | collective-permute-start | bytes 737288 | tf_op jit(solution)/shard_map/ppermute | solution.py:35
  54.9 1.5 %collective-permute-start.10 = (bf16[64,1920]{1,0:T(8,128)(2,1)S(1)}, bf16[64,1920]{1,0:T(8,128)(2,1)S(1)}, u32[]{:S(2)}, u32[]{:S(2)}) collective-permute-start(bf16[64,1920]{1,0:T(8,128)(2,1)S(1)} %collective-permute-done.7.refs_4_.rest_1_), channel_id=1, source_target_pairs={{0,1},{1,0},{4,5},{5,4},{2,3},{3,2},{6,7},{7,6},{8,9},{9,8},{12,13... | collective-permute-start | bytes 737288 | tf_op jit(solution)/shard_map/ppermute | solution.py:35
  56.9 15.1 %collective-permute-start.11 = (bf16[2048,128]{1,0:T(8,128)(2,1)S(1)}, bf16[2048,128]{1,0:T(8,128)(2,1)S(1)}, u32[]{:S(2)}, u32[]{:S(2)}) collective-permute-start(bf16[2048,128]{1,0:T(8,128)(2,1)S(1)} %get-tuple-element.34), channel_id=1, source_target_pairs={{0,2},{1,17},{4,6},{5,21},{2,0},{3,19},{6,4},{7,23},{8,10},{9,25},... | collective-permute-start | bytes 1572872 | tf_op jit(solution)/shard_map/ppermute | solution.py:35
  59.7 12.9 %collective-permute-start.12 = (bf16[2048,128]{1,0:T(8,128)(2,1)S(1)}, bf16[2048,128]{1,0:T(8,128)(2,1)S(1)}, u32[]{:S(2)}, u32[]{:S(2)}) collective-permute-start(bf16[2048,128]{1,0:T(8,128)(2,1)S(1)} %get-tuple-element.35), channel_id=1, source_target_pairs={{0,4},{1,9},{4,0},{5,13},{2,6},{3,11},{6,2},{7,15},{8,12},{9,1},{1... | collective-permute-start | bytes 1572872 | tf_op jit(solution)/shard_map/ppermute | solution.py:35
  60.1 12.5 %collective-permute-start.13 = (bf16[2048,128]{1,0:T(8,128)(2,1)S(1)}, bf16[2048,128]{1,0:T(8,128)(2,1)S(1)}, u32[]{:S(2)}, u32[]{:S(2)}) collective-permute-start(bf16[2048,128]{1,0:T(8,128)(2,1)S(1)} %get-tuple-element.36), channel_id=1, source_target_pairs={{0,6},{1,25},{4,2},{5,29},{2,4},{3,27},{6,0},{7,31},{8,14},{9,17},... | collective-permute-start | bytes 1572872 | tf_op jit(solution)/shard_map/ppermute | solution.py:35
  60.5 11.6 %collective-permute-start.15 = (bf16[256,512]{1,0:T(8,128)(2,1)S(1)}, bf16[256,512]{1,0:T(8,128)(2,1)S(1)}, u32[]{:S(2)}, u32[]{:S(2)}) collective-permute-start(bf16[256,512]{1,0:T(8,128)(2,1)S(1)} %get-tuple-element.37.refs_10_), channel_id=1, source_target_pairs={{0,64},{1,65},{4,68},{5,69},{2,66},{3,67},{6,70},{7,71},{8,72},{9,... | collective-permute-start | bytes 786440 | tf_op jit(solution)/shard_map/ppermute | solution.py:35
  72.9 7.2 %collective-permute-start.19 = (bf16[256,1920]{1,0:T(8,128)(2,1)S(1)}, bf16[256,1920]{1,0:T(8,128)(2,1)S(1)}, u32[]{:S(2)}, u32[]{:S(2)}) collective-permute-start(bf16[256,1920]{1,0:T(8,128)(2,1)S(1)} %wait_for.11.near_ref), channel_id=1, source_target_pairs={{0,1},{1,0},{4,5},{5,4},{2,3},{3,2},{6,7},{7,6},{8,9},{9,8},{12,13... | collective-permute-start | bytes 2949128 | tf_op jit(solution)/shard_map/ppermute | solution.py:35
  75.9 7.9 %collective-permute-start.20 = (bf16[256,512]{1,0:T(8,128)(2,1)S(1)}, bf16[256,512]{1,0:T(8,128)(2,1)S(1)}, u32[]{:S(2)}, u32[]{:S(2)}) collective-permute-start(bf16[256,512]{1,0:T(8,128)(2,1)S(1)} %get-tuple-element.37.refs_10_), channel_id=1, source_target_pairs={{0,32},{1,33},{4,36},{5,37},{2,34},{3,35},{6,38},{7,39},{8,40},{9,... | collective-permute-start | bytes 786440 | tf_op jit(solution)/shard_map/ppermute | solution.py:35
  75.9 8.9 %collective-permute-start.21 = (bf16[256,512]{1,0:T(8,128)(2,1)S(1)}, bf16[256,512]{1,0:T(8,128)(2,1)S(1)}, u32[]{:S(2)}, u32[]{:S(2)}) collective-permute-start(bf16[256,512]{1,0:T(8,128)(2,1)S(1)} %get-tuple-element.37.refs_10_), channel_id=1, source_target_pairs={{0,96},{1,97},{4,100},{5,101},{2,98},{3,99},{6,102},{7,103},{8,104... | collective-permute-start | bytes 786440 | tf_op jit(solution)/shard_map/ppermute | solution.py:35
  77.0 7.8 %collective-permute-start.16 = (bf16[512,128]{1,0:T(8,128)(2,1)S(1)}, bf16[512,128]{1,0:T(8,128)(2,1)S(1)}, u32[]{:S(2)}, u32[]{:S(2)}) collective-permute-start(bf16[512,128]{1,0:T(8,128)(2,1)S(1)} %get-tuple-element.39), channel_id=1, source_target_pairs={{0,16},{1,3},{4,20},{5,7},{2,18},{3,1},{6,22},{7,5},{8,24},{9,11},... | collective-permute-start | bytes 393224 | tf_op jit(solution)/shard_map/ppermute | solution.py:35
  78.6 6.3 %collective-permute-start.17 = (bf16[512,128]{1,0:T(8,128)(2,1)S(1)}, bf16[512,128]{1,0:T(8,128)(2,1)S(1)}, u32[]{:S(2)}, u32[]{:S(2)}) collective-permute-start(bf16[512,128]{1,0:T(8,128)(2,1)S(1)} %get-tuple-element.40), channel_id=1, source_target_pairs={{0,8},{1,5},{4,12},{5,1},{2,10},{3,7},{6,14},{7,3},{8,0},{9,13},{1... | collective-permute-start | bytes 393224 | tf_op jit(solution)/shard_map/ppermute | solution.py:35
  80.1 5.3 %collective-permute-start.18 = (bf16[512,128]{1,0:T(8,128)(2,1)S(1)}, bf16[512,128]{1,0:T(8,128)(2,1)S(1)}, u32[]{:S(2)}, u32[]{:S(2)}) collective-permute-start(bf16[512,128]{1,0:T(8,128)(2,1)S(1)} %get-tuple-element.41), channel_id=1, source_target_pairs={{0,24},{1,7},{4,28},{5,3},{2,26},{3,5},{6,30},{7,1},{8,16},{9,15},... | collective-permute-start | bytes 393224 | tf_op jit(solution)/shard_map/ppermute | solution.py:35
  86.1 5.0 %collective-permute-start.24 = (bf16[256,2048]{1,0:T(8,128)(2,1)S(1)}, bf16[256,2048]{1,0:T(8,128)(2,1)S(1)}, u32[]{:S(2)}, u32[]{:S(2)}) collective-permute-start(bf16[256,2048]{1,0:T(8,128)(2,1)S(1)} %wait_for.14.refs_8_), channel_id=1, source_target_pairs={{0,1},{1,0},{4,5},{5,4},{2,3},{3,2},{6,7},{7,6},{8,9},{9,8},{12,13... | collective-permute-start | bytes 3145736 | tf_op jit(solution)/shard_map/ppermute | solution.py:35
  88.2 3.8 %collective-permute-start.23 = (bf16[256,2048]{1,0:T(8,128)(2,1)S(1)}, bf16[256,2048]{1,0:T(8,128)(2,1)S(1)}, u32[]{:S(2)}, u32[]{:S(2)}) collective-permute-start(bf16[256,2048]{1,0:T(8,128)(2,1)S(1)} %wait_for.13.refs_6_), channel_id=1, source_target_pairs={{0,1},{1,0},{4,5},{5,4},{2,3},{3,2},{6,7},{7,6},{8,9},{9,8},{12,13... | collective-permute-start | bytes 3145736 | tf_op jit(solution)/shard_map/ppermute | solution.py:35
  88.3 5.2 %collective-permute-start.22 = (bf16[256,2048]{1,0:T(8,128)(2,1)S(1)}, bf16[256,2048]{1,0:T(8,128)(2,1)S(1)}, u32[]{:S(2)}, u32[]{:S(2)}) collective-permute-start(bf16[256,2048]{1,0:T(8,128)(2,1)S(1)} %wait_for.12.refs_4_), channel_id=1, source_target_pairs={{0,1},{1,0},{4,5},{5,4},{2,3},{3,2},{6,7},{7,6},{8,9},{9,8},{12,13... | collective-permute-start | bytes 3145736 | tf_op jit(solution)/shard_map/ppermute | solution.py:35
  88.7 10.4 %collective-permute-start.27 = (bf16[512,128]{1,0:T(8,128)(2,1)S(1)}, bf16[512,128]{1,0:T(8,128)(2,1)S(1)}, u32[]{:S(2)}, u32[]{:S(2)}) collective-permute-start(bf16[512,128]{1,0:T(8,128)(2,1)S(1)} %add_second.1.refs_1_.refs_14_.refs_0_), channel_id=1, source_target_pairs={{0,96},{1,97},{4,100},{5,101},{2,98},{3,99},{6,102},{7,103},{8,104... | collective-permute-start | bytes 393224 | tf_op jit(solution)/shard_map/ppermute | solution.py:35
  90.3 9.2 %collective-permute-start.26 = (bf16[512,128]{1,0:T(8,128)(2,1)S(1)}, bf16[512,128]{1,0:T(8,128)(2,1)S(1)}, u32[]{:S(2)}, u32[]{:S(2)}) collective-permute-start(bf16[512,128]{1,0:T(8,128)(2,1)S(1)} %add_second.1.refs_1_.refs_14_.refs_0_), channel_id=1, source_target_pairs={{0,64},{1,65},{4,68},{5,69},{2,66},{3,67},{6,70},{7,71},{8,72},{9,... | collective-permute-start | bytes 393224 | tf_op jit(solution)/shard_map/ppermute | solution.py:35
  91.1 8.6 %collective-permute-start.25 = (bf16[512,128]{1,0:T(8,128)(2,1)S(1)}, bf16[512,128]{1,0:T(8,128)(2,1)S(1)}, u32[]{:S(2)}, u32[]{:S(2)}) collective-permute-start(bf16[512,128]{1,0:T(8,128)(2,1)S(1)} %add_second.1.refs_1_.refs_14_.refs_0_), channel_id=1, source_target_pairs={{0,32},{1,33},{4,36},{5,37},{2,34},{3,35},{6,38},{7,39},{8,40},{9,... | collective-permute-start | bytes 393224 | tf_op jit(solution)/shard_map/ppermute | solution.py:35
  92.0 8.0 %collective-permute-start.28 = (bf16[512,128]{1,0:T(8,128)(2,1)S(1)}, bf16[512,128]{1,0:T(8,128)(2,1)S(1)}, u32[]{:S(2)}, u32[]{:S(2)}) collective-permute-start(bf16[512,128]{1,0:T(8,128)(2,1)S(1)} %add_second.1.refs_1_.refs_14_.refs_0_), channel_id=1, source_target_pairs={{0,1},{1,0},{4,5},{5,4},{2,3},{3,2},{6,7},{7,6},{8,9},{9,8},{12,13... | collective-permute-start | bytes 393224 | tf_op jit(solution)/shard_map/ppermute | solution.py:35
  99.2 1.4 %collective-permute-start.31 = (bf16[512,128]{1,0:T(8,128)(2,1)S(1)}, bf16[512,128]{1,0:T(8,128)(2,1)S(1)}, u32[]{:S(2)}, u32[]{:S(2)}) collective-permute-start(bf16[512,128]{1,0:T(8,128)(2,1)S(1)} %wait_for.17.refs_3_), channel_id=1, source_target_pairs={{0,1},{1,0},{4,5},{5,4},{2,3},{3,2},{6,7},{7,6},{8,9},{9,8},{12,13... | collective-permute-start | bytes 393224 | tf_op jit(solution)/shard_map/ppermute | solution.py:35
  99.5 1.3 %collective-permute-start.30 = (bf16[512,128]{1,0:T(8,128)(2,1)S(1)}, bf16[512,128]{1,0:T(8,128)(2,1)S(1)}, u32[]{:S(2)}, u32[]{:S(2)}) collective-permute-start(bf16[512,128]{1,0:T(8,128)(2,1)S(1)} %wait_for.16.refs_2_), channel_id=1, source_target_pairs={{0,1},{1,0},{4,5},{5,4},{2,3},{3,2},{6,7},{7,6},{8,9},{9,8},{12,13... | collective-permute-start | bytes 393224 | tf_op jit(solution)/shard_map/ppermute | solution.py:35
  99.7 1.4 %collective-permute-start.29 = (bf16[512,128]{1,0:T(8,128)(2,1)S(1)}, bf16[512,128]{1,0:T(8,128)(2,1)S(1)}, u32[]{:S(2)}, u32[]{:S(2)}) collective-permute-start(bf16[512,128]{1,0:T(8,128)(2,1)S(1)} %wait_for.15.refs_1_), channel_id=1, source_target_pairs={{0,1},{1,0},{4,5},{5,4},{2,3},{3,2},{6,7},{7,6},{8,9},{9,8},{12,13... | collective-permute-start | bytes 393224 | tf_op jit(solution)/shard_map/ppermute | solution.py:35

commit v5 on v4

--- a/solution.py
+++ b/solution.py
@@ -114,10 +114,14 @@
             return pl.ds(pl.multiple_of(table[k] * width, 128), width)
 
         lines = pl.ds(pl.multiple_of(table[at_quarter] * quarter, quarter), quarter)
-        copies = [
-            pltpu.make_async_copy(source.at[lines, columns(at_far)], far, sems.at[0]),
-            pltpu.make_async_copy(source.at[:, columns(at_near)], near, sems.at[1]),
-        ]
+        copies = [pltpu.make_async_copy(source.at[lines, columns(at_far)], far, sems.at[4])]
+        for i in range(4):
+            part = pl.ds(i * quarter, quarter)
+            copies.append(
+                pltpu.make_async_copy(
+                    source.at[part, columns(at_near)], near.at[part, :], sems.at[i]
+                )
+            )
         for copy in copies:
             copy.start()
         for copy in copies:
@@ -128,7 +132,7 @@
         in_specs=[in_smem, in_hbm],
         out_specs=[in_vmem] * 2,
         out_shape=[jax.ShapeDtypeStruct((r, width), bf16) for r in (rows, quarter)],
-        scratch_shapes=[pltpu.SemaphoreType.DMA((2,))],
+        scratch_shapes=[pltpu.SemaphoreType.DMA((5,))],
         compiler_params=small_params,
         name="cut_features",
     )(table, far_away(features))

time: 104 us -> 105 us (level)
  no operation moved by 1% of the time
where the time goes in v5:
time: 105 us; the launch traced here: 104 us
  starting transfers between devices  42.6 us (41%)
  Pallas kernels  34.9 us (33%)
  waiting for transfers between devices  21.7 us (21%)
  local copies, waits for them, and re-layouts  4 us (4%)
    ppermute x32, starting transfers between devices, send(): return lax.ppermute(array, every_axis, exchange_pairs(moved))  42.6 us
    ppermute x32, waiting for transfers between devices, send(): return lax.ppermute(array, every_axis, exchange_pairs(moved))  21.7 us
    pallas_call x1, Pallas kernels, middle(): pl.pallas_call(kernel, in_specs=[in_smem] + [in_vmem] * 8, out_specs=[in_...  12.3 us
    pallas_call x1, Pallas kernels, weight_grads(): pl.pallas_call(kernel, grid_spec=pltpu.PrefetchScalarGridSpec(num_scalar_...  5.64 us
    pallas_call x1, Pallas kernels, project(): pl.pallas_call(kernel, in_specs=[in_smem] + [in_vmem] * n + [in_hbm] * 2,...  5.33 us
    pallas_call x1, Pallas kernels, cut_features(): pl.pallas_call(kernel, in_specs=[in_smem, in_hbm], out_specs=[in_vmem] *...  2.99 us
    unnamed x16, local copies, waits for them, and re-layouts  2.97 us
    pallas_call x1, Pallas kernels, turn_features(): pl.pallas_call(kernel, grid_spec=pltpu.PrefetchScalarGridSpec(num_scalar_...  2.94 us
  transfers between devices with their start and end apart: 32, of which 12 were waited for; matrix products, arithmetic and copies ran while one was open for 1% of the time, Pallas kernels for 30%

profile of v5, /device:TPU:1, one launch (start us, length us, event | category | flops | bytes accessed | tf_op | source)
XLA Modules:
  0.0 104.2 jit_solution(2353732053097205455)
XLA Ops:
  0.6 1.5 %collective-permute-start = (bf16[256,2048]{1,0:T(8,128)(2,1)}, bf16[256,2048]{1,0:T(8,128)(2,1)S(1)}, u32[]{:S(2)}, u32[]{:S(2)}) collective-permute-start(bf16[256,2048]{1,0:T(8,128)(2,1)} %refs_0_.3), channel_id=1, source_target_pairs={{0,1},{1,0},{4,5},{5,4},{2,3},{3,2},{6,7},{7,6},{8,9},{9,8},{12,13... | collective-permute-start | bytes 3145736 | tf_op jit(solution)/shard_map/ppermute | solution.py:35
  2.1 2.6 %collective-permute-start.1 = (bf16[256,2048]{1,0:T(8,128)(2,1)}, bf16[256,2048]{1,0:T(8,128)(2,1)S(1)}, u32[]{:S(2)}, u32[]{:S(2)}) collective-permute-start(bf16[256,2048]{1,0:T(8,128)(2,1)} %refs_0_.3), channel_id=1, source_target_pairs={{0,6},{1,7},{4,2},{5,3},{2,4},{3,5},{6,0},{7,1},{8,14},{9,15},{12,... | collective-permute-start | bytes 3145736 | tf_op jit(solution)/shard_map/ppermute | solution.py:35
  4.9 3.0 %cut_features.1 = (bf16[256,1920]{1,0:T(8,128)(2,1)}, bf16[64,1920]{1,0:T(8,128)(2,1)}) custom-call(s32[45]{0:T(128)S(1)} %stack.183.table, bf16[256,7680]{1,0:T(8,128)(2,1)} %own_ref.1), custom_call_target="tpu_custom_call" | custom-call | tf_op jit(solution)/shard_map/cut_features/pallas_call | solution.py:130
  7.9 3.8 %collective-permute-start.2 = (bf16[256,1920]{1,0:T(8,128)(2,1)}, bf16[256,1920]{1,0:T(8,128)(2,1)S(1)}, u32[]{:S(2)}, u32[]{:S(2)}) collective-permute-start(bf16[256,1920]{1,0:T(8,128)(2,1)} %get-tuple-element.26), channel_id=1, source_target_pairs={{0,32},{1,97},{4,36},{5,101},{2,34},{3,99},{6,38},{7,103},{8,40},{... | collective-permute-start | bytes 2949128 | tf_op jit(solution)/shard_map/ppermute | solution.py:35
  11.7 0.9 copy.20.mask_ref
  12.6 1.6 %copy-done.3 = bf16[512,2048]{1,0:T(8,128)(2,1)S(1)} copy-done((bf16[512,2048]{1,0:T(8,128)(2,1)S(1)}, bf16[512,2048]{1,0:T(8,128)(2,1)}, u32[]{:S(2)}) %copy-start.3) | copy-done | bytes 2097176
  14.2 0.9 copy-done.5
  15.1 0.8 mask_rows.1.refs_2_.masked_ref
  15.9 0.4 copy-done.2
  16.4 5.3 %project.1 = (f32[256,512]{1,0:T(8,128)S(1)}, f32[8,128]{1,0:T(8,128)S(1)}) custom-call(s32[45]{0:T(128)S(1)} %stack.183.table, bf16[256,2048]{1,0:T(8,128)(2,1)S(1)} %copy-done.2, bf16[256,2048]{1,0:T(8,128)(2,1)S(1)} %collective-permute-done.refs_1_, bf16[8192,256]{1,0:T(8,128)(2,1)} %bitcast.50, bf16[8192,256]{1,0:T(8,128)(2,1)} %bitcast.52), custom_call_target="tpu_custom_call" | custom-call | tf_op jit(solution)/shard_map/project/pallas_call | solution.py:180
  21.7 6.6 %collective-permute-done.2.refs_3_.refs_0_ = bf16[256,1920]{1,0:T(8,128)(2,1)S(1)} collective-permute-done((bf16[256,1920]{1,0:T(8,128)(2,1)}, bf16[256,1920]{1,0:T(8,128)(2,1)S(1)}, u32[]{:S(2)}, u32[]{:S(2)}) %collective-permute-start.2) | collective-permute-done | bytes 983072 | tf_op jit(solution)/shard_map/ppermute | solution.py:35
  28.4 3.1 %collective-permute-start.4 = (bf16[256,2048]{1,0:T(8,128)(2,1)S(1)}, bf16[256,2048]{1,0:T(8,128)(2,1)S(1)}, u32[]{:S(2)}, u32[]{:S(2)}) collective-permute-start(bf16[256,2048]{1,0:T(8,128)(2,1)S(1)} %wait_for.9.second.slice_one.refs_2_), channel_id=1, source_target_pairs={{0,1},{1,0},{4,5},{5,4},{2,3},{3,2},{6,7},{7,6},{8,9},{9,8},{12,13... | collective-permute-start | bytes 3145736 | tf_op jit(solution)/shard_map/ppermute | solution.py:35
  31.5 0.7 choose.1
  32.2 1.6 %collective-permute-start.5 = (bf16[256,2048]{1,0:T(8,128)(2,1)S(1)}, bf16[256,2048]{1,0:T(8,128)(2,1)S(1)}, u32[]{:S(2)}, u32[]{:S(2)}) collective-permute-start(bf16[256,2048]{1,0:T(8,128)(2,1)S(1)} %get-tuple-element.28), channel_id=1, source_target_pairs={{1,33},{5,37},{3,35},{7,39},{9,41},{13,45},{11,43},{15,47},{17,49}... | collective-permute-start | bytes 3145736 | tf_op jit(solution)/shard_map/ppermute | solution.py:35
  33.8 3.3 %collective-permute-start.6 = (bf16[256,2048]{1,0:T(8,128)(2,1)S(1)}, bf16[256,2048]{1,0:T(8,128)(2,1)S(1)}, u32[]{:S(2)}, u32[]{:S(2)}) collective-permute-start(bf16[256,2048]{1,0:T(8,128)(2,1)S(1)} %get-tuple-element.32), channel_id=1, source_target_pairs={{1,97},{5,101},{3,99},{7,103},{9,105},{13,109},{11,107},{15,111},{... | collective-permute-start | bytes 3145736 | tf_op jit(solution)/shard_map/ppermute | solution.py:35
  37.2 1.6 %collective-permute-start.7 = (bf16[64,1920]{1,0:T(8,128)(2,1)S(1)}, bf16[64,1920]{1,0:T(8,128)(2,1)S(1)}, u32[]{:S(2)}, u32[]{:S(2)}) collective-permute-start(bf16[64,1920]{1,0:T(8,128)(2,1)S(1)} %collective-permute-done.3.refs_4_.refs_3_.rest_0_), channel_id=1, source_target_pairs={{0,8},{1,9},{4,12},{5,13},{2,10},{3,11},{6,14},{7,15},{8,0},{9,1},... | collective-permute-start | bytes 737288 | tf_op jit(solution)/shard_map/ppermute | solution.py:35
  38.8 12.3 %middle.1 = (bf16[256,512]{1,0:T(8,128)(2,1)S(1)}, bf16[8192,128]{1,0:T(8,128)(2,1)S(1)}, bf16[8192,128]{1,0:T(8,128)(2,1)S(1)}) custom-call(s32[45]{0:T(128)S(1)} %stack.183.table, bf16[256,2048]{1,0:T(8,128)(2,1)S(1)} %wait_for.9.second.slice_one.refs_2_, bf16[256,2048]{1,0:T(8,128)(2,1)S(1)} %collective-permute-done.4.slice_two.refs_3_, ...), custom_call_target="tpu_custom_call" | custom-call | tf_op jit(solution)/shard_map/middle/pallas_call | solution.py:277
  51.1 0.6 collective-permute-start.8
  51.7 1.3 %collective-permute-start.14 = (bf16[256,2048]{1,0:T(8,128)(2,1)S(1)}, bf16[256,2048]{1,0:T(8,128)(2,1)S(1)}, u32[]{:S(2)}, u32[]{:S(2)}) collective-permute-start(bf16[256,2048]{1,0:T(8,128)(2,1)S(1)} %get-tuple-element.28), channel_id=1, source_target_pairs={{0,65},{4,69},{2,67},{6,71},{8,73},{12,77},{10,75},{14,79},{16,81}... | collective-permute-start | bytes 3145736 | tf_op jit(solution)/shard_map/ppermute | solution.py:35
  53.0 1.9 %collective-permute-start.9 = (bf16[64,1920]{1,0:T(8,128)(2,1)S(1)}, bf16[64,1920]{1,0:T(8,128)(2,1)S(1)}, u32[]{:S(2)}, u32[]{:S(2)}) collective-permute-start(bf16[64,1920]{1,0:T(8,128)(2,1)S(1)} %collective-permute-done.3.refs_4_.refs_3_.rest_0_), channel_id=1, source_target_pairs={{0,1},{1,0},{4,5},{5,4},{2,3},{3,2},{6,7},{7,6},{8,9},{9,8},{12,13... | collective-permute-start | bytes 737288 | tf_op jit(solution)/shard_map/ppermute | solution.py:35
  55.0 1.0 %collective-permute-done.9.rest_2_ = bf16[64,1920]{1,0:T(8,128)(2,1)S(1)} collective-permute-done((bf16[64,1920]{1,0:T(8,128)(2,1)S(1)}, bf16[64,1920]{1,0:T(8,128)(2,1)S(1)}, u32[]{:S(2)}, u32[]{:S(2)}) %collective-permute-start.9) | collective-permute-done | bytes 245792 | tf_op jit(solution)/shard_map/ppermute | solution.py:35
  56.4 0.5 add_terms.1
  56.9 2.8 %collective-permute-start.11 = (bf16[2048,128]{1,0:T(8,128)(2,1)S(1)}, bf16[2048,128]{1,0:T(8,128)(2,1)S(1)}, u32[]{:S(2)}, u32[]{:S(2)}) collective-permute-start(bf16[2048,128]{1,0:T(8,128)(2,1)S(1)} %get-tuple-element.34), channel_id=1, source_target_pairs={{0,2},{1,17},{4,6},{5,21},{2,0},{3,19},{6,4},{7,23},{8,10},{9,25},... | collective-permute-start | bytes 1572872 | tf_op jit(solution)/shard_map/ppermute | solution.py:35
  59.7 0.4 collective-permute-start.12
  60.1 0.4 collective-permute-start.13
  60.5 2.3 %collective-permute-start.15 = (bf16[256,512]{1,0:T(8,128)(2,1)S(1)}, bf16[256,512]{1,0:T(8,128)(2,1)S(1)}, u32[]{:S(2)}, u32[]{:S(2)}) collective-permute-start(bf16[256,512]{1,0:T(8,128)(2,1)S(1)} %get-tuple-element.37.refs_10_), channel_id=1, source_target_pairs={{0,64},{1,65},{4,68},{5,69},{2,66},{3,67},{6,70},{7,71},{8,72},{9,... | collective-permute-start | bytes 786440 | tf_op jit(solution)/shard_map/ppermute | solution.py:35
  62.9 9.2 %collective-permute-done.14.refs_4_.refs_0_ = bf16[256,2048]{1,0:T(8,128)(2,1)S(1)} collective-permute-done((bf16[256,2048]{1,0:T(8,128)(2,1)S(1)}, bf16[256,2048]{1,0:T(8,128)(2,1)S(1)}, u32[]{:S(2)}, u32[]{:S(2)}) %collective-permute-start.14) | collective-permute-done | bytes 1048608 | tf_op jit(solution)/shard_map/ppermute | solution.py:35
  72.1 0.6 collective-permute-done.12.refs_2_
  72.9 3.0 %collective-permute-start.19 = (bf16[256,1920]{1,0:T(8,128)(2,1)S(1)}, bf16[256,1920]{1,0:T(8,128)(2,1)S(1)}, u32[]{:S(2)}, u32[]{:S(2)}) collective-permute-start(bf16[256,1920]{1,0:T(8,128)(2,1)S(1)} %wait_for.11.near_ref), channel_id=1, source_target_pairs={{0,1},{1,0},{4,5},{5,4},{2,3},{3,2},{6,7},{7,6},{8,9},{9,8},{12,13... | collective-permute-start | bytes 2949128 | tf_op jit(solution)/shard_map/ppermute | solution.py:35
  76.0 1.1 %collective-permute-start.21 = (bf16[256,512]{1,0:T(8,128)(2,1)S(1)}, bf16[256,512]{1,0:T(8,128)(2,1)S(1)}, u32[]{:S(2)}, u32[]{:S(2)}) collective-permute-start(bf16[256,512]{1,0:T(8,128)(2,1)S(1)} %get-tuple-element.37.refs_10_), channel_id=1, source_target_pairs={{0,96},{1,97},{4,100},{5,101},{2,98},{3,99},{6,102},{7,103},{8,104... | collective-permute-start | bytes 786440 | tf_op jit(solution)/shard_map/ppermute | solution.py:35
  77.0 1.5 %collective-permute-start.16 = (bf16[512,128]{1,0:T(8,128)(2,1)S(1)}, bf16[512,128]{1,0:T(8,128)(2,1)S(1)}, u32[]{:S(2)}, u32[]{:S(2)}) collective-permute-start(bf16[512,128]{1,0:T(8,128)(2,1)S(1)} %get-tuple-element.39), channel_id=1, source_target_pairs={{0,16},{1,3},{4,20},{5,7},{2,18},{3,1},{6,22},{7,5},{8,24},{9,11},... | collective-permute-start | bytes 393224 | tf_op jit(solution)/shard_map/ppermute | solution.py:35
  78.6 1.5 %collective-permute-start.17 = (bf16[512,128]{1,0:T(8,128)(2,1)S(1)}, bf16[512,128]{1,0:T(8,128)(2,1)S(1)}, u32[]{:S(2)}, u32[]{:S(2)}) collective-permute-start(bf16[512,128]{1,0:T(8,128)(2,1)S(1)} %get-tuple-element.40), channel_id=1, source_target_pairs={{0,8},{1,5},{4,12},{5,1},{2,10},{3,7},{6,14},{7,3},{8,0},{9,13},{1... | collective-permute-start | bytes 393224 | tf_op jit(solution)/shard_map/ppermute | solution.py:35
  80.3 2.9 %turn_features.1 = (bf16[1920,1024]{1,0:T(8,128)(2,1)S(1)}, f32[8,128]{1,0:T(8,128)S(1)}) custom-call(s32[45]{0:T(128)S(1)} %stack.183.table, bf16[256,7680]{1,0:T(8,128)(2,1)} %own_ref.1, bf16[256,1920]{1,0:T(8,128)(2,1)S(1)} %wait_for.11.near_ref, bf16[256,1920]{1,0:T(8,128)(2,1)S(1)} %collective-permute-done.19.near_pair_ref, ...), custom_call_target="tpu_custom_call" | custom-call | tf_op jit(solution)/shard_map/turn_features/pallas_call | solution.py:428
  83.2 0.6 collective-permute-done.20.refs_5_.refs_11_
  83.8 1.1 %collective-permute-done.21.refs_6_.refs_12_ = bf16[256,512]{1,0:T(8,128)(2,1)S(1)} collective-permute-done((bf16[256,512]{1,0:T(8,128)(2,1)S(1)}, bf16[256,512]{1,0:T(8,128)(2,1)S(1)}, u32[]{:S(2)}, u32[]{:S(2)}) %collective-permute-start.21) | collective-permute-done | bytes 262176 | tf_op jit(solution)/shard_map/ppermute | solution.py:35
  84.9 0.5 collective-permute-done.18.refs_3_
  85.4 0.6 add_second.1.refs_1_.refs_14_.refs_0_
  86.1 2.2 %collective-permute-start.24 = (bf16[256,2048]{1,0:T(8,128)(2,1)S(1)}, bf16[256,2048]{1,0:T(8,128)(2,1)S(1)}, u32[]{:S(2)}, u32[]{:S(2)}) collective-permute-start(bf16[256,2048]{1,0:T(8,128)(2,1)S(1)} %wait_for.14.refs_8_), channel_id=1, source_target_pairs={{0,1},{1,0},{4,5},{5,4},{2,3},{3,2},{6,7},{7,6},{8,9},{9,8},{12,13... | collective-permute-start | bytes 3145736 | tf_op jit(solution)/shard_map/ppermute | solution.py:35
  88.4 0.4 collective-permute-start.22
  88.8 1.6 %collective-permute-start.27 = (bf16[512,128]{1,0:T(8,128)(2,1)S(1)}, bf16[512,128]{1,0:T(8,128)(2,1)S(1)}, u32[]{:S(2)}, u32[]{:S(2)}) collective-permute-start(bf16[512,128]{1,0:T(8,128)(2,1)S(1)} %add_second.1.refs_1_.refs_14_.refs_0_), channel_id=1, source_target_pairs={{0,96},{1,97},{4,100},{5,101},{2,98},{3,99},{6,102},{7,103},{8,104... | collective-permute-start | bytes 393224 | tf_op jit(solution)/shard_map/ppermute | solution.py:35
  90.4 0.8 collective-permute-start.26
  91.2 0.9 collective-permute-start.25
  92.1 0.9 collective-permute-start.28
  93.0 0.6 collective-permute-done.22.refs_5_
  93.6 5.6 %weight_grads.1 = (f32[2048,256]{1,0:T(8,128)}, f32[2048,256]{1,0:T(8,128)}, f32[8,128]{1,0:T(8,128)S(1)}) custom-call(s32[45]{0:T(128)S(1)} %stack.183.table, bf16[256,2048]{1,0:T(8,128)(2,1)S(1)} %copy-done.2, bf16[256,2048]{1,0:T(8,128)(2,1)S(1)} %collective-permute-done.refs_1_, bf16[256,2048]{1,0:T(8,128)(2,1)S(1)} %wait_for.9.second.slice_one.refs_2_, ...), custom_call_target="tpu_custom_call" | custom-call | tf_op jit(solution)/shard_map/weight_grads/pallas_call | solution.py:395
  99.2 0.4 collective-permute-start.31
  100.1 0.5 collective-permute-done.31.refs_7_
  101.1 2.9 %projector_grad.1 = f32[1920,256]{1,0:T(8,128)} custom-call(s32[45]{0:T(128)S(1)} %stack.183.table, bf16[1920,1024]{1,0:T(8,128)(2,1)S(1)} %get-tuple-element.45.feature_ref, bf16[512,128]{1,0:T(8,128)(2,1)S(1)} %add_second.1.refs_1_.refs_14_.refs_0_, bf16[512,128]{1,0:T(8,128)(2,1)S(1)} %wait_for.15.refs_1_, bf16[512,128]{1,0:T(8,128)(2,1)S(1)} %wait_for.16.refs_2_, ...), custom_call_target="tpu_custom_call" | custom-call | tf_op jit(solution)/shard_map/projector_grad/pallas_call | solution.py:477
  (54 shorter events, 2.3 us)
Async XLA Ops:
  0.6 15.3 %collective-permute-start = (bf16[256,2048]{1,0:T(8,128)(2,1)}, bf16[256,2048]{1,0:T(8,128)(2,1)S(1)}, u32[]{:S(2)}, u32[]{:S(2)}) collective-permute-start(bf16[256,2048]{1,0:T(8,128)(2,1)} %refs_0_.3), channel_id=1, source_target_pairs={{0,1},{1,0},{4,5},{5,4},{2,3},{3,2},{6,7},{7,6},{8,9},{9,8},{12,13... | collective-permute-start | bytes 3145736 | tf_op jit(solution)/shard_map/ppermute | solution.py:35
  2.1 26.2 %collective-permute-start.1 = (bf16[256,2048]{1,0:T(8,128)(2,1)}, bf16[256,2048]{1,0:T(8,128)(2,1)S(1)}, u32[]{:S(2)}, u32[]{:S(2)}) collective-permute-start(bf16[256,2048]{1,0:T(8,128)(2,1)} %refs_0_.3), channel_id=1, source_target_pairs={{0,6},{1,7},{4,2},{5,3},{2,4},{3,5},{6,0},{7,1},{8,14},{9,15},{12,... | collective-permute-start | bytes 3145736 | tf_op jit(solution)/shard_map/ppermute | solution.py:35
  4.7 7.0 %copy-start.7 = (s32[512]{0:T(512)S(1)}, s32[512]{0:T(512)}, u32[]{:S(2)}) copy-start(s32[512]{0:T(512)} %param.12) | copy-start | bytes 6148
  7.9 20.5 %collective-permute-start.2 = (bf16[256,1920]{1,0:T(8,128)(2,1)}, bf16[256,1920]{1,0:T(8,128)(2,1)S(1)}, u32[]{:S(2)}, u32[]{:S(2)}) collective-permute-start(bf16[256,1920]{1,0:T(8,128)(2,1)} %get-tuple-element.26), channel_id=1, source_target_pairs={{0,32},{1,97},{4,36},{5,101},{2,34},{3,99},{6,38},{7,103},{8,40},{... | collective-permute-start | bytes 2949128 | tf_op jit(solution)/shard_map/ppermute | solution.py:35
  11.7 10.0 %collective-permute-start.3 = (bf16[64,1920]{1,0:T(8,128)(2,1)}, bf16[64,1920]{1,0:T(8,128)(2,1)S(1)}, u32[]{:S(2)}, u32[]{:S(2)}) collective-permute-start(bf16[64,1920]{1,0:T(8,128)(2,1)} %get-tuple-element.27), channel_id=1, source_target_pairs={{0,64},{1,65},{4,68},{5,69},{2,66},{3,67},{6,70},{7,71},{8,72},{9,... | collective-permute-start | bytes 737288 | tf_op jit(solution)/shard_map/ppermute | solution.py:35
  12.6 1.6 %copy-start.3 = (bf16[512,2048]{1,0:T(8,128)(2,1)S(1)}, bf16[512,2048]{1,0:T(8,128)(2,1)}, u32[]{:S(2)}) copy-start(bf16[512,2048]{1,0:T(8,128)(2,1)} %grad_ref.1) | copy-start | bytes 6291460
  14.2 0.9 copy-start.5
  15.1 1.2 %copy-start.2 = (bf16[256,2048]{1,0:T(8,128)(2,1)S(1)}, bf16[256,2048]{1,0:T(8,128)(2,1)}, u32[]{:S(2)}) copy-start(bf16[256,2048]{1,0:T(8,128)(2,1)} %refs_0_.3) | copy-start | bytes 3145732
  16.4 22.4 %copy-start.1 = (bf16[1,8192,256]{2,1,0:T(8,128)(2,1)S(1)}, bf16[1,8192,256]{2,1,0:T(8,128)(2,1)}, u32[]{:S(2)}) copy-start(bf16[1,8192,256]{2,1,0:T(8,128)(2,1)} %param.14) | copy-start | bytes 12582916
  28.3 10.4 %copy-start = (bf16[1,8192,256]{2,1,0:T(8,128)(2,1)S(1)}, bf16[1,8192,256]{2,1,0:T(8,128)(2,1)}, u32[]{:S(2)}) copy-start(bf16[1,8192,256]{2,1,0:T(8,128)(2,1)} %param.13) | copy-start | bytes 12582916
  28.4 10.4 %copy-start.4 = (bf16[512,2048]{1,0:T(8,128)(2,1)S(1)}, bf16[512,2048]{1,0:T(8,128)(2,1)}, u32[]{:S(2)}) copy-start(bf16[512,2048]{1,0:T(8,128)(2,1)} %query_ref.1) | copy-start | bytes 6291460
  28.4 10.4 %copy-start.6 = (f32[1,128]{1,0:T(1,128)S(1)}, f32[1,128]{1,0:T(1,128)}, u32[]{:S(2)}) copy-start(f32[1,128]{1,0:T(1,128)} %gain_ref.1) | copy-start | bytes 1540
  28.4 10.4 %collective-permute-start.4 = (bf16[256,2048]{1,0:T(8,128)(2,1)S(1)}, bf16[256,2048]{1,0:T(8,128)(2,1)S(1)}, u32[]{:S(2)}, u32[]{:S(2)}) collective-permute-start(bf16[256,2048]{1,0:T(8,128)(2,1)S(1)} %wait_for.9.second.slice_one.refs_2_), channel_id=1, source_target_pairs={{0,1},{1,0},{4,5},{5,4},{2,3},{3,2},{6,7},{7,6},{8,9},{9,8},{12,13... | collective-permute-start | bytes 3145736 | tf_op jit(solution)/shard_map/ppermute | solution.py:35
  32.2 18.9 %collective-permute-start.5 = (bf16[256,2048]{1,0:T(8,128)(2,1)S(1)}, bf16[256,2048]{1,0:T(8,128)(2,1)S(1)}, u32[]{:S(2)}, u32[]{:S(2)}) collective-permute-start(bf16[256,2048]{1,0:T(8,128)(2,1)S(1)} %get-tuple-element.28), channel_id=1, source_target_pairs={{1,33},{5,37},{3,35},{7,39},{9,41},{13,45},{11,43},{15,47},{17,49}... | collective-permute-start | bytes 3145736 | tf_op jit(solution)/shard_map/ppermute | solution.py:35
  33.8 17.3 %collective-permute-start.6 = (bf16[256,2048]{1,0:T(8,128)(2,1)S(1)}, bf16[256,2048]{1,0:T(8,128)(2,1)S(1)}, u32[]{:S(2)}, u32[]{:S(2)}) collective-permute-start(bf16[256,2048]{1,0:T(8,128)(2,1)S(1)} %get-tuple-element.32), channel_id=1, source_target_pairs={{1,97},{5,101},{3,99},{7,103},{9,105},{13,109},{11,107},{15,111},{... | collective-permute-start | bytes 3145736 | tf_op jit(solution)/shard_map/ppermute | solution.py:35
  37.2 13.9 %collective-permute-start.7 = (bf16[64,1920]{1,0:T(8,128)(2,1)S(1)}, bf16[64,1920]{1,0:T(8,128)(2,1)S(1)}, u32[]{:S(2)}, u32[]{:S(2)}) collective-permute-start(bf16[64,1920]{1,0:T(8,128)(2,1)S(1)} %collective-permute-done.3.refs_4_.refs_3_.rest_0_), channel_id=1, source_target_pairs={{0,8},{1,9},{4,12},{5,13},{2,10},{3,11},{6,14},{7,15},{8,0},{9,1},... | collective-permute-start | bytes 737288 | tf_op jit(solution)/shard_map/ppermute | solution.py:35
  51.1 5.3 %collective-permute-start.8 = (bf16[8192,128]{1,0:T(8,128)(2,1)S(1)}, bf16[8192,128]{1,0:T(8,128)(2,1)S(1)}, u32[]{:S(2)}, u32[]{:S(2)}) collective-permute-start(bf16[8192,128]{1,0:T(8,128)(2,1)S(1)} %wait_for.10), channel_id=1, source_target_pairs={{0,1},{1,0},{4,5},{5,4},{2,3},{3,2},{6,7},{7,6},{8,9},{9,8},{12,13... | collective-permute-start | bytes 6291464 | tf_op jit(solution)/shard_map/ppermute | solution.py:35
  51.7 20.4 %collective-permute-start.14 = (bf16[256,2048]{1,0:T(8,128)(2,1)S(1)}, bf16[256,2048]{1,0:T(8,128)(2,1)S(1)}, u32[]{:S(2)}, u32[]{:S(2)}) collective-permute-start(bf16[256,2048]{1,0:T(8,128)(2,1)S(1)} %get-tuple-element.28), channel_id=1, source_target_pairs={{0,65},{4,69},{2,67},{6,71},{8,73},{12,77},{10,75},{14,79},{16,81}... | collective-permute-start | bytes 3145736 | tf_op jit(solution)/shard_map/ppermute | solution.py:35
  53.0 3.1 %collective-permute-start.9 = (bf16[64,1920]{1,0:T(8,128)(2,1)S(1)}, bf16[64,1920]{1,0:T(8,128)(2,1)S(1)}, u32[]{:S(2)}, u32[]{:S(2)}) collective-permute-start(bf16[64,1920]{1,0:T(8,128)(2,1)S(1)} %collective-permute-done.3.refs_4_.refs_3_.rest_0_), channel_id=1, source_target_pairs={{0,1},{1,0},{4,5},{5,4},{2,3},{3,2},{6,7},{7,6},{8,9},{9,8},{12,13... | collective-permute-start | bytes 737288 | tf_op jit(solution)/shard_map/ppermute | solution.py:35
  54.9 1.5 %collective-permute-start.10 = (bf16[64,1920]{1,0:T(8,128)(2,1)S(1)}, bf16[64,1920]{1,0:T(8,128)(2,1)S(1)}, u32[]{:S(2)}, u32[]{:S(2)}) collective-permute-start(bf16[64,1920]{1,0:T(8,128)(2,1)S(1)} %collective-permute-done.7.refs_4_.rest_1_), channel_id=1, source_target_pairs={{0,1},{1,0},{4,5},{5,4},{2,3},{3,2},{6,7},{7,6},{8,9},{9,8},{12,13... | collective-permute-start | bytes 737288 | tf_op jit(solution)/shard_map/ppermute | solution.py:35
  56.9 15.2 %collective-permute-start.11 = (bf16[2048,128]{1,0:T(8,128)(2,1)S(1)}, bf16[2048,128]{1,0:T(8,128)(2,1)S(1)}, u32[]{:S(2)}, u32[]{:S(2)}) collective-permute-start(bf16[2048,128]{1,0:T(8,128)(2,1)S(1)} %get-tuple-element.34), channel_id=1, source_target_pairs={{0,2},{1,17},{4,6},{5,21},{2,0},{3,19},{6,4},{7,23},{8,10},{9,25},... | collective-permute-start | bytes 1572872 | tf_op jit(solution)/shard_map/ppermute | solution.py:35
  59.7 12.9 %collective-permute-start.12 = (bf16[2048,128]{1,0:T(8,128)(2,1)S(1)}, bf16[2048,128]{1,0:T(8,128)(2,1)S(1)}, u32[]{:S(2)}, u32[]{:S(2)}) collective-permute-start(bf16[2048,128]{1,0:T(8,128)(2,1)S(1)} %get-tuple-element.35), channel_id=1, source_target_pairs={{0,4},{1,9},{4,0},{5,13},{2,6},{3,11},{6,2},{7,15},{8,12},{9,1},{1... | collective-permute-start | bytes 1572872 | tf_op jit(solution)/shard_map/ppermute | solution.py:35
  60.1 12.5 %collective-permute-start.13 = (bf16[2048,128]{1,0:T(8,128)(2,1)S(1)}, bf16[2048,128]{1,0:T(8,128)(2,1)S(1)}, u32[]{:S(2)}, u32[]{:S(2)}) collective-permute-start(bf16[2048,128]{1,0:T(8,128)(2,1)S(1)} %get-tuple-element.36), channel_id=1, source_target_pairs={{0,6},{1,25},{4,2},{5,29},{2,4},{3,27},{6,0},{7,31},{8,14},{9,17},... | collective-permute-start | bytes 1572872 | tf_op jit(solution)/shard_map/ppermute | solution.py:35
  60.5 11.6 %collective-permute-start.15 = (bf16[256,512]{1,0:T(8,128)(2,1)S(1)}, bf16[256,512]{1,0:T(8,128)(2,1)S(1)}, u32[]{:S(2)}, u32[]{:S(2)}) collective-permute-start(bf16[256,512]{1,0:T(8,128)(2,1)S(1)} %get-tuple-element.37.refs_10_), channel_id=1, source_target_pairs={{0,64},{1,65},{4,68},{5,69},{2,66},{3,67},{6,70},{7,71},{8,72},{9,... | collective-permute-start | bytes 786440 | tf_op jit(solution)/shard_map/ppermute | solution.py:35
  72.9 7.2 %collective-permute-start.19 = (bf16[256,1920]{1,0:T(8,128)(2,1)S(1)}, bf16[256,1920]{1,0:T(8,128)(2,1)S(1)}, u32[]{:S(2)}, u32[]{:S(2)}) collective-permute-start(bf16[256,1920]{1,0:T(8,128)(2,1)S(1)} %wait_for.11.near_ref), channel_id=1, source_target_pairs={{0,1},{1,0},{4,5},{5,4},{2,3},{3,2},{6,7},{7,6},{8,9},{9,8},{12,13... | collective-permute-start | bytes 2949128 | tf_op jit(solution)/shard_map/ppermute | solution.py:35
  76.0 7.9 %collective-permute-start.20 = (bf16[256,512]{1,0:T(8,128)(2,1)S(1)}, bf16[256,512]{1,0:T(8,128)(2,1)S(1)}, u32[]{:S(2)}, u32[]{:S(2)}) collective-permute-start(bf16[256,512]{1,0:T(8,128)(2,1)S(1)} %get-tuple-element.37.refs_10_), channel_id=1, source_target_pairs={{0,32},{1,33},{4,36},{5,37},{2,34},{3,35},{6,38},{7,39},{8,40},{9,... | collective-permute-start | bytes 786440 | tf_op jit(solution)/shard_map/ppermute | solution.py:35
  76.0 8.9 %collective-permute-start.21 = (bf16[256,512]{1,0:T(8,128)(2,1)S(1)}, bf16[256,512]{1,0:T(8,128)(2,1)S(1)}, u32[]{:S(2)}, u32[]{:S(2)}) collective-permute-start(bf16[256,512]{1,0:T(8,128)(2,1)S(1)} %get-tuple-element.37.refs_10_), channel_id=1, source_target_pairs={{0,96},{1,97},{4,100},{5,101},{2,98},{3,99},{6,102},{7,103},{8,104... | collective-permute-start | bytes 786440 | tf_op jit(solution)/shard_map/ppermute | solution.py:35
  77.0 7.9 %collective-permute-start.16 = (bf16[512,128]{1,0:T(8,128)(2,1)S(1)}, bf16[512,128]{1,0:T(8,128)(2,1)S(1)}, u32[]{:S(2)}, u32[]{:S(2)}) collective-permute-start(bf16[512,128]{1,0:T(8,128)(2,1)S(1)} %get-tuple-element.39), channel_id=1, source_target_pairs={{0,16},{1,3},{4,20},{5,7},{2,18},{3,1},{6,22},{7,5},{8,24},{9,11},... | collective-permute-start | bytes 393224 | tf_op jit(solution)/shard_map/ppermute | solution.py:35
  78.6 6.3 %collective-permute-start.17 = (bf16[512,128]{1,0:T(8,128)(2,1)S(1)}, bf16[512,128]{1,0:T(8,128)(2,1)S(1)}, u32[]{:S(2)}, u32[]{:S(2)}) collective-permute-start(bf16[512,128]{1,0:T(8,128)(2,1)S(1)} %get-tuple-element.40), channel_id=1, source_target_pairs={{0,8},{1,5},{4,12},{5,1},{2,10},{3,7},{6,14},{7,3},{8,0},{9,13},{1... | collective-permute-start | bytes 393224 | tf_op jit(solution)/shard_map/ppermute | solution.py:35
  80.1 5.3 %collective-permute-start.18 = (bf16[512,128]{1,0:T(8,128)(2,1)S(1)}, bf16[512,128]{1,0:T(8,128)(2,1)S(1)}, u32[]{:S(2)}, u32[]{:S(2)}) collective-permute-start(bf16[512,128]{1,0:T(8,128)(2,1)S(1)} %get-tuple-element.41), channel_id=1, source_target_pairs={{0,24},{1,7},{4,28},{5,3},{2,26},{3,5},{6,30},{7,1},{8,16},{9,15},... | collective-permute-start | bytes 393224 | tf_op jit(solution)/shard_map/ppermute | solution.py:35
  86.1 5.1 %collective-permute-start.24 = (bf16[256,2048]{1,0:T(8,128)(2,1)S(1)}, bf16[256,2048]{1,0:T(8,128)(2,1)S(1)}, u32[]{:S(2)}, u32[]{:S(2)}) collective-permute-start(bf16[256,2048]{1,0:T(8,128)(2,1)S(1)} %wait_for.14.refs_8_), channel_id=1, source_target_pairs={{0,1},{1,0},{4,5},{5,4},{2,3},{3,2},{6,7},{7,6},{8,9},{9,8},{12,13... | collective-permute-start | bytes 3145736 | tf_op jit(solution)/shard_map/ppermute | solution.py:35
  88.3 3.8 %collective-permute-start.23 = (bf16[256,2048]{1,0:T(8,128)(2,1)S(1)}, bf16[256,2048]{1,0:T(8,128)(2,1)S(1)}, u32[]{:S(2)}, u32[]{:S(2)}) collective-permute-start(bf16[256,2048]{1,0:T(8,128)(2,1)S(1)} %wait_for.13.refs_6_), channel_id=1, source_target_pairs={{0,1},{1,0},{4,5},{5,4},{2,3},{3,2},{6,7},{7,6},{8,9},{9,8},{12,13... | collective-permute-start | bytes 3145736 | tf_op jit(solution)/shard_map/ppermute | solution.py:35
  88.4 5.2 %collective-permute-start.22 = (bf16[256,2048]{1,0:T(8,128)(2,1)S(1)}, bf16[256,2048]{1,0:T(8,128)(2,1)S(1)}, u32[]{:S(2)}, u32[]{:S(2)}) collective-permute-start(bf16[256,2048]{1,0:T(8,128)(2,1)S(1)} %wait_for.12.refs_4_), channel_id=1, source_target_pairs={{0,1},{1,0},{4,5},{5,4},{2,3},{3,2},{6,7},{7,6},{8,9},{9,8},{12,13... | collective-permute-start | bytes 3145736 | tf_op jit(solution)/shard_map/ppermute | solution.py:35
  88.8 10.4 %collective-permute-start.27 = (bf16[512,128]{1,0:T(8,128)(2,1)S(1)}, bf16[512,128]{1,0:T(8,128)(2,1)S(1)}, u32[]{:S(2)}, u32[]{:S(2)}) collective-permute-start(bf16[512,128]{1,0:T(8,128)(2,1)S(1)} %add_second.1.refs_1_.refs_14_.refs_0_), channel_id=1, source_target_pairs={{0,96},{1,97},{4,100},{5,101},{2,98},{3,99},{6,102},{7,103},{8,104... | collective-permute-start | bytes 393224 | tf_op jit(solution)/shard_map/ppermute | solution.py:35
  90.4 9.2 %collective-permute-start.26 = (bf16[512,128]{1,0:T(8,128)(2,1)S(1)}, bf16[512,128]{1,0:T(8,128)(2,1)S(1)}, u32[]{:S(2)}, u32[]{:S(2)}) collective-permute-start(bf16[512,128]{1,0:T(8,128)(2,1)S(1)} %add_second.1.refs_1_.refs_14_.refs_0_), channel_id=1, source_target_pairs={{0,64},{1,65},{4,68},{5,69},{2,66},{3,67},{6,70},{7,71},{8,72},{9,... | collective-permute-start | bytes 393224 | tf_op jit(solution)/shard_map/ppermute | solution.py:35
  91.2 8.6 %collective-permute-start.25 = (bf16[512,128]{1,0:T(8,128)(2,1)S(1)}, bf16[512,128]{1,0:T(8,128)(2,1)S(1)}, u32[]{:S(2)}, u32[]{:S(2)}) collective-permute-start(bf16[512,128]{1,0:T(8,128)(2,1)S(1)} %add_second.1.refs_1_.refs_14_.refs_0_), channel_id=1, source_target_pairs={{0,32},{1,33},{4,36},{5,37},{2,34},{3,35},{6,38},{7,39},{8,40},{9,... | collective-permute-start | bytes 393224 | tf_op jit(solution)/shard_map/ppermute | solution.py:35
  92.1 8.0 %collective-permute-start.28 = (bf16[512,128]{1,0:T(8,128)(2,1)S(1)}, bf16[512,128]{1,0:T(8,128)(2,1)S(1)}, u32[]{:S(2)}, u32[]{:S(2)}) collective-permute-start(bf16[512,128]{1,0:T(8,128)(2,1)S(1)} %add_second.1.refs_1_.refs_14_.refs_0_), channel_id=1, source_target_pairs={{0,1},{1,0},{4,5},{5,4},{2,3},{3,2},{6,7},{7,6},{8,9},{9,8},{12,13... | collective-permute-start | bytes 393224 | tf_op jit(solution)/shard_map/ppermute | solution.py:35
  99.2 1.4 %collective-permute-start.31 = (bf16[512,128]{1,0:T(8,128)(2,1)S(1)}, bf16[512,128]{1,0:T(8,128)(2,1)S(1)}, u32[]{:S(2)}, u32[]{:S(2)}) collective-permute-start(bf16[512,128]{1,0:T(8,128)(2,1)S(1)} %wait_for.17.refs_3_), channel_id=1, source_target_pairs={{0,1},{1,0},{4,5},{5,4},{2,3},{3,2},{6,7},{7,6},{8,9},{9,8},{12,13... | collective-permute-start | bytes 393224 | tf_op jit(solution)/shard_map/ppermute | solution.py:35
  99.6 1.3 %collective-permute-start.30 = (bf16[512,128]{1,0:T(8,128)(2,1)S(1)}, bf16[512,128]{1,0:T(8,128)(2,1)S(1)}, u32[]{:S(2)}, u32[]{:S(2)}) collective-permute-start(bf16[512,128]{1,0:T(8,128)(2,1)S(1)} %wait_for.16.refs_2_), channel_id=1, source_target_pairs={{0,1},{1,0},{4,5},{5,4},{2,3},{3,2},{6,7},{7,6},{8,9},{9,8},{12,13... | collective-permute-start | bytes 393224 | tf_op jit(solution)/shard_map/ppermute | solution.py:35
  99.8 1.4 %collective-permute-start.29 = (bf16[512,128]{1,0:T(8,128)(2,1)S(1)}, bf16[512,128]{1,0:T(8,128)(2,1)S(1)}, u32[]{:S(2)}, u32[]{:S(2)}) collective-permute-start(bf16[512,128]{1,0:T(8,128)(2,1)S(1)} %wait_for.15.refs_1_), channel_id=1, source_target_pairs={{0,1},{1,0},{4,5},{5,4},{2,3},{3,2},{6,7},{7,6},{8,9},{9,8},{12,13... | collective-permute-start | bytes 393224 | tf_op jit(solution)/shard_map/ppermute | solution.py:35
